TPU v7x, 512 devices: a whole 4x8x8 slice. The times are simulated.
512 devices in a mesh: segment: 4 (over x), dp: 128 (over z, y, core).
Axes of the slice: x: 4, y: 8, z: 8, core: 2. Of those that a mesh axis runs over, the one named last changes fastest.
Arguments:
- events: bfloat16 [512, 64, 512], P('dp'), may hold values from -6 to 6
- lengths: int32 [512], P('dp'), may hold values from 8 to 64, as said below
- balance_plan: int32 [512], P('dp'), may hold values from 0 to 7, as said below
- routes: int32 [512, 1], P('dp'), may hold values from 0 to 127; in each aligned block of 512 rows (0 to 511, 512 to 1023, ...) at most 8 rows name the same one
- w_uvqk: bfloat16 [4, 512, 2048], P('segment'), may hold values from -0.25 to 0.25
- w_out: bfloat16 [4, 512, 512], P('segment'), may hold values from -0.25 to 0.25
- rel_bias: float32 [4, 8, 64], P('segment'), may hold values from -4 to 4
- state_cotangent: bfloat16 [128, 8, 512], P('dp', None, 'segment'), may hold values from -6 to 6
Outputs:
- served: bfloat16 [128, 8, 512], P('dp', None, 'segment')
- segment_grads: bfloat16 [4, 512, 64, 512], P('segment', 'dp')
- weight_grads: float32 [4, 512, 512], P('segment', 'dp')
Inputs may be any that keep to these rules, and one draw needn't show every extreme that they name: `lengths`: every device's block of 4 consecutive histories holds at least one history of 64 events. `balance_plan`: device i and device i + 64 form a pair (i below 64); over the 8 histories of a pair each value appears once. `routes`: no owner is named more than 8 times over all histories, a bound that some block reaches.
All inputs are finite; a program needn't handle non-finite values.
Results may differ from a plain program's by a relative error of at most 0.034.
Values may be sent and summed in bfloat16 or wider, within the bound.
No kernel may reach another device: no remote copies, remote signals or barrier semaphores. Data moves between devices by JAX's collectives and lax.ppermute only.
A program may use at most 128 MiB of HBM per device.

v0:
```python
import jax
import jax.numpy as jnp
from jax import lax
from jax.sharding import PartitionSpec as P

MB = 4


def partner(value, axis, distance):
    return lax.ppermute(value, axis, [(i, i ^ 1 << distance) for i in range(lax.axis_size(axis))])


def shifted(value, axis, steps):
    count = lax.axis_size(axis)
    initial, last = (max(0, -steps), min(count, count - steps))
    return lax.ppermute(value, axis, [(source, source + steps) for source in range(initial, last)])


def prefix(value, axis, combine, identity):
    length, position = (lax.axis_size(axis), lax.axis_index(axis))
    everything = lax.all_gather(value, axis)
    start = jnp.broadcast_to(jnp.asarray(identity, value.dtype), value.shape)

    def step(k, before):
        reached = k < position
        new = combine(before, everything[k])
        return jnp.where(reached, new, before)

    return lax.fori_loop(0, length, step, start)


def for_sending(value):
    return jax.tree.map(lambda a: a.astype(jnp.bfloat16) if a.dtype == jnp.float32 else a, value)


def normalize(values_in):
    average = jnp.mean(values_in, axis=-1, keepdims=True)
    centred = values_in - average
    return centred * lax.rsqrt(jnp.mean(centred * centred, axis=-1, keepdims=True) + 1e-06)


def hstu_layer(inputs, seq_lengths, w_uvqk, w_out, rel_bias):
    histories, positions, features = inputs.shape
    head_count = rel_bias.shape[0]
    head_size = features // head_count
    flat_rows = inputs.reshape(histories * positions, features).astype(jnp.float32)
    normed = normalize(flat_rows).astype(jnp.bfloat16)
    projected = jax.nn.silu(jnp.dot(normed, w_uvqk, preferred_element_type=jnp.float32)).astype(
        jnp.bfloat16
    )
    gate_rows = projected[:, :features]
    value_rows = projected[:, features : 2 * features].reshape(
        histories, positions, head_count, head_size
    )
    queries = projected[:, 2 * features : 3 * features].reshape(
        histories, positions, head_count, head_size
    )
    key_rows = projected[:, 3 * features :].reshape(histories, positions, head_count, head_size)
    scores = jnp.einsum(
        "bihe,bjhe->bhij", queries, key_rows, preferred_element_type=jnp.float32
    ) * head_size ** (-0.5)
    row_pos = jnp.arange(positions, dtype=jnp.int32)
    offset = row_pos[:, None] - row_pos[None, :]
    pos_bias = jnp.take(rel_bias, jnp.clip(offset, 0, positions - 1), axis=1)
    allowed = (offset >= 0)[None, None] & (
        row_pos[None, None, None, :] < seq_lengths[:, None, None, None]
    )
    weights = jnp.where(allowed, jax.nn.silu(scores + pos_bias[None]), 0.0).astype(jnp.bfloat16)
    attended = jnp.einsum(
        "bhij,bjhe->bihe", weights, value_rows, preferred_element_type=jnp.float32
    )
    attended = attended.reshape(histories * positions, features)
    branch = (normalize(attended) * gate_rows.astype(jnp.float32)).astype(jnp.bfloat16)
    output = (flat_rows + jnp.dot(branch, w_out, preferred_element_type=jnp.float32)).astype(
        jnp.bfloat16
    )
    return (output.reshape(histories, positions, features), branch)


def keep_block(store, block, where_at, active):
    old_block = lax.dynamic_index_in_dim(store, where_at, 0, keepdims=False)
    return lax.dynamic_update_index_in_dim(store, jnp.where(active, block, old_block), where_at, 0)


def add_counts(earlier, later):
    return earlier + later


def body(events, lengths, balance_plan, routes, w_uvqk, w_out, rel_bias, state_cotangent):
    hist_dev, positions, features = events.shape
    dp_count = lax.axis_size("dp")
    segment_count = lax.axis_size("segment")
    segment_at = lax.axis_index("segment")
    my_index = lax.axis_index("dp")
    top_bit = dp_count.bit_length() - 2
    partner_events, partner_lengths, partner_plan = partner(
        (events, lengths, balance_plan), "dp", top_bit
    )
    upper_half = my_index >= dp_count // 2
    joined_events = jnp.where(
        upper_half,
        jnp.concatenate([partner_events, events]),
        jnp.concatenate([events, partner_events]),
    )
    joined_lengths = jnp.where(
        upper_half,
        jnp.concatenate([partner_lengths, lengths]),
        jnp.concatenate([lengths, partner_lengths]),
    )
    joined_plan = jnp.where(
        upper_half,
        jnp.concatenate([partner_plan, balance_plan]),
        jnp.concatenate([balance_plan, partner_plan]),
    )
    wanted = upper_half.astype(jnp.int32) * hist_dev + jnp.arange(hist_dev, dtype=jnp.int32)
    chosen = joined_plan[None, :] == wanted[:, None]
    balanced = (
        jnp.dot(
            chosen.astype(jnp.bfloat16),
            joined_events.reshape(2 * hist_dev, positions * features),
            preferred_element_type=jnp.float32,
        )
        .astype(jnp.bfloat16)
        .reshape(hist_dev, positions, features)
    )
    balanced_lengths = jnp.sum(jnp.where(chosen, joined_lengths[None, :], 0), axis=1).astype(
        jnp.int32
    )
    per_micro = hist_dev // MB
    last_event = jnp.arange(positions, dtype=jnp.int32)[None, :] == balanced_lengths[:, None] - 1
    empty_block = jnp.zeros((per_micro, positions, features), jnp.bfloat16)
    step_count = MB + segment_count - 1
    weight_in = w_uvqk[0]
    weight_back = w_out[0]
    bias_table = rel_bias[0]

    def layer_at(segment_input, micro_lengths):
        return hstu_layer(segment_input, micro_lengths, weight_in, weight_back, bias_table)

    stored_inputs = jnp.zeros((MB, per_micro, positions, features), jnp.bfloat16)
    stored_outputs = jnp.zeros((MB, per_micro, positions, features), jnp.bfloat16)
    received = empty_block
    for tick in range(step_count):
        micro = tick - segment_at
        active = (micro >= 0) & (micro < MB)
        block_at = jnp.clip(micro, 0, MB - 1)
        first_input = lax.dynamic_slice_in_dim(balanced, block_at * per_micro, per_micro, 0)
        segment_input = jnp.where(segment_at == 0, first_input, received)
        micro_lengths = lax.dynamic_slice_in_dim(
            balanced_lengths, block_at * per_micro, per_micro, 0
        )
        produced = lax.cond(
            active, lambda: layer_at(segment_input, micro_lengths)[0], lambda: empty_block
        )
        stored_inputs = keep_block(stored_inputs, segment_input, block_at, active)
        stored_outputs = keep_block(stored_outputs, produced, block_at, active)
        received = shifted(produced, "segment", 1)
    finals = stored_outputs.reshape(hist_dev, positions, features)
    states = jnp.einsum(
        "al,ald->ad", last_event.astype(jnp.bfloat16), finals, preferred_element_type=jnp.float32
    ).astype(jnp.bfloat16)
    owner_of = routes[:, 0]
    inner = jnp.arange(hist_dev, dtype=jnp.int32)
    same_owner = (owner_of[:, None] == owner_of[None, :]) & (inner[None, :] < inner[:, None])
    owner_rank = jnp.sum(same_owner.astype(jnp.int32), axis=1)
    owner_hit = owner_of[:, None] == jnp.arange(dp_count, dtype=jnp.int32)[None, :]
    owner_totals = jnp.sum(owner_hit.astype(jnp.int32), axis=0)
    earlier_counts = prefix(owner_totals, "dp", add_counts, jnp.zeros_like(owner_totals))
    slot_base = jnp.sum(jnp.where(owner_hit, earlier_counts[None, :], 0), axis=1).astype(jnp.int32)
    slot_key = slot_base + owner_rank
    slot_count = state_cotangent.shape[1]
    quarter = features // segment_count
    slot_ids = jnp.arange(slot_count, dtype=jnp.int32)
    piece_states = lax.all_gather(states, "dp", axis=0, tiled=True)
    piece_owner = lax.all_gather(owner_of, "dp", axis=0, tiled=True)
    piece_slot = lax.all_gather(slot_key, "dp", axis=0, tiled=True)
    hit = (piece_owner[:, None] == my_index) & (piece_slot[:, None] == slot_ids[None, :])
    collected = jnp.dot(
        hit.astype(jnp.bfloat16).T, piece_states, preferred_element_type=jnp.float32
    )
    split_up = lax.all_to_all(
        collected.astype(jnp.bfloat16).reshape(slot_count, segment_count, quarter),
        "segment",
        split_axis=1,
        concat_axis=1,
        tiled=True,
    )
    served = split_up[:, segment_count - 1, :]
    joined_cot = lax.all_gather(state_cotangent[0], "segment", axis=1, tiled=True)
    piece = lax.all_gather(joined_cot[None], "dp", axis=0, tiled=True)
    flat_piece = piece.reshape(piece.shape[0] * piece.shape[1], piece.shape[2])
    wanted_row = owner_of * slot_count + slot_key
    hit = wanted_row[:, None] == jnp.arange(flat_piece.shape[0], dtype=jnp.int32)[None, :]
    final_cot = jnp.dot(
        hit.astype(jnp.bfloat16), flat_piece, preferred_element_type=jnp.float32
    ).astype(jnp.bfloat16)
    seeded = jnp.where(last_event[:, :, None], final_cot[:, None, :], jnp.zeros((), jnp.bfloat16))
    seeded = seeded.reshape(MB, per_micro, positions, features)
    received_cot = empty_block
    input_grads = jnp.zeros((MB, per_micro, positions, features), jnp.bfloat16)
    w_total = jnp.zeros((features, features), jnp.float32)
    empty_branch = jnp.zeros((per_micro * positions, features), jnp.bfloat16)
    for tick in range(step_count):
        micro = tick - (segment_count - 1 - segment_at)
        active = (micro >= 0) & (micro < MB)
        block_at = jnp.clip(micro, 0, MB - 1)
        cotan = jnp.where(
            segment_at == segment_count - 1,
            lax.dynamic_index_in_dim(seeded, block_at, 0, keepdims=False),
            received_cot,
        )
        segment_input = lax.dynamic_index_in_dim(stored_inputs, block_at, 0, keepdims=False)
        micro_lengths = lax.dynamic_slice_in_dim(
            balanced_lengths, block_at * per_micro, per_micro, 0
        )

        def backward_step():
            produced, pull_back, branch = jax.vjp(
                lambda value_in: layer_at(value_in, micro_lengths), segment_input, has_aux=True
            )
            return (pull_back(cotan)[0], branch)

        input_grad, branch_used = lax.cond(
            active, backward_step, lambda: (empty_block, empty_branch)
        )
        w_total = w_total + jnp.dot(
            branch_used.T, cotan.reshape(-1, features), preferred_element_type=jnp.float32
        )
        input_grads = keep_block(input_grads, input_grad, block_at, active)
        received_cot = jax.tree.map(
            lambda part, own: part.astype(own.dtype),
            shifted(for_sending(input_grad), "segment", -1),
            input_grad,
        )
    weight_share = lax.psum_scatter(w_total, "dp", scatter_dimension=0, tiled=True)
    return (
        served[None],
        input_grads.reshape(hist_dev, positions, features)[None],
        weight_share[None],
    )


def solution(mesh):
    return jax.shard_map(
        body,
        mesh=mesh,
        in_specs=(
            P("dp", None, None),
            P("dp"),
            P("dp"),
            P("dp", None),
            P("segment", None, None),
            P("segment", None, None),
            P("segment", None, None),
            P("dp", None, "segment"),
        ),
        out_specs=(
            P("dp", None, "segment"),
            P("segment", "dp", None, None),
            P("segment", "dp", None),
        ),
        check_vma=False,
    )
```

profile of v0, /device:TPU:30, one launch (start us, length us, event | category | flops | bytes accessed | tf_op | source)
XLA Modules:
  0.0 897.6 jit_solution(17687704528726813940)
XLA Ops:
  7.2 10.9 %all-gather.2 = bf16[1,8,512]{2,1,0:T(8,128)(2,1)} all-gather(bf16[1,8,128]{2,1,0:T(8,128)(2,1)} %param.47), channel_id=4, replica_groups=mesh['segment'=4,'dp'=128] {'segment'}, dimensions={2}, use_global_device_ids=true | all-gather | bytes 10240 | tf_op jit(solution)/shard_map/all_gather | solution.py:189
  18.1 10.9 %collective-permute-start.1 = (s32[4]{0:T(128)}, s32[4]{0:T(128)S(1)}, u32[]{:S(2)}, u32[]{:S(2)}) collective-permute-start(s32[4]{0:T(128)} %param.41), channel_id=1, source_target_pairs={{0,64},{1,65},{2,66},{3,67},{4,68},{5,69},{6,70},{7,71},{8,72},{9,... | collective-permute-start | bytes 56 | tf_op jit(solution)/shard_map/ppermute | solution.py:10
  41.3 43.0 %all-gather.4 = s32[128,1,128]{2,1,0:T(1,128)S(1)} all-gather(s32[1,1,128]{2,1,0:T(1,128)S(1)} %bitcast.1212), channel_id=3, replica_groups=mesh['segment'=4,'dp'=128] {'dp'}, dimensions={0}, use_global_device_ids=true | all-gather | bytes 66048 | tf_op jit(solution)/shard_map/all_gather | solution.py:21
  93.2 22.7 %all-reduce.31 = (s32[512]{0:T(512)}, s32[512]{0:T(512)S(1)}) all-reduce(s32[512]{0:T(512)S(1)} %add_dynamic-update-slice_fusion, s32[512]{0:T(512)S(1)} %bitcast_dynamic-update-slice_fusion.20), channel_id=1, replica_groups=mesh['segment'=4,'dp'=128] {'dp'}, use_global_device_ids=true, to_apply=%add.29 | all-reduce | flops 1024 | bytes 8192
  137.2 64.7 %collective-permute-done.5 = bf16[1,64,512]{2,1,0:T(8,128)(2,1)S(1)} collective-permute-done((bf16[1,64,512]{2,1,0:T(8,128)(2,1)}, bf16[1,64,512]{2,1,0:T(8,128)(2,1)S(1)}, u32[]{:S(2)}, u32[]{:S(2)}) %collective-permute-start.5) | collective-permute-done | bytes 65568 | tf_op jit(solution)/shard_map/ppermute | solution.py:16
  202.0 22.4 %conditional.17 = (bf16[1,64,512]{2,1,0:T(8,128)(2,1)}) conditional(s32[]{:T(128)} %convert_element_type.1079, () %tuple.180, (bf16[1,64,512]{2,1,0:T(8,128)(2,1)S(1)}, bf16[512,2048]{1,0:T(8,128)(2,1)}, s32[4]{0:T(128)}, s32[]{:T(128)}, f32[8,64]{0,1:T(8,128)S(1)}, /*index=5*/bf16[512,512]{1,0:T(8,128)(2,1)S(1)}) %tuple.422), branch_computations={%region_24.26_spmd, %region_25.31_spmd} | conditional | flops 177897664 | bytes 6738612 | solution.py:152
  208.8 10.8 %gather_fusion.3 = f32[4096,8]{1,0:T(8,128)S(1)} fusion(f32[8,64]{0,1:T(8,128)S(1)} %get-tuple-element.563, s32[4096]{0:T(1024)S(1)} %broadcast_clamp_fusion.3), kind=kCustom, calls=%fused_computation.3.clone | custom fusion | bytes 278528 | tf_op jit(solution)/shard_map/cond/branch_1_fun/jit(_take)/gather | solution.py:64
  230.8 22.6 %conditional.18 = (bf16[1,64,512]{2,1,0:T(8,128)(2,1)}) conditional(s32[]{:T(128)} %convert_element_type.1080, () %tuple.182, (bf16[1,64,512]{2,1,0:T(8,128)(2,1)S(1)}, bf16[512,2048]{1,0:T(8,128)(2,1)}, s32[4]{0:T(128)}, s32[]{:T(128)}, f32[8,64]{0,1:T(8,128)S(1)}, /*index=5*/bf16[512,512]{1,0:T(8,128)(2,1)S(1)}) %tuple.423), branch_computations={%region_30.32_spmd, %region_31.37_spmd} | conditional | flops 177897664 | bytes 6738612 | solution.py:152
  237.8 10.8 %gather_fusion.4 = f32[4096,8]{1,0:T(8,128)S(1)} fusion(f32[8,64]{0,1:T(8,128)S(1)} %get-tuple-element.569, s32[4096]{0:T(1024)S(1)} %broadcast_clamp_fusion.4), kind=kCustom, calls=%fused_computation.4.clone | custom fusion | bytes 278528 | tf_op jit(solution)/shard_map/cond/branch_1_fun/jit(_take)/gather | solution.py:64
  259.7 22.4 %conditional.19 = (bf16[1,64,512]{2,1,0:T(8,128)(2,1)}) conditional(s32[]{:T(128)} %convert_element_type.1081, () %tuple.184, (bf16[1,64,512]{2,1,0:T(8,128)(2,1)S(1)}, bf16[512,2048]{1,0:T(8,128)(2,1)}, s32[4]{0:T(128)}, s32[]{:T(128)}, f32[8,64]{0,1:T(8,128)S(1)}, /*index=5*/bf16[512,512]{1,0:T(8,128)(2,1)S(1)}) %tuple.424), branch_computations={%region_36.38_spmd, %region_37.43_spmd} | conditional | flops 177897664 | bytes 6738612 | solution.py:152
  266.6 10.8 %gather_fusion.5 = f32[4096,8]{1,0:T(8,128)S(1)} fusion(f32[8,64]{0,1:T(8,128)S(1)} %get-tuple-element.575, s32[4096]{0:T(1024)S(1)} %broadcast_clamp_fusion.5), kind=kCustom, calls=%fused_computation.5.clone | custom fusion | bytes 278528 | tf_op jit(solution)/shard_map/cond/branch_1_fun/jit(_take)/gather | solution.py:64
  288.5 21.8 %conditional.20 = (bf16[1,64,512]{2,1,0:T(8,128)(2,1)S(1)}) conditional(s32[]{:T(128)} %convert_element_type.1082, () %tuple.186, (bf16[1,64,512]{2,1,0:T(8,128)(2,1)S(1)}, bf16[512,2048]{1,0:T(8,128)(2,1)}, s32[4]{0:T(128)}, s32[]{:T(128)}, f32[8,64]{0,1:T(8,128)S(1)}, /*index=5*/bf16[512,512]{1,0:T(8,128)(2,1)S(1)}) %tuple.425), branch_computations={%region_42.44_spmd, %region_43.49_spmd} | conditional | flops 177897664 | bytes 6738612 | solution.py:152
  295.4 10.8 %gather_fusion.6 = f32[4096,8]{1,0:T(8,128)S(1)} fusion(f32[8,64]{0,1:T(8,128)S(1)} %get-tuple-element.581, s32[4096]{0:T(1024)S(1)} %broadcast_clamp_fusion.6), kind=kCustom, calls=%fused_computation.6.clone | custom fusion | bytes 278528 | tf_op jit(solution)/shard_map/cond/branch_1_fun/jit(_take)/gather | solution.py:64
  310.6 49.3 %all-gather.5 = bf16[128,4,512]{2,1,0:T(4,128)(2,1)S(1)} all-gather(bf16[1,4,512]{2,1,0:T(4,128)(2,1)S(1)} %bitcast.1211), channel_id=1, replica_groups=mesh['segment'=4,'dp'=128] {'dp'}, dimensions={0}, use_global_device_ids=true | all-gather | bytes 528384 | tf_op jit(solution)/shard_map/all_gather | solution.py:174
  371.7 27.2 %conditional.21 = (bf16[1,64,512]{2,1,0:T(8,128)(2,1)S(1)}, bf16[64,512]{1,0:T(8,128)(2,1)}) conditional(s32[]{:T(128)} %convert_element_type.1085, () %tuple.188, (bf16[1,64,512]{2,1,0:T(8,128)(2,1)S(1)}, s32[4]{0:T(128)S(1)}, s32[]{:T(128)}, bf16[512,512]{1,0:T(8,128)(2,1)S(1)}, bf16[4,1,64,512]{3,2,0,1:T(8,128)(2,1)S(1)}, ...), branch_computations={%region_48.50_spmd, %region_49.59_spmd} | conditional | flops 332960576 | bytes 17173800 | solution.py:223
  378.3 10.8 %gather_fusion.7 = f32[4096,8]{1,0:T(8,128)S(1)} fusion(f32[8,64]{0,1:T(8,128)S(1)} %get-tuple-element.589, s32[4096]{0:T(1024)S(1)} %broadcast_clamp_fusion.7), kind=kCustom, calls=%fused_computation.7.clone | custom fusion | bytes 278528 | tf_op jit(solution)/shard_map/cond/branch_1_fun/jvp(jit(_take))/gather | solution.py:64
  402.1 31.4 %conditional.22 = (bf16[1,64,512]{2,1,0:T(8,128)(2,1)}, bf16[64,512]{1,0:T(8,128)(2,1)S(1)}) conditional(s32[]{:T(128)} %convert_element_type.1087, () %tuple.190, (bf16[1,64,512]{2,1,0:T(8,128)(2,1)S(1)}, s32[4]{0:T(128)S(1)}, s32[]{:T(128)}, bf16[512,512]{1,0:T(8,128)(2,1)S(1)}, bf16[4,1,64,512]{3,2,0,1:T(8,128)(2,1)S(1)}, ...), branch_computations={%region_58.60_spmd, %region_59.69_spmd} | conditional | flops 332960576 | bytes 13765872 | solution.py:223
  407.8 14.1 %gather_fusion.8 = f32[4096,8]{1,0:T(8,128)} fusion(f32[8,64]{0,1:T(8,128)S(1)} %get-tuple-element.596, s32[4096]{0:T(1024)S(1)} %broadcast_clamp_fusion.8), kind=kCustom, calls=%fused_computation.8.clone | custom fusion | bytes 278528 | tf_op jit(solution)/shard_map/cond/branch_1_fun/jvp(jit(_take))/gather | solution.py:64
  440.5 31.1 %conditional.23 = (bf16[1,64,512]{2,1,0:T(8,128)(2,1)}, bf16[64,512]{1,0:T(8,128)(2,1)S(1)}) conditional(s32[]{:T(128)} %convert_element_type.1088, () %tuple.192, (bf16[1,64,512]{2,1,0:T(8,128)(2,1)S(1)}, s32[4]{0:T(128)S(1)}, s32[]{:T(128)}, bf16[512,512]{1,0:T(8,128)(2,1)S(1)}, bf16[4,1,64,512]{3,2,0,1:T(8,128)(2,1)S(1)}, ...), branch_computations={%region_68.70_spmd, %region_69.79_spmd} | conditional | flops 332960576 | bytes 14290216 | solution.py:223
  446.4 14.1 %gather_fusion.9 = f32[4096,8]{1,0:T(8,128)} fusion(f32[8,64]{0,1:T(8,128)S(1)} %get-tuple-element.603, s32[4096]{0:T(1024)S(1)} %broadcast_clamp_fusion.9), kind=kCustom, calls=%fused_computation.9.clone | custom fusion | bytes 278528 | tf_op jit(solution)/shard_map/cond/branch_1_fun/jvp(jit(_take))/gather | solution.py:64
  478.1 33.0 %conditional.24 = (bf16[1,64,512]{2,1,0:T(8,128)(2,1)}, bf16[64,512]{1,0:T(8,128)(2,1)}) conditional(s32[]{:T(128)} %convert_element_type.1089, () %tuple.194, (bf16[1,64,512]{2,1,0:T(8,128)(2,1)}, s32[4]{0:T(128)S(1)}, s32[]{:T(128)}, bf16[512,512]{1,0:T(8,128)(2,1)S(1)}, bf16[4,1,64,512]{3,2,0,1:T(8,128)(2,1)S(1)}, ...), branch_computations={%region_78.80_spmd, %region_79.89_spmd} | conditional | flops 332960576 | bytes 13765872 | solution.py:223
  483.8 14.1 %gather_fusion.10 = f32[4096,8]{1,0:T(8,128)} fusion(f32[8,64]{0,1:T(8,128)S(1)} %get-tuple-element.610, s32[4096]{0:T(1024)S(1)} %broadcast_clamp_fusion.10), kind=kCustom, calls=%fused_computation.10.clone | custom fusion | bytes 278528 | tf_op jit(solution)/shard_map/cond/branch_1_fun/jvp(jit(_take))/gather | solution.py:64
  519.6 61.1 %collective-permute-start.13 = (bf16[1,64,512]{2,1,0:T(8,128)(2,1)S(1)}, bf16[1,64,512]{2,1,0:T(8,128)(2,1)S(1)}, u32[]{:S(2)}, u32[]{:S(2)}) collective-permute-start(bf16[1,64,512]{2,1,0:T(8,128)(2,1)S(1)} %get-tuple-element.655), channel_id=1, source_target_pairs={{128,0},{256,128},{384,256},{129,1},{257,129},{385,257},{130,2},{2... | collective-permute-start | bytes 196616 | tf_op jit(solution)/shard_map/ppermute | solution.py:16
  597.4 291.9 %all-reduce.34.cloned.1.call-done = f32[512,512]{1,0:T(8,128)} async-done(((f32[512,512]{1,0:T(8,128)}), f32[512,512]{1,0:T(8,128)}) %all-reduce.34.cloned.1.call-update) | async-done | bytes 1048592
  (574 shorter events, 234.9 us)
Async XLA Ops:
  7.2 362.9 %all-gather.8.cloned.1.call-start = ((), (), s32[]{:S(2)}) async-start(), calls=%async_computation.1 | async-start | bytes 1056768 | tf_op jit(solution)/shard_map/all_gather | solution.py:190
  18.1 99.5 %collective-permute-start.1 = (s32[4]{0:T(128)}, s32[4]{0:T(128)S(1)}, u32[]{:S(2)}, u32[]{:S(2)}) collective-permute-start(s32[4]{0:T(128)} %param.41), channel_id=1, source_target_pairs={{0,64},{1,65},{2,66},{3,67},{4,68},{5,69},{6,70},{7,71},{8,72},{9,... | collective-permute-start | bytes 56 | tf_op jit(solution)/shard_map/ppermute | solution.py:10
  29.1 89.4 %collective-permute-start = (s32[4]{0:T(128)}, s32[4]{0:T(128)S(1)}, u32[]{:S(2)}, u32[]{:S(2)}) collective-permute-start(s32[4]{0:T(128)} %param.42), channel_id=1, source_target_pairs={{0,64},{1,65},{2,66},{3,67},{4,68},{5,69},{6,70},{7,71},{8,72},{9,... | collective-permute-start | bytes 56 | tf_op jit(solution)/shard_map/ppermute | solution.py:10
  31.0 88.6 %collective-permute-start.2 = (bf16[4,64,512]{2,1,0:T(8,128)(2,1)}, bf16[4,64,512]{2,1,0:T(8,128)(2,1)S(1)}, u32[]{:S(2)}, u32[]{:S(2)}) collective-permute-start(bf16[4,64,512]{2,1,0:T(8,128)(2,1)} %param.40), channel_id=1, source_target_pairs={{0,64},{1,65},{2,66},{3,67},{4,68},{5,69},{6,70},{7,71},{8,72},{9,... | collective-permute-start | bytes 786440 | tf_op jit(solution)/shard_map/ppermute | solution.py:10
  119.5 7.2 copy-start.54
  120.5 6.2 collective-permute-start.3
  127.4 6.4 collective-permute-start.4
  134.4 67.5 %collective-permute-start.5 = (bf16[1,64,512]{2,1,0:T(8,128)(2,1)}, bf16[1,64,512]{2,1,0:T(8,128)(2,1)S(1)}, u32[]{:S(2)}, u32[]{:S(2)}) collective-permute-start(bf16[1,64,512]{2,1,0:T(8,128)(2,1)} %get-tuple-element.1096), channel_id=1, source_target_pairs={{0,128},{128,256},{256,384},{1,129},{129,257},{257,385},{2,130},{1... | collective-permute-start | bytes 196616 | tf_op jit(solution)/shard_map/ppermute | solution.py:16
  224.4 6.4 collective-permute-start.6
  253.4 6.4 collective-permute-start.7
  282.1 6.4 collective-permute-start.8
  288.5 21.9 %copy-start.4 = (bf16[4,64,512]{2,1,0:T(8,128)(2,1)S(1)}, bf16[4,64,512]{2,1,0:T(8,128)(2,1)}, u32[]{:S(2)}) copy-start(bf16[4,64,512]{2,1,0:T(8,128)(2,1)} %copy.744) | copy-start | bytes 786436
  310.4 55.8 %copy-start.53 = (s32[4,1]{0,1:T(1,128)S(1)}, s32[4,1]{0,1:T(1,128)}, u32[]{:S(2)}) copy-start(s32[4,1]{0,1:T(1,128)} %param.43) | copy-start | bytes 52
  310.4 61.3 %copy-start.55 = (s32[4]{0:T(128)S(1)}, s32[4]{0:T(128)}, u32[]{:S(2)}) copy-start(s32[4]{0:T(128)} %copy-done.54) | copy-start | bytes 52
  361.7 7.8 all-to-all-start
  366.2 523.1 %all-reduce.34.cloned.1.call-start = ((), (), s32[]{:S(2)}) async-start(), calls=%async_computation.2 | async-start | bytes 2097152
  371.7 30.4 %copy-start.56 = (s32[4]{0:T(128)S(1)}, s32[4]{0:T(128)}, u32[]{:S(2)}) copy-start(s32[4]{0:T(128)} %copy-done.54) | copy-start | bytes 52
  398.9 3.2 collective-permute-start.9
  433.5 6.9 collective-permute-start.10
  471.5 5.9 collective-permute-start.11
  511.1 6.9 collective-permute-start.12
  519.6 64.1 %collective-permute-start.13 = (bf16[1,64,512]{2,1,0:T(8,128)(2,1)S(1)}, bf16[1,64,512]{2,1,0:T(8,128)(2,1)S(1)}, u32[]{:S(2)}, u32[]{:S(2)}) collective-permute-start(bf16[1,64,512]{2,1,0:T(8,128)(2,1)S(1)} %get-tuple-element.655), channel_id=1, source_target_pairs={{128,0},{256,128},{384,256},{129,1},{257,129},{385,257},{130,2},{2... | collective-permute-start | bytes 196616 | tf_op jit(solution)/shard_map/ppermute | solution.py:16
  585.1 5.9 collective-permute-start.14
  597.4 293.2 %copy-start.27 = (bf16[1,4,64,512]{3,2,1,0:T(8,128)(2,1)}, bf16[1,4,64,512]{3,2,1,0:T(8,128)(2,1)S(1)}, u32[]{:S(2)}) copy-start(bf16[1,4,64,512]{3,2,1,0:T(8,128)(2,1)S(1)} %bitcast_dynamic-update-slice_fusion.13) | copy-start | bytes 786436
  (21 other events, 54.4 us)
Sparse Core Ops, SparseCore 0:
  18.2 84.6 all-gather.7
  597.4 291.8 all-reduce.33
where the time goes:
time: 910 us; the launch traced here: 898 us
  waiting for transfers between devices  379 us (42%)
  local copies, waits for them, and re-layouts  151 us (17%)
  blocking collectives  126 us (14%)
  starting transfers between devices  111 us (12%)
  matrix products  73.7 us (8%)
  other arithmetic  35 us (4%)
  between operations  16.1 us (2%)
    unnamed x3, waiting for transfers between devices  292 us
    gather x16, local copies, waits for them, and re-layouts, hstu_layer(): pos_bias = jnp.take(rel_bias, jnp.clip(offset, 0, positions - 1), axis=1)  109 us
    ppermute x12, starting transfers between devices, shifted(): lax.ppermute(value, axis, [(source, source + steps) for source in range(i...  85.9 us
    ppermute x12, waiting for transfers between devices, shifted(): lax.ppermute(value, axis, [(source, source + steps) for source in range(i...  84.9 us
    all_gather x1, blocking collectives, body(): piece_states = lax.all_gather(states, 'dp', axis=0, tiled=True)  49.3 us
    all_gather x1, blocking collectives, prefix(): everything = lax.all_gather(value, axis)  43 us
    dot_general x12, matrix products, hstu_layer(): jnp.dot(normed, w_uvqk, preferred_element_type=jnp.float32)  30.6 us
    unnamed x1, blocking collectives  22.7 us
  transfers between devices with their start and end apart: 18, of which 10 were waited for; matrix products, arithmetic and copies ran while one was open for 14% of the time, Pallas kernels for 0%

commit v1 on v0

v1 whole, which is shorter than its diff:
```python
import functools

import jax
import jax.numpy as jnp
from jax import lax
from jax.experimental import pallas as pl
from jax.experimental.pallas import tpu as pltpu
from jax.sharding import Mesh, PartitionSpec as P

BF = jnp.bfloat16
F32 = jnp.float32
DP = ("z", "y", "core")
DEV_HIST = 4
ROWS = 64
WIDTH = 512
HEAD_COLS = 64
PAIRS = 4
LAYERS = 4
SLOTS = 8
MSG = 208
NN = (((1,), (0,)), ((), ()))
NT = (((1,), (1,)), ((), ()))
TN = (((0,), (0,)), ((), ()))


def mm(a, b, dims=NN):
    return lax.dot_general(a, b, dims, preferred_element_type=F32)


def iota(shape, dim):
    return lax.broadcasted_iota(jnp.int32, shape, dim)


def row_mean(a):
    return jnp.mean(a, axis=-1, keepdims=True)


def sigmoid(a):
    return 0.5 * jnp.tanh(0.5 * a) + 0.5


def dp_place():
    ny, nc = lax.axis_size("y"), lax.axis_size("core")
    return (lax.axis_index("z") * ny + lax.axis_index("y")) * nc + lax.axis_index("core")


def wanted_value():
    upper = (lax.axis_index("z") >= lax.axis_size("z") // 2).astype(jnp.int32)
    return upper * DEV_HIST + lax.axis_index("segment")


def routing_kernel(block_rows, own_rows, table_ref, seg_ref, payload_ref, hot_ref, count_ref):
    n_dp = table_ref.shape[0]
    hist = n_dp * DEV_HIST
    me = dp_place()
    segment = lax.axis_index("segment")
    table = table_ref[...].astype(F32).astype(BF)
    spread = mm(table, (iota((128, hist), 0) == iota((128, hist), 1) % DEV_HIST).astype(BF))
    own = iota((n_dp, hist), 1) // DEV_HIST == iota((n_dp, hist), 0)
    routes = jnp.sum(jnp.where(own, spread, 0.0), axis=0, keepdims=True)
    hit = jnp.broadcast_to((routes == me.astype(F32)).astype(F32), (16, hist))
    earlier = (iota((hist, hist), 0) < iota((hist, hist), 1)).astype(BF)
    slot = mm(hit.astype(BF), earlier)
    hot = jnp.where(slot == iota((16, hist), 0).astype(F32), hit, 0.0).astype(BF)
    mine = (iota((hist, n_dp), 0) == iota((hist, n_dp), 1) * DEV_HIST + segment).astype(BF)
    picks = mm(hot, mine).astype(BF)
    cotangent = jnp.concatenate([seg_ref[q, 0:16, :] for q in range(LAYERS)], axis=1)
    payload_ref[...] = mm(picks, cotangent, TN).astype(BF)
    total = hot_ref.shape[2]
    place, history = iota((hist, total), 1), iota((hist, total), 0)
    within = place % block_rows - own_rows
    first = ((place // block_rows) * 2 + within) * DEV_HIST
    valid = (within >= 0) & (within < 2)
    for h in range(DEV_HIST):
        move = jnp.where(valid & (history == first + h), 1.0, 0.0).astype(BF)
        hot_ref[h] = mm(hot, move).astype(BF)
    other = lax.rem(me + n_dp // 2, n_dp)
    pair = jnp.concatenate([table_ref[pl.ds(me, 1), :], table_ref[pl.ds(other, 1), :]], axis=0)
    lane = iota((2, 128), 1)
    fits = (lane >= 4) & (lane < 8) & (pair // 128 == wanted_value())
    length = jnp.sum(jnp.where(fits, (pair % 128).astype(F32), 0.0), axis=1, keepdims=True)
    length = jnp.sum(length, axis=0, keepdims=True)
    count_ref[...] = jnp.broadcast_to(length, count_ref.shape).astype(jnp.int32)


def layers_kernel(
    plan_ref, events_ref, other_ref, count_ref, cot_ref, seg_ref,
    w_in_ref, w_out_ref, near_a, near_b, swap_a, swap_b, far_a, far_b,
    out_ref,
    weights, proj_s, dsilu_s, normed_s, rstd_s, norm_o_s, rstd_o_s, bias_s, att_s, datt_s, sems,
):
    segment, core = lax.axis_index("segment"), lax.axis_index("core")
    half = WIDTH // 2
    near = lax.rem(segment + 1 + 2 * core, LAYERS)
    swap = lax.rem(segment + 3 + 2 * core, LAYERS)
    far = lax.rem(segment + 2, LAYERS)
    low = pl.ds(pl.multiple_of(core * half, half), half)
    high = pl.ds(pl.multiple_of((1 - core) * half, half), half)
    pltpu.make_async_copy(w_in_ref, weights.at[segment, :, pl.ds(0, 4 * WIDTH)], sems.at[segment]).start()
    pltpu.make_async_copy(w_out_ref, weights.at[segment, :, pl.ds(4 * WIDTH, WIDTH)], sems.at[segment]).start()
    pltpu.make_async_copy(near_a, weights.at[near, low], sems.at[near]).start()
    pltpu.make_async_copy(near_b, weights.at[near, high], sems.at[near]).start()
    pltpu.make_async_copy(swap_a, weights.at[swap, high], sems.at[swap]).start()
    pltpu.make_async_copy(swap_b, weights.at[swap, low], sems.at[swap]).start()
    pltpu.make_async_copy(far_a, weights.at[far, low], sems.at[far]).start()
    pltpu.make_async_copy(far_b, weights.at[far, high], sems.at[far]).start()

    lane, row = iota((ROWS, 128), 1), iota((ROWS, 128), 0)
    left = (lane < HEAD_COLS).astype(F32)
    left_b, right_b = left.astype(BF), (1.0 - left).astype(BF)
    column = jnp.where(lane < HEAD_COLS, lane, lane - HEAD_COLS)
    count = count_ref[...]
    allowed = (column <= row) & (column < count)

    for l in range(LAYERS):
        table = seg_ref[l, 16:32, :].astype(F32)
        table = table[0:4] + table[4:8] + table[8:12]
        for p in range(PAIRS):
            wide = jnp.broadcast_to(table[p : p + 1], (ROWS, 128))
            bias_s[l, p] = pltpu.roll(wide, 0, 1, stride=1, stride_axis=0)

    def block_diagonal(a):
        return jnp.concatenate([a * left_b, a * right_b], axis=0)

    def merge(a):
        return jnp.where(lane < HEAD_COLS, a[:ROWS], a[ROWS:])

    def part(kind, p):
        return pl.ds(kind * WIDTH + p * 128, 128)

    value = wanted_value()
    found = jnp.int32(0)
    acts = jnp.zeros((ROWS, WIDTH), F32)
    for h in range(DEV_HIST):
        same = (plan_ref[h] == value).astype(jnp.int32)
        found = found + same
        acts = jnp.where(same == 1, events_ref[h].astype(F32), acts)
    acts = jnp.where(found > 0, acts, other_ref[...].astype(F32))

    for l in range(LAYERS):
        average = row_mean(acts)
        centred = acts - average
        rstd = lax.rsqrt(row_mean(centred * centred) + 1e-6)
        normed = centred * rstd
        normed_s[l] = normed
        rstd_s[l] = jnp.broadcast_to(rstd, (ROWS, 128))
        pltpu.make_async_copy(weights.at[l], weights.at[l], sems.at[l]).wait()
        normed_b = normed.astype(BF)
        for kind in range(4):
            cols = pl.ds(kind * WIDTH, WIDTH)
            pre = mm(normed_b, weights[l, :, cols])
            gated = sigmoid(pre)
            silu = pre * gated
            proj_s[l, :, cols] = silu.astype(BF)
            dsilu_s[l, :, cols] = gated + silu * (1.0 - gated)
        outs = []
        for p in range(PAIRS):
            keys = block_diagonal(proj_s[l, :, part(3, p)])
            score = mm(proj_s[l, :, part(2, p)], keys, NT) * 0.125 + bias_s[l, p]
            gated = sigmoid(score)
            silu = score * gated
            att = jnp.where(allowed, silu, 0.0).astype(BF)
            att_s[l, p] = att
            datt_s[l, p] = jnp.where(allowed, gated + silu * (1.0 - gated), 0.0) * 0.125
            outs.append(mm(att, block_diagonal(proj_s[l, :, part(1, p)])))
        mixed = jnp.concatenate(outs, axis=1)
        centred = mixed - row_mean(mixed)
        rstd = lax.rsqrt(row_mean(centred * centred) + 1e-6)
        norm_o = centred * rstd
        norm_o_s[l] = norm_o
        rstd_o_s[l] = jnp.broadcast_to(rstd, (ROWS, 128))
        branch = (norm_o * proj_s[l, :, pl.ds(0, WIDTH)].astype(F32)).astype(BF)
        out_ref[l, 64:128, :] = branch
        acts = (acts + mm(branch, weights[l, :, pl.ds(4 * WIDTH, WIDTH)])).astype(BF).astype(F32)

    last = iota((ROWS, WIDTH), 0) == count[:, 0:1] - 1
    state = jnp.sum(jnp.where(last, acts, 0.0), axis=0, keepdims=True)
    for q in range(LAYERS):
        quarter = jnp.broadcast_to(state[:, 128 * q : 128 * q + 128], (16, 128))
        out_ref[q, 192:208, :] = jnp.concatenate([quarter] * 4, axis=1).astype(BF)
    seed = jnp.sum(cot_ref[...].astype(F32), axis=0, keepdims=True)
    cot = jnp.where(last, jnp.broadcast_to(seed, (ROWS, WIDTH)), 0.0).astype(BF)

    for l in reversed(range(LAYERS)):
        out_ref[l, 128:192, :] = cot
        d_branch = mm(cot, weights[l, :, pl.ds(4 * WIDTH, WIDTH)], NT).astype(BF).astype(F32)
        norm_o = norm_o_s[l]
        d_gate = (d_branch * norm_o).astype(BF)
        d_norm = d_branch * proj_s[l, :, pl.ds(0, WIDTH)].astype(F32)
        d_mixed = rstd_o_s[l][:, 0:1] * (d_norm - row_mean(d_norm) - norm_o * row_mean(d_norm * norm_o))
        d_mixed = d_mixed.astype(BF)
        d_value, d_query, d_key = [], [], []
        for p in range(PAIRS):
            d_out = d_mixed[:, 128 * p : 128 * p + 128]
            d_att = mm(d_out, block_diagonal(proj_s[l, :, part(1, p)]), NT).astype(BF).astype(F32)
            d_value.append(merge(mm(att_s[l, p], d_out, TN)))
            d_score = (d_att * datt_s[l, p]).astype(BF)
            d_query.append(mm(d_score, block_diagonal(proj_s[l, :, part(3, p)])))
            d_key.append(merge(mm(d_score, proj_s[l, :, part(2, p)], TN)))
        d_normed = jnp.zeros((ROWS, WIDTH), F32)
        for kind, pieces in enumerate(([d_gate], d_value, d_query, d_key)):
            cols = pl.ds(kind * WIDTH, WIDTH)
            whole = pieces[0] if len(pieces) == 1 else jnp.concatenate(pieces, axis=1)
            d_pre = whole.astype(BF).astype(F32) * dsilu_s[l, :, cols]
            d_normed = d_normed + mm(d_pre.astype(BF), weights[l, :, cols], NT)
        d_normed = d_normed.astype(BF).astype(F32)
        normed = normed_s[l]
        d_in = rstd_s[l][:, 0:1] * (d_normed - row_mean(d_normed) - normed * row_mean(d_normed * normed))
        cot = (d_in + cot.astype(F32)).astype(BF)
        out_ref[l, 0:64, :] = cot


def gradient_kernel(own_rows, got_ref, grads_ref, keep_ref, send_ref):
    core = lax.axis_index("core")
    for t in range(LAYERS):
        grads_ref[t] = got_ref[t, 0:64, :]
    branch = jnp.concatenate([got_ref[t, 64:128, :] for t in range(LAYERS)], axis=0)
    cot = jnp.concatenate([got_ref[t, 128:192, :] for t in range(LAYERS)], axis=0)
    half = WIDTH // 2
    to, source = iota((WIDTH, WIDTH), 1), iota((WIDTH, WIDTH), 0)
    side = jnp.where(to < half, core, 1 - core)
    within = jnp.where(to < half, to, to - half)
    wanted = (within // own_rows) * (2 * own_rows) + side * own_rows + within % own_rows
    order = (source == wanted).astype(F32).astype(BF)
    ordered = mm(branch, order).astype(BF)
    keep_ref[...] = mm(ordered[:, :half], cot, TN)
    send_ref[0:half, :] = mm(ordered[:, half:], cot, TN).astype(BF)
    states = [got_ref[t, 192:208, 0:128] for t in range(LAYERS)]
    send_ref[half : half + 16, :] = jnp.concatenate(states, axis=1)


def packing_kernel(block_rows, own_rows, keep_ref, send_ref, got_ref, out_ref):
    half = WIDTH // 2
    core = lax.axis_index("core")
    total = (keep_ref[...] + got_ref[0:half, :].astype(F32)).astype(BF)
    rows = out_ref.shape[0]
    place, source = iota((rows, half), 0), iota((rows, half), 1)
    within = place % block_rows
    pick = (within < own_rows) & (source == (place // block_rows) * own_rows + within)
    laid = mm(pick.astype(F32).astype(BF), total)
    own = send_ref[half : half + 16, :].astype(F32)[0:1]
    other = got_ref[half : half + 16, :].astype(F32)[0:1]
    first = jnp.where(core == 0, own, other)
    second = jnp.where(core == 0, other, own)
    at = iota((rows, WIDTH), 0) % block_rows
    laid = laid + jnp.where(at == own_rows, first, 0.0) + jnp.where(at == own_rows + 1, second, 0.0)
    out_ref[...] = laid.astype(BF)


def result_kernel(block_rows, got_ref, hot_ref, served_ref, weight_ref):
    rows = got_ref.shape[0]
    out_rows = weight_ref.shape[0]
    lead = max(16, out_rows)
    pick = (iota((lead, rows), 1) % block_rows == iota((lead, rows), 0)).astype(F32).astype(BF)
    got = got_ref[...]
    weight_ref[...] = mm(pick, got)[0:out_rows]
    served = jnp.zeros((16, 128), F32)
    for h in range(DEV_HIST):
        served = served + mm(hot_ref[h], got[:, 128 * h : 128 * h + 128])
    served_ref[...] = served[0:SLOTS].astype(BF)


def shape(dims, dtype):
    return jax.ShapeDtypeStruct(dims, dtype)


def call(kernel, outs, scratch=(), in_specs=None, limit=48):
    specs = {} if in_specs is None else {"in_specs": in_specs}
    return pl.pallas_call(
        kernel,
        out_shape=outs,
        scratch_shapes=scratch,
        **specs,
        compiler_params=pltpu.CompilerParams(vmem_limit_bytes=limit * 1024 * 1024),
    )


def body(events, lengths, balance_plan, routes, w_uvqk, w_out, rel_bias, state_cotangent):
    n_z, n_y, n_core = (lax.axis_size(a) for a in DP)
    n_dp = n_z * n_y * n_core
    chips = n_z * n_y
    core = lax.axis_index("core")
    own_rows = WIDTH // n_dp
    block_rows = -(-(own_rows + 2) // 8) * 8
    half = WIDTH // 2

    with jax.named_scope("section_weights"):
        ring = [(s * 2, (s - 1) % LAYERS * 2) for s in range(LAYERS)]
        ring += [(s * 2 + 1, (s + 1) % LAYERS * 2 + 1) for s in range(LAYERS)]
        swap = [(0, 1), (1, 0)]
        w_in, w_back = w_uvqk[0], w_out[0]
        upper = jnp.concatenate([w_in[:half], w_back[:half]], axis=1)
        lower = jnp.concatenate([w_in[half:], w_back[half:]], axis=1)
        first = jnp.where(core == 0, upper, lower)
        second = jnp.where(core == 0, lower, upper)
        near_a = lax.ppermute(first, ("segment", "core"), ring)
        near_b = lax.ppermute(second, ("segment", "core"), ring)
        far_a = lax.ppermute(near_a, ("segment", "core"), ring)
        swap_a = lax.ppermute(near_a, "core", swap)
        swap_b = lax.ppermute(near_b, "core", swap)
        far_b = lax.ppermute(far_a, "core", swap)

    with jax.named_scope("events"):
        partner_value = DEV_HIST + 2 * lax.axis_index("segment") - wanted_value()
        chosen = (balance_plan == partner_value)[:, None, None]
        outgoing = jnp.sum(jnp.where(chosen, events, jnp.zeros((), BF)), axis=0, dtype=BF)
        other_events = lax.ppermute(outgoing, "z", [(i, (i + n_z // 2) % n_z) for i in range(n_z)])

    with jax.named_scope("routing"):
        packed = balance_plan * 128 + lengths
        facts = jnp.concatenate([routes[:, 0], packed, jnp.zeros((120,), jnp.int32)])
        table = lax.all_gather(facts, DP)
        table = table.reshape(n_dp, 128)
        even, odd = rel_bias[0, 0::2], rel_bias[0, 1::2]
        base = jnp.concatenate([even[:, 0:1], odd[:, ::-1], even[:, :0:-1]], axis=1)
        high = lax.reduce_precision(base, 8, 7)
        middle = lax.reduce_precision(base - high, 8, 7)
        low = base - high - middle
        cot = jnp.concatenate(
            [state_cotangent[0], jnp.zeros((8, 128), BF)]
            + [a.astype(BF) for a in (high, middle, low)]
            + [jnp.zeros((4, 128), BF)]
        )
        seg_facts = lax.all_gather(cot, "segment")
        payload, hot, count = call(
            functools.partial(routing_kernel, block_rows, own_rows),
            (
                shape((n_dp, WIDTH), BF),
                shape((DEV_HIST, 16, chips * block_rows), BF),
                shape((ROWS, 128), jnp.int32),
            ),
        )(table, seg_facts)
        cot_rows = lax.all_to_all(payload.reshape(n_dp, 1, WIDTH), DP, 0, 0, tiled=True)
        cot_rows = cot_rows.reshape(n_dp, WIDTH)

    any_spec, vmem = pl.BlockSpec(memory_space=pl.ANY), pl.BlockSpec(memory_space=pltpu.VMEM)
    with jax.named_scope("layers"):
        message = call(
            layers_kernel,
            shape((LAYERS, MSG, WIDTH), BF),
            scratch=[
                pltpu.VMEM((LAYERS, WIDTH, 5 * WIDTH), BF),
                pltpu.VMEM((LAYERS, ROWS, 4 * WIDTH), BF),
                pltpu.VMEM((LAYERS, ROWS, 4 * WIDTH), F32),
                pltpu.VMEM((LAYERS, ROWS, WIDTH), F32),
                pltpu.VMEM((LAYERS, ROWS, 128), F32),
                pltpu.VMEM((LAYERS, ROWS, WIDTH), F32),
                pltpu.VMEM((LAYERS, ROWS, 128), F32),
                pltpu.VMEM((LAYERS, PAIRS, ROWS, 128), F32),
                pltpu.VMEM((LAYERS, PAIRS, ROWS, 128), BF),
                pltpu.VMEM((LAYERS, PAIRS, ROWS, 128), F32),
                pltpu.SemaphoreType.DMA((LAYERS,)),
            ],
            in_specs=[pl.BlockSpec(memory_space=pltpu.SMEM)] + [vmem] * 5 + [any_spec] * 8,
        )(
            balance_plan, events, other_events, count, cot_rows, seg_facts,
            w_in, w_back, near_a, near_b, swap_a, swap_b, far_a, far_b,
        )

    with jax.named_scope("section_exchange"):
        arrived = lax.all_to_all(message, "segment", 0, 0, tiled=True)
    with jax.named_scope("weight_gradient"):
        grads, keep, send = call(
            functools.partial(gradient_kernel, own_rows),
            (
                shape((LAYERS, ROWS, WIDTH), BF),
                shape((half, WIDTH), F32),
                shape((half + 16, WIDTH), BF),
            ),
        )(arrived)
        partner = lax.ppermute(send, "core", swap)
        blocks = call(
            functools.partial(packing_kernel, block_rows, own_rows),
            shape((chips * block_rows, WIDTH), BF),
        )(keep, send, partner)
        blocks = lax.all_to_all(
            blocks.reshape(chips, block_rows, WIDTH), ("z", "y"), 0, 0, tiled=True
        )
        served, weight = call(
            functools.partial(result_kernel, block_rows),
            (shape((SLOTS, 128), BF), shape((own_rows, WIDTH), F32)),
        )(blocks.reshape(chips * block_rows, WIDTH), hot)
    return served[None], grads[None], weight[None]


def solution(mesh):
    devices = mesh.devices
    n_segment, n_dp = devices.shape
    side = 1
    while side * side * 2 < n_dp:
        side *= 2
    fine = Mesh(
        devices.reshape(n_segment, n_dp // (2 * side), side, 2), ("segment",) + DP
    )
    return jax.shard_map(
        body,
        mesh=fine,
        in_specs=(
            P(DP, None, None),
            P(DP),
            P(DP),
            P(DP, None),
            P("segment", None, None),
            P("segment", None, None),
            P("segment", None, None),
            P(DP, None, "segment"),
        ),
        out_specs=(
            P(DP, None, "segment"),
            P("segment", DP, None, None),
            P("segment", DP, None),
        ),
        check_vma=False,
    )
```

time: 910 us -> 218 us (0.24)
  the two profiles are of different devices: /device:TPU:30 before, /device:TPU:8 now
where the time goes in v1:
time: 218 us; the launch traced here: 217 us
  blocking collectives  108 us (50%)
  starting transfers between devices  39.6 us (18%)
  waiting for transfers between devices  35.6 us (16%)
  Pallas kernels  19.7 us (9%)
  local copies, waits for them, and re-layouts  9.61 us (4%)
  other arithmetic  3.71 us (2%)
    all_gather x1, blocking collectives, body(): table = lax.all_gather(facts, DP)  49.2 us
    all_to_all x1, blocking collectives, body(): lax.all_to_all(blocks.reshape(chips, block_rows, WIDTH), ('z', 'y'), 0, 0...  27.9 us
    all_to_all x1, blocking collectives, body(): arrived = lax.all_to_all(message, 'segment', 0, 0, tiled=True)  18.2 us
    pallas_call x1, Pallas kernels, body(): call(layers_kernel, shape((LAYERS, MSG, WIDTH), BF), scratch=[pltpu.VMEM(...  16.2 us
    all_gather x1, blocking collectives, body(): seg_facts = lax.all_gather(cot, 'segment')  12.5 us
    ppermute x1, waiting for transfers between devices, body(): near_a = lax.ppermute(first, ('segment', 'core'), ring)  12.4 us
    ppermute x1, waiting for transfers between devices, body(): far_a = lax.ppermute(near_a, ('segment', 'core'), ring)  12.1 us
    all_to_all x1, starting transfers between devices, body(): lax.all_to_all(payload.reshape(n_dp, 1, WIDTH), DP, 0, 0, tiled=True)  11.1 us
  transfers between devices with their start and end apart: 9, of which 5 were waited for; matrix products, arithmetic and copies ran while one was open for 4% of the time, Pallas kernels for 0%

profile of v1, /device:TPU:8, one launch (start us, length us, event | category | flops | bytes accessed | tf_op | source)
XLA Modules:
  0.0 217.0 jit_solution(6863102505367750981)
XLA Ops:
  1.7 1.8 slice_bitcast_fusion.1
  4.1 4.8 %collective-permute-start.1 = (bf16[256,2560]{1,0:T(8,128)(2,1)S(1)}, bf16[256,2560]{1,0:T(8,128)(2,1)S(1)}, u32[]{:S(2)}, u32[]{:S(2)}) collective-permute-start(bf16[256,2560]{1,0:T(8,128)(2,1)S(1)} %get-tuple-element.22), channel_id=1, source_target_pairs={{0,384},{128,0},{256,128},{384,256},{1,129},{129,257},{257,385},{3... | collective-permute-start | bytes 3932168 | tf_op jit(solution)/shard_map/section_weights/ppermute | solution.py:296
  8.9 2.7 %collective-permute-start.2 = (bf16[256,2560]{1,0:T(8,128)(2,1)S(1)}, bf16[256,2560]{1,0:T(8,128)(2,1)S(1)}, u32[]{:S(2)}, u32[]{:S(2)}) collective-permute-start(bf16[256,2560]{1,0:T(8,128)(2,1)S(1)} %get-tuple-element.21), channel_id=1, source_target_pairs={{0,384},{128,0},{256,128},{384,256},{1,129},{129,257},{257,385},{3... | collective-permute-start | bytes 3932168 | tf_op jit(solution)/shard_map/section_weights/ppermute | solution.py:297
  11.7 12.4 %collective-permute-done.1.near_a = bf16[256,2560]{1,0:T(8,128)(2,1)S(1)} collective-permute-done((bf16[256,2560]{1,0:T(8,128)(2,1)S(1)}, bf16[256,2560]{1,0:T(8,128)(2,1)S(1)}, u32[]{:S(2)}, u32[]{:S(2)}) %collective-permute-start.1) | collective-permute-done | bytes 1310752 | tf_op jit(solution)/shard_map/section_weights/ppermute | solution.py:296
  24.0 5.6 %collective-permute-start.5 = (bf16[256,2560]{1,0:T(8,128)(2,1)S(1)}, bf16[256,2560]{1,0:T(8,128)(2,1)}, u32[]{:S(2)}, u32[]{:S(2)}) collective-permute-start(bf16[256,2560]{1,0:T(8,128)(2,1)S(1)} %collective-permute-done.1.near_a), channel_id=1, source_target_pairs={{0,384},{128,0},{256,128},{384,256},{1,129},{129,257},{257,385},{3... | collective-permute-start | bytes 3932168 | tf_op jit(solution)/shard_map/section_weights/ppermute | solution.py:298
  29.6 1.9 collective-permute-start.3
  31.5 6.5 %collective-permute-done.2.near_b = bf16[256,2560]{1,0:T(8,128)(2,1)S(1)} collective-permute-done((bf16[256,2560]{1,0:T(8,128)(2,1)S(1)}, bf16[256,2560]{1,0:T(8,128)(2,1)S(1)}, u32[]{:S(2)}, u32[]{:S(2)}) %collective-permute-start.2) | collective-permute-done | bytes 1310752 | tf_op jit(solution)/shard_map/section_weights/ppermute | solution.py:297
  38.1 1.9 collective-permute-start.4
  40.0 12.1 %collective-permute-done.5.far_a = bf16[256,2560]{1,0:T(8,128)(2,1)} collective-permute-done((bf16[256,2560]{1,0:T(8,128)(2,1)S(1)}, bf16[256,2560]{1,0:T(8,128)(2,1)}, u32[]{:S(2)}, u32[]{:S(2)}) %collective-permute-start.5) | collective-permute-done | bytes 1310752 | tf_op jit(solution)/shard_map/section_weights/ppermute | solution.py:298
  52.1 1.9 collective-permute-start.6
  54.5 12.5 %all-gather.1 = bf16[128,128]{1,0:T(8,128)(2,1)S(1)} all-gather(bf16[32,128]{1,0:T(8,128)(2,1)S(1)} %concatenate.17), channel_id=3, replica_groups=mesh['segment'=4,'z'=8,'y'=8,'core'=2] {'segment'}, dimensions={0}, use_global_device_ids=true | all-gather | bytes 40960 | tf_op jit(solution)/shard_map/routing/all_gather | solution.py:324
  67.1 49.2 %all-gather.2 = s32[128,1,128]{2,1,0:T(1,128)S(1)} all-gather(s32[1,1,128]{2,1,0:T(1,128)S(1)} %add_bitcast_fusion), channel_id=2, replica_groups=mesh['segment'=4,'z'=8,'y'=8,'core'=2] {'z','y','core'}, dimensions={0}, use_global_device_ids=true | all-gather | bytes 66048 | tf_op jit(solution)/shard_map/routing/all_gather | solution.py:312
  119.2 2.3 %reduce = bf16[128,512]{1,0:T(8,128)(2,1)} reduce(bf16[128,1,512]{2,0,1:T(8,128)(2,1)} %bitcast.35, bf16[]{:T(256)} %broadcast.7), dimensions={1}, to_apply=%copy.13.reduce_sub_computation | reduce | bytes 262146 | tf_op jit(solution)/shard_map/routing/reshape | solution.py:333
  121.5 1.6 reshape.32
  123.1 11.1 %all-to-all-start = ((bf16[128,2,256]{2,1,0:T(2,128)(2,1)}), bf16[128,2,256]{2,1,0:T(2,128)(2,1)}, u32[]{:S(2)}, u32[]{:S(2)}) async-start(bf16[128,2,256]{2,1,0:T(2,128)(2,1)} %reshape.32), calls=%async_computation | async-start | bytes 262144 | tf_op jit(solution)/shard_map/routing/all_to_all | solution.py:333
  135.0 7.8 %collective-permute-start = (bf16[64,512]{1,0:T(8,128)(2,1)}, bf16[64,512]{1,0:T(8,128)(2,1)S(1)}, u32[]{:S(2)}, u32[]{:S(2)}) collective-permute-start(bf16[64,512]{1,0:T(8,128)(2,1)} %select_reduce_fusion), channel_id=1, source_target_pairs={{0,64},{16,80},{32,96},{48,112},{64,0},{80,16},{96,32},{112,48},{1... | collective-permute-start | bytes 196616 | tf_op jit(solution)/shard_map/events/ppermute | solution.py:307
  142.8 3.1 %all-to-all-done = bf16[128,2,256]{2,1,0:T(2,128)(2,1)} async-done(((bf16[128,2,256]{2,1,0:T(2,128)(2,1)}), bf16[128,2,256]{2,1,0:T(2,128)(2,1)}, u32[]{:S(2)}, u32[]{:S(2)}) %all-to-all-start) | async-done | bytes 131104 | tf_op jit(solution)/shard_map/routing/all_to_all | solution.py:333
  145.8 2.0 reshape.33
  148.8 16.2 %layers.1 = bf16[4,208,512]{2,1,0:T(8,128)(2,1)S(1)} custom-call(s32[4]{0:T(128)S(1)} %copy-done.5, bf16[4,64,512]{2,1,0:T(8,128)(2,1)S(1)} %copy-done.1, bf16[64,512]{1,0:T(8,128)(2,1)S(1)} %collective-permute-done.other_ref, s32[64,128]{1,0:T(8,128)S(1)} %get-tuple-element.11.count_ref, bf16[128,512]{1,0:T(8,128)(2,1)S(1)} %bitcast.31, ...), custom_call_target="tpu_custom_call" | custom-call | tf_op jit(solution)/shard_map/layers/pallas_call | solution.py:338
  165.0 18.2 %all_to_all.15.got_ref = bf16[4,208,512]{2,1,0:T(8,128)(2,1)S(1)} all-to-all(bf16[4,208,512]{2,1,0:T(8,128)(2,1)S(1)} %layers.1), channel_id=1, replica_groups=mesh['segment'=4,'z'=8,'y'=8,'core'=2] {'segment'}, dimensions={0} | all-to-all | bytes 1703936 | tf_op jit(solution)/shard_map/section_exchange/all_to_all | solution.py:361
  183.2 1.3 weight_gradient.3
  184.5 1.9 collective-permute-start.7
  186.4 1.5 collective-permute-done.7.got_ref
  188.3 27.9 %all_to_all.16 = bf16[64,8,512]{2,1,0:T(8,128)(2,1)S(1)} all-to-all(bf16[64,8,512]{2,1,0:T(8,128)(2,1)S(1)} %bitcast.29), channel_id=1, replica_groups=mesh['segment'=4,'z'=8,'y'=8,'core'=2] {'z','y'}, dimensions={0} | all-to-all | bytes 1048576 | tf_op jit(solution)/shard_map/weight_gradient/all_to_all | solution.py:376
  (46 shorter events, 8.0 us)
Async XLA Ops:
  3.5 50.5 %copy-start.6 = (f32[1,8,64]{2,1,0:T(8,128)S(1)}, f32[1,8,64]{2,1,0:T(8,128)}, u32[]{:S(2)}) copy-start(f32[1,8,64]{2,1,0:T(8,128)} %param.14) | copy-start | bytes 6148
  3.5 50.9 %copy-start.7 = (bf16[1,8,128]{2,1,0:T(8,128)(2,1)S(1)}, bf16[1,8,128]{2,1,0:T(8,128)(2,1)}, u32[]{:S(2)}) copy-start(bf16[1,8,128]{2,1,0:T(8,128)(2,1)} %param.15) | copy-start | bytes 6148
  3.5 63.5 %copy-start.5 = (s32[4]{0:T(128)S(1)}, s32[4]{0:T(128)}, u32[]{:S(2)}) copy-start(s32[4]{0:T(128)} %plan_ref.1) | copy-start | bytes 52
  3.5 63.5 %copy-start.9 = (s32[4]{0:T(128)S(1)}, s32[4]{0:T(128)}, u32[]{:S(2)}) copy-start(s32[4]{0:T(128)} %param.9) | copy-start | bytes 52
  3.5 63.5 %copy-start.8 = (s32[4,1]{0,1:T(1,128)S(1)}, s32[4,1]{0,1:T(1,128)}, u32[]{:S(2)}) copy-start(s32[4,1]{0,1:T(1,128)} %param.11) | copy-start | bytes 52
  3.6 130.7 %copy-start.1 = (bf16[4,64,512]{2,1,0:T(8,128)(2,1)S(1)}, bf16[4,64,512]{2,1,0:T(8,128)(2,1)}, u32[]{:S(2)}) copy-start(bf16[4,64,512]{2,1,0:T(8,128)(2,1)} %events_ref.1) | copy-start | bytes 786436
  4.1 144.7 %copy-start = (bf16[1,512,512]{2,1,0:T(8,128)(2,1)S(1)}, bf16[1,512,512]{2,1,0:T(8,128)(2,1)}, u32[]{:S(2)}) copy-start(bf16[1,512,512]{2,1,0:T(8,128)(2,1)} %param.13) | copy-start | bytes 1572868
  4.1 19.9 %collective-permute-start.1 = (bf16[256,2560]{1,0:T(8,128)(2,1)S(1)}, bf16[256,2560]{1,0:T(8,128)(2,1)S(1)}, u32[]{:S(2)}, u32[]{:S(2)}) collective-permute-start(bf16[256,2560]{1,0:T(8,128)(2,1)S(1)} %get-tuple-element.22), channel_id=1, source_target_pairs={{0,384},{128,0},{256,128},{384,256},{1,129},{129,257},{257,385},{3... | collective-permute-start | bytes 3932168 | tf_op jit(solution)/shard_map/section_weights/ppermute | solution.py:296
  8.9 29.1 %collective-permute-start.2 = (bf16[256,2560]{1,0:T(8,128)(2,1)S(1)}, bf16[256,2560]{1,0:T(8,128)(2,1)S(1)}, u32[]{:S(2)}, u32[]{:S(2)}) collective-permute-start(bf16[256,2560]{1,0:T(8,128)(2,1)S(1)} %get-tuple-element.21), channel_id=1, source_target_pairs={{0,384},{128,0},{256,128},{384,256},{1,129},{129,257},{257,385},{3... | collective-permute-start | bytes 3932168 | tf_op jit(solution)/shard_map/section_weights/ppermute | solution.py:297
  24.0 28.1 %collective-permute-start.5 = (bf16[256,2560]{1,0:T(8,128)(2,1)S(1)}, bf16[256,2560]{1,0:T(8,128)(2,1)}, u32[]{:S(2)}, u32[]{:S(2)}) collective-permute-start(bf16[256,2560]{1,0:T(8,128)(2,1)S(1)} %collective-permute-done.1.near_a), channel_id=1, source_target_pairs={{0,384},{128,0},{256,128},{384,256},{1,129},{129,257},{257,385},{3... | collective-permute-start | bytes 3932168 | tf_op jit(solution)/shard_map/section_weights/ppermute | solution.py:298
  29.6 119.2 %collective-permute-start.3 = (bf16[256,2560]{1,0:T(8,128)(2,1)S(1)}, bf16[256,2560]{1,0:T(8,128)(2,1)}, u32[]{:S(2)}, u32[]{:S(2)}) collective-permute-start(bf16[256,2560]{1,0:T(8,128)(2,1)S(1)} %collective-permute-done.1.near_a), channel_id=1, source_target_pairs={{0,1},{1,0},{2,3},{3,2},{4,5},{5,4},{6,7},{7,6},{8,9},{9,8},{10,11... | collective-permute-start | bytes 3932168 | tf_op jit(solution)/shard_map/section_weights/ppermute | solution.py:299
  38.1 110.7 %collective-permute-start.4 = (bf16[256,2560]{1,0:T(8,128)(2,1)S(1)}, bf16[256,2560]{1,0:T(8,128)(2,1)}, u32[]{:S(2)}, u32[]{:S(2)}) collective-permute-start(bf16[256,2560]{1,0:T(8,128)(2,1)S(1)} %collective-permute-done.2.near_b), channel_id=1, source_target_pairs={{0,1},{1,0},{2,3},{3,2},{4,5},{5,4},{6,7},{7,6},{8,9},{9,8},{10,11... | collective-permute-start | bytes 3932168 | tf_op jit(solution)/shard_map/section_weights/ppermute | solution.py:300
  52.1 96.7 %collective-permute-start.6 = (bf16[256,2560]{1,0:T(8,128)(2,1)}, bf16[256,2560]{1,0:T(8,128)(2,1)}, u32[]{:S(2)}, u32[]{:S(2)}) collective-permute-start(bf16[256,2560]{1,0:T(8,128)(2,1)} %collective-permute-done.5.far_a), channel_id=1, source_target_pairs={{0,1},{1,0},{2,3},{3,2},{4,5},{5,4},{6,7},{7,6},{8,9},{9,8},{10,11... | collective-permute-start | bytes 3932168 | tf_op jit(solution)/shard_map/section_weights/ppermute | solution.py:301
  117.4 0.7 copy-start.2
  118.1 0.6 copy-start.3
  123.1 22.7 %all-to-all-start = ((bf16[128,2,256]{2,1,0:T(2,128)(2,1)}), bf16[128,2,256]{2,1,0:T(2,128)(2,1)}, u32[]{:S(2)}, u32[]{:S(2)}) async-start(bf16[128,2,256]{2,1,0:T(2,128)(2,1)} %reshape.32), calls=%async_computation | async-start | bytes 262144 | tf_op jit(solution)/shard_map/routing/all_to_all | solution.py:333
  135.0 13.8 %collective-permute-start = (bf16[64,512]{1,0:T(8,128)(2,1)}, bf16[64,512]{1,0:T(8,128)(2,1)S(1)}, u32[]{:S(2)}, u32[]{:S(2)}) collective-permute-start(bf16[64,512]{1,0:T(8,128)(2,1)} %select_reduce_fusion), channel_id=1, source_target_pairs={{0,64},{16,80},{32,96},{48,112},{64,0},{80,16},{96,32},{112,48},{1... | collective-permute-start | bytes 196616 | tf_op jit(solution)/shard_map/events/ppermute | solution.py:307
  184.5 3.4 %collective-permute-start.7 = (bf16[272,512]{1,0:T(8,128)(2,1)S(1)}, bf16[272,512]{1,0:T(8,128)(2,1)S(1)}, u32[]{:S(2)}, u32[]{:S(2)}) collective-permute-start(bf16[272,512]{1,0:T(8,128)(2,1)S(1)} %get-tuple-element.14.send_ref), channel_id=1, source_target_pairs={{0,1},{1,0},{2,3},{3,2},{4,5},{5,4},{6,7},{7,6},{8,9},{9,8},{10,11... | collective-permute-start | bytes 835592 | tf_op jit(solution)/shard_map/weight_gradient/ppermute | solution.py:371
  187.9 28.3 %copy-start.4 = (bf16[4,16,512]{2,1,0:T(8,128)(2,1)S(1)}, bf16[4,16,512]{2,1,0:T(8,128)(2,1)}, u32[]{:S(2)}) copy-start(bf16[4,16,512]{2,1,0:T(8,128)(2,1)} %copy-done.3) | copy-start | bytes 196612

commit v2 on v1

--- a/solution.py
+++ b/solution.py
@@ -49,61 +49,74 @@
     return upper * DEV_HIST + lax.axis_index("segment")
 
 
-def routing_kernel(block_rows, own_rows, table_ref, seg_ref, payload_ref, hot_ref, count_ref):
+def whole_part(a, d):
+    if d & (d - 1) == 0:
+        return a // d
+    return jnp.floor((a.astype(F32) + 0.5) * (1.0 / d)).astype(jnp.int32)
+
+
+def routing_kernel(block_rows, own_rows, table_ref, seeds_ref, hot_ref, count_ref):
     n_dp = table_ref.shape[0]
     hist = n_dp * DEV_HIST
     me = dp_place()
-    segment = lax.axis_index("segment")
-    table = table_ref[...].astype(F32).astype(BF)
-    spread = mm(table, (iota((128, hist), 0) == iota((128, hist), 1) % DEV_HIST).astype(BF))
+    facts = table_ref[:, SLOTS * 128 : SLOTS * 128 + 128]
+    spread = mm(facts, (iota((128, hist), 0) == iota((128, hist), 1) % DEV_HIST).astype(F32).astype(BF))
     own = iota((n_dp, hist), 1) // DEV_HIST == iota((n_dp, hist), 0)
     routes = jnp.sum(jnp.where(own, spread, 0.0), axis=0, keepdims=True)
+
+    routes_wide = jnp.broadcast_to(routes, (16, hist))
+    history, mine = iota((16, hist), 1), me * DEV_HIST + iota((16, hist), 0)
+    route = jnp.sum(jnp.where(history == mine, routes_wide, 0.0), axis=1, keepdims=True)
+    before = (routes_wide == route) & (history < mine)
+    slot = jnp.sum(before.astype(F32), axis=1, keepdims=True)
+    source = iota((16, n_dp), 1).astype(F32)
+    seeds = jnp.zeros((16, 128), F32)
+    for k in range(SLOTS):
+        pick = jnp.where((source == route) & (slot == float(k)), 1.0, 0.0).astype(BF)
+        seeds = seeds + mm(pick, table_ref[:, 128 * k : 128 * k + 128])
+    for q in range(LAYERS):
+        seeds_ref[q] = jnp.broadcast_to(seeds[q : q + 1], (16, 128)).astype(BF)
+
     hit = jnp.broadcast_to((routes == me.astype(F32)).astype(F32), (16, hist))
-    earlier = (iota((hist, hist), 0) < iota((hist, hist), 1)).astype(BF)
-    slot = mm(hit.astype(BF), earlier)
-    hot = jnp.where(slot == iota((16, hist), 0).astype(F32), hit, 0.0).astype(BF)
-    mine = (iota((hist, n_dp), 0) == iota((hist, n_dp), 1) * DEV_HIST + segment).astype(BF)
-    picks = mm(hot, mine).astype(BF)
-    cotangent = jnp.concatenate([seg_ref[q, 0:16, :] for q in range(LAYERS)], axis=1)
-    payload_ref[...] = mm(picks, cotangent, TN).astype(BF)
+    earlier = (iota((hist, hist), 0) < iota((hist, hist), 1)).astype(F32).astype(BF)
+    place_of = mm(hit.astype(BF), earlier)
+    hot = jnp.where(place_of == iota((16, hist), 0).astype(F32), hit, 0.0).astype(BF)
     total = hot_ref.shape[2]
     place, history = iota((hist, total), 1), iota((hist, total), 0)
-    within = place % block_rows - own_rows
-    first = ((place // block_rows) * 2 + within) * DEV_HIST
+    chip = whole_part(place, block_rows)
+    within = place - chip * block_rows - own_rows
+    first = (chip * 2 + within) * DEV_HIST
     valid = (within >= 0) & (within < 2)
     for h in range(DEV_HIST):
         move = jnp.where(valid & (history == first + h), 1.0, 0.0).astype(BF)
         hot_ref[h] = mm(hot, move).astype(BF)
+
     other = lax.rem(me + n_dp // 2, n_dp)
-    pair = jnp.concatenate([table_ref[pl.ds(me, 1), :], table_ref[pl.ds(other, 1), :]], axis=0)
-    lane = iota((2, 128), 1)
-    fits = (lane >= 4) & (lane < 8) & (pair // 128 == wanted_value())
-    length = jnp.sum(jnp.where(fits, (pair % 128).astype(F32), 0.0), axis=1, keepdims=True)
+    known = facts.astype(F32)
+    ahead = pltpu.roll(known, 124, 1)
+    row, lane = iota((n_dp, 128), 0), iota((n_dp, 128), 1)
+    fits = ((row == me) | (row == other)) & (lane >= 4) & (lane < 8)
+    fits = fits & (known == wanted_value().astype(F32))
+    length = jnp.sum(jnp.where(fits, ahead, 0.0), axis=1, keepdims=True)
     length = jnp.sum(length, axis=0, keepdims=True)
     count_ref[...] = jnp.broadcast_to(length, count_ref.shape).astype(jnp.int32)
 
 
 def layers_kernel(
-    plan_ref, events_ref, other_ref, count_ref, cot_ref, seg_ref,
-    w_in_ref, w_out_ref, near_a, near_b, swap_a, swap_b, far_a, far_b,
+    plan_ref, events_ref, other_ref, count_ref, cot_ref, gathered_ref,
     out_ref,
-    weights, proj_s, dsilu_s, normed_s, rstd_s, norm_o_s, rstd_o_s, bias_s, att_s, datt_s, sems,
+    weights, tables, proj_s, dsilu_s, normed_s, rstd_s, norm_o_s, rstd_o_s, bias_s, att_s, datt_s, sems, table_sem,
 ):
-    segment, core = lax.axis_index("segment"), lax.axis_index("core")
     half = WIDTH // 2
-    near = lax.rem(segment + 1 + 2 * core, LAYERS)
-    swap = lax.rem(segment + 3 + 2 * core, LAYERS)
-    far = lax.rem(segment + 2, LAYERS)
-    low = pl.ds(pl.multiple_of(core * half, half), half)
-    high = pl.ds(pl.multiple_of((1 - core) * half, half), half)
-    pltpu.make_async_copy(w_in_ref, weights.at[segment, :, pl.ds(0, 4 * WIDTH)], sems.at[segment]).start()
-    pltpu.make_async_copy(w_out_ref, weights.at[segment, :, pl.ds(4 * WIDTH, WIDTH)], sems.at[segment]).start()
-    pltpu.make_async_copy(near_a, weights.at[near, low], sems.at[near]).start()
-    pltpu.make_async_copy(near_b, weights.at[near, high], sems.at[near]).start()
-    pltpu.make_async_copy(swap_a, weights.at[swap, high], sems.at[swap]).start()
-    pltpu.make_async_copy(swap_b, weights.at[swap, low], sems.at[swap]).start()
-    pltpu.make_async_copy(far_a, weights.at[far, low], sems.at[far]).start()
-    pltpu.make_async_copy(far_b, weights.at[far, high], sems.at[far]).start()
+    for l in range(LAYERS):
+        pltpu.make_async_copy(
+            gathered_ref.at[l, 0, pl.ds(half, 16), pl.ds(0, 128)], tables.at[l], table_sem.at[l]
+        ).start()
+    for l in range(LAYERS):
+        for c in range(2):
+            pltpu.make_async_copy(
+                gathered_ref.at[l, c, pl.ds(0, half)], weights.at[l, pl.ds(c * half, half)], sems.at[l, c]
+            ).start()
 
     lane, row = iota((ROWS, 128), 1), iota((ROWS, 128), 0)
     left = (lane < HEAD_COLS).astype(F32)
@@ -113,7 +126,8 @@
     allowed = (column <= row) & (column < count)
 
     for l in range(LAYERS):
-        table = seg_ref[l, 16:32, :].astype(F32)
+        pltpu.make_async_copy(tables.at[l], tables.at[l], table_sem.at[l]).wait()
+        table = tables[l].astype(F32)
         table = table[0:4] + table[4:8] + table[8:12]
         for p in range(PAIRS):
             wide = jnp.broadcast_to(table[p : p + 1], (ROWS, 128))
@@ -144,7 +158,9 @@
         normed = centred * rstd
         normed_s[l] = normed
         rstd_s[l] = jnp.broadcast_to(rstd, (ROWS, 128))
-        pltpu.make_async_copy(weights.at[l], weights.at[l], sems.at[l]).wait()
+        for c in range(2):
+            piece = weights.at[l, pl.ds(c * half, half)]
+            pltpu.make_async_copy(piece, piece, sems.at[l, c]).wait()
         normed_b = normed.astype(BF)
         for kind in range(4):
             cols = pl.ds(kind * WIDTH, WIDTH)
@@ -178,7 +194,7 @@
     for q in range(LAYERS):
         quarter = jnp.broadcast_to(state[:, 128 * q : 128 * q + 128], (16, 128))
         out_ref[q, 192:208, :] = jnp.concatenate([quarter] * 4, axis=1).astype(BF)
-    seed = jnp.sum(cot_ref[...].astype(F32), axis=0, keepdims=True)
+    seed = jnp.concatenate([cot_ref[q].astype(F32)[0:1] for q in range(LAYERS)], axis=1)
     cot = jnp.where(last, jnp.broadcast_to(seed, (ROWS, WIDTH)), 0.0).astype(BF)
 
     for l in reversed(range(LAYERS)):
@@ -235,14 +251,16 @@
     total = (keep_ref[...] + got_ref[0:half, :].astype(F32)).astype(BF)
     rows = out_ref.shape[0]
     place, source = iota((rows, half), 0), iota((rows, half), 1)
-    within = place % block_rows
-    pick = (within < own_rows) & (source == (place // block_rows) * own_rows + within)
+    chip = whole_part(place, block_rows)
+    within = place - chip * block_rows
+    pick = (within < own_rows) & (source == chip * own_rows + within)
     laid = mm(pick.astype(F32).astype(BF), total)
     own = send_ref[half : half + 16, :].astype(F32)[0:1]
     other = got_ref[half : half + 16, :].astype(F32)[0:1]
     first = jnp.where(core == 0, own, other)
     second = jnp.where(core == 0, other, own)
-    at = iota((rows, WIDTH), 0) % block_rows
+    place = iota((rows, WIDTH), 0)
+    at = place - whole_part(place, block_rows) * block_rows
     laid = laid + jnp.where(at == own_rows, first, 0.0) + jnp.where(at == own_rows + 1, second, 0.0)
     out_ref[...] = laid.astype(BF)
 
@@ -251,7 +269,9 @@
     rows = got_ref.shape[0]
     out_rows = weight_ref.shape[0]
     lead = max(16, out_rows)
-    pick = (iota((lead, rows), 1) % block_rows == iota((lead, rows), 0)).astype(F32).astype(BF)
+    place = iota((lead, rows), 1)
+    within = place - whole_part(place, block_rows) * block_rows
+    pick = ((within == iota((lead, rows), 0)) & (within < out_rows)).astype(F32).astype(BF)
     got = got_ref[...]
     weight_ref[...] = mm(pick, got)[0:out_rows]
     served = jnp.zeros((16, 128), F32)
@@ -281,24 +301,22 @@
     chips = n_z * n_y
     core = lax.axis_index("core")
     own_rows = WIDTH // n_dp
-    block_rows = -(-(own_rows + 2) // 8) * 8
+    block_rows = own_rows + 2
     half = WIDTH // 2
 
     with jax.named_scope("section_weights"):
-        ring = [(s * 2, (s - 1) % LAYERS * 2) for s in range(LAYERS)]
-        ring += [(s * 2 + 1, (s + 1) % LAYERS * 2 + 1) for s in range(LAYERS)]
-        swap = [(0, 1), (1, 0)]
-        w_in, w_back = w_uvqk[0], w_out[0]
-        upper = jnp.concatenate([w_in[:half], w_back[:half]], axis=1)
-        lower = jnp.concatenate([w_in[half:], w_back[half:]], axis=1)
-        first = jnp.where(core == 0, upper, lower)
-        second = jnp.where(core == 0, lower, upper)
-        near_a = lax.ppermute(first, ("segment", "core"), ring)
-        near_b = lax.ppermute(second, ("segment", "core"), ring)
-        far_a = lax.ppermute(near_a, ("segment", "core"), ring)
-        swap_a = lax.ppermute(near_a, "core", swap)
-        swap_b = lax.ppermute(near_b, "core", swap)
-        far_b = lax.ppermute(far_a, "core", swap)
+        even, odd = rel_bias[0, 0::2], rel_bias[0, 1::2]
+        base = jnp.concatenate([even[:, 0:1], odd[:, ::-1], even[:, :0:-1]], axis=1)
+        high = lax.reduce_precision(base, 8, 7)
+        middle = lax.reduce_precision(base - high, 8, 7)
+        low = base - high - middle
+        table = jnp.concatenate([a.astype(BF) for a in (high, middle, low)])
+        table = jnp.pad(table, ((0, 4), (0, 5 * WIDTH - 128)))
+        w_in = lax.dynamic_slice_in_dim(w_uvqk[0], core * half, half, 0)
+        w_back = lax.dynamic_slice_in_dim(w_out[0], core * half, half, 0)
+        mine = jnp.concatenate([jnp.concatenate([w_in, w_back], axis=1), table])
+        gathered = lax.all_gather(mine, ("segment", "core"))
+        gathered = gathered.reshape(LAYERS, 2, half + 16, 5 * WIDTH)
 
     with jax.named_scope("events"):
         partner_value = DEV_HIST + 2 * lax.axis_index("segment") - wanted_value()
@@ -307,31 +325,19 @@
         other_events = lax.ppermute(outgoing, "z", [(i, (i + n_z // 2) % n_z) for i in range(n_z)])
 
     with jax.named_scope("routing"):
-        packed = balance_plan * 128 + lengths
-        facts = jnp.concatenate([routes[:, 0], packed, jnp.zeros((120,), jnp.int32)])
-        table = lax.all_gather(facts, DP)
-        table = table.reshape(n_dp, 128)
-        even, odd = rel_bias[0, 0::2], rel_bias[0, 1::2]
-        base = jnp.concatenate([even[:, 0:1], odd[:, ::-1], even[:, :0:-1]], axis=1)
-        high = lax.reduce_precision(base, 8, 7)
-        middle = lax.reduce_precision(base - high, 8, 7)
-        low = base - high - middle
-        cot = jnp.concatenate(
-            [state_cotangent[0], jnp.zeros((8, 128), BF)]
-            + [a.astype(BF) for a in (high, middle, low)]
-            + [jnp.zeros((4, 128), BF)]
-        )
-        seg_facts = lax.all_gather(cot, "segment")
-        payload, hot, count = call(
+        facts = jnp.concatenate([routes[:, 0], balance_plan, lengths, jnp.zeros((116,), jnp.int32)])
+        facts = jnp.concatenate([state_cotangent[0].reshape(SLOTS * 128), facts.astype(BF)])
+        facts = jnp.broadcast_to(facts[None], (n_dp, (SLOTS + 1) * 128))
+        facts = lax.all_to_all(facts, DP, 0, 0, tiled=True)
+        seeds, hot, count = call(
             functools.partial(routing_kernel, block_rows, own_rows),
             (
-                shape((n_dp, WIDTH), BF),
+                shape((LAYERS, 16, 128), BF),
                 shape((DEV_HIST, 16, chips * block_rows), BF),
                 shape((ROWS, 128), jnp.int32),
             ),
-        )(table, seg_facts)
-        cot_rows = lax.all_to_all(payload.reshape(n_dp, 1, WIDTH), DP, 0, 0, tiled=True)
-        cot_rows = cot_rows.reshape(n_dp, WIDTH)
+        )(facts)
+        seeds = lax.all_to_all(seeds, "segment", 0, 0, tiled=True)
 
     any_spec, vmem = pl.BlockSpec(memory_space=pl.ANY), pl.BlockSpec(memory_space=pltpu.VMEM)
     with jax.named_scope("layers"):
@@ -340,6 +346,7 @@
             shape((LAYERS, MSG, WIDTH), BF),
             scratch=[
                 pltpu.VMEM((LAYERS, WIDTH, 5 * WIDTH), BF),
+                pltpu.VMEM((LAYERS, 16, 128), BF),
                 pltpu.VMEM((LAYERS, ROWS, 4 * WIDTH), BF),
                 pltpu.VMEM((LAYERS, ROWS, 4 * WIDTH), F32),
                 pltpu.VMEM((LAYERS, ROWS, WIDTH), F32),
@@ -349,16 +356,15 @@
                 pltpu.VMEM((LAYERS, PAIRS, ROWS, 128), F32),
                 pltpu.VMEM((LAYERS, PAIRS, ROWS, 128), BF),
                 pltpu.VMEM((LAYERS, PAIRS, ROWS, 128), F32),
+                pltpu.SemaphoreType.DMA((LAYERS, 2)),
                 pltpu.SemaphoreType.DMA((LAYERS,)),
             ],
-            in_specs=[pl.BlockSpec(memory_space=pltpu.SMEM)] + [vmem] * 5 + [any_spec] * 8,
-        )(
-            balance_plan, events, other_events, count, cot_rows, seg_facts,
-            w_in, w_back, near_a, near_b, swap_a, swap_b, far_a, far_b,
-        )
+            in_specs=[pl.BlockSpec(memory_space=pltpu.SMEM)] + [vmem] * 4 + [any_spec],
+        )(balance_plan, events, other_events, count, seeds, gathered)
 
     with jax.named_scope("section_exchange"):
         arrived = lax.all_to_all(message, "segment", 0, 0, tiled=True)
+    swap = [(0, 1), (1, 0)]
     with jax.named_scope("weight_gradient"):
         grads, keep, send = call(
             functools.partial(gradient_kernel, own_rows),

time: 218 us -> 164 us (0.75)
  blocking collectives: 108 us -> 49.2 us
  between operations: 0.93 us -> 14.3 us
  starting transfers between devices: 39.6 us -> 31.2 us
  local copies, waits for them, and re-layouts: 9.61 us -> 5.72 us
    all_gather x2 -> x0, blocking collectives: 61.7 us -> none  [the longest x1 49.2 us: body(): table = lax.all_gather(facts, DP)]
    ppermute x6 -> x0, waiting for transfers between devices: 31 us -> none  [the longest x1 12.4 us: body(): near_a = lax.ppermute(first, ('segment', 'core'), ring)]
    all_gather x0 -> x1, waiting for transfers between devices: none -> 22 us  [body(): gathered = lax.all_gather(mine, ('segment', 'core'))]
    ppermute x6 -> x0, starting transfers between devices: 18.9 us -> none  [the longest x1 5.59 us: body(): far_a = lax.ppermute(near_a, ('segment', 'core'), ring)]
    all_to_all x1 -> x2, waiting for transfers between devices: 3.08 us -> 13.8 us  [the longest x1 8.31 us: body(): facts = lax.all_to_all(facts, DP, 0, 0, tiled=True)]
    all_to_all x1 -> x2, starting transfers between devices: 11.1 us -> 21.7 us  [the longest x1 17.4 us: body(): facts = lax.all_to_all(facts, DP, 0, 0, tiled=True)]
    all_to_all x1, blocking collectives: 27.9 us -> 32.7 us  [body(): lax.all_to_all(blocks.reshape(chips, block_rows, WIDTH), ('z', 'y'), 0, 0...]
    unnamed x23 -> x17, local copies, waits for them, and re-layouts: 5.86 us -> 2.65 us
  transfers between devices with their start and end apart: 9 -> 5, of which waited for: 5 -> 4; matrix products, arithmetic and copies ran while one was open for 4% -> 3% of each run, Pallas kernels for 0% -> 1%
where the time goes in v2:
time: 164 us; the launch traced here: 163 us
  blocking collectives  49.2 us (30%)
  waiting for transfers between devices  37.3 us (23%)
  starting transfers between devices  31.2 us (19%)
  Pallas kernels  21.8 us (13%)
  between operations  14.3 us (9%)
  local copies, waits for them, and re-layouts  5.72 us (3%)
  other arithmetic  3.9 us (2%)
    all_to_all x1, blocking collectives, body(): lax.all_to_all(blocks.reshape(chips, block_rows, WIDTH), ('z', 'y'), 0, 0...  32.7 us
    all_gather x1, waiting for transfers between devices, body(): gathered = lax.all_gather(mine, ('segment', 'core'))  22 us
    pallas_call x1, Pallas kernels, body(): call(layers_kernel, shape((LAYERS, MSG, WIDTH), BF), scratch=[pltpu.VMEM(...  18.3 us
    all_to_all x1, starting transfers between devices, body(): facts = lax.all_to_all(facts, DP, 0, 0, tiled=True)  17.4 us
    all_to_all x1, blocking collectives, body(): arrived = lax.all_to_all(message, 'segment', 0, 0, tiled=True)  16.5 us
    all_to_all x1, waiting for transfers between devices, body(): facts = lax.all_to_all(facts, DP, 0, 0, tiled=True)  8.31 us
    ppermute x1, starting transfers between devices, body(): lax.ppermute(outgoing, 'z', [(i, (i + n_z // 2) % n_z) for i in range(n_z)])  7.61 us
    all_to_all x1, waiting for transfers between devices, body(): seeds = lax.all_to_all(seeds, 'segment', 0, 0, tiled=True)  5.51 us
  transfers between devices with their start and end apart: 5, of which 4 were waited for; matrix products, arithmetic and copies ran while one was open for 3% of the time, Pallas kernels for 1%

profile of v2, /device:TPU:8, one launch (start us, length us, event | category | flops | bytes accessed | tf_op | source)
XLA Modules:
  0.0 163.4 jit_solution(13965572405204241047)
XLA Ops:
  7.2 0.8 slice.12
  8.1 0.7 slice.14
  8.9 1.0 copy-done.3
  10.3 1.2 pad_maximum_fusion
  11.7 0.3 broadcast_in_dim.34
  12.0 0.5 broadcast.24
  12.5 2.5 %reduce = bf16[128,1152]{1,0:T(8,128)(2,1)S(1)} reduce(bf16[128,1,1152]{2,1,0:T(2,128)(2,1)S(1)} %broadcast_in_dim.34, bf16[]{:T(256)} %broadcast.24), dimensions={1}, to_apply=%broadcast_in_dim.34.reduce_sub_computation | reduce | bytes 589826 | tf_op jit(solution)/shard_map/routing/broadcast_in_dim | solution.py:330
  15.0 1.1 reshape.29
  16.1 17.4 %all-to-all-start = ((bf16[128,2,576]{2,1,0:T(2,128)(2,1)}), bf16[128,2,576]{2,1,0:T(2,128)(2,1)S(1)}, u32[]{:S(2)}, u32[]{:S(2)}) async-start(bf16[128,2,576]{2,1,0:T(2,128)(2,1)} %reshape.29), calls=%async_computation | async-start | bytes 655360 | tf_op jit(solution)/shard_map/routing/all_to_all | solution.py:331
  33.6 7.6 %collective-permute-start = (bf16[64,512]{1,0:T(8,128)(2,1)S(1)}, bf16[64,512]{1,0:T(8,128)(2,1)S(1)}, u32[]{:S(2)}, u32[]{:S(2)}) collective-permute-start(bf16[64,512]{1,0:T(8,128)(2,1)S(1)} %select_reduce_fusion), channel_id=1, source_target_pairs={{0,64},{16,80},{32,96},{48,112},{64,0},{80,16},{96,32},{112,48},{1... | collective-permute-start | bytes 196616 | tf_op jit(solution)/shard_map/events/ppermute | solution.py:325
  41.2 8.3 %all-to-all-done = bf16[128,2,576]{2,1,0:T(2,128)(2,1)S(1)} async-done(((bf16[128,2,576]{2,1,0:T(2,128)(2,1)}), bf16[128,2,576]{2,1,0:T(2,128)(2,1)S(1)}, u32[]{:S(2)}, u32[]{:S(2)}) %all-to-all-start) | async-done | bytes 294944 | tf_op jit(solution)/shard_map/routing/all_to_all | solution.py:331
  49.5 0.5 reshape.30
  50.1 1.2 routing.1
  51.2 4.3 %all-to-all-start.1 = ((bf16[4,16,128]{2,1,0:T(8,128)(2,1)}), bf16[4,16,128]{2,1,0:T(8,128)(2,1)S(1)}, u32[]{:S(2)}, u32[]{:S(2)}) async-start(bf16[4,16,128]{2,1,0:T(8,128)(2,1)} %get-tuple-element.12), calls=%async_computation.1 | async-start | bytes 32768 | tf_op jit(solution)/shard_map/routing/all_to_all | solution.py:340
  55.5 5.5 %all-to-all-done.1.cot_ref = bf16[4,16,128]{2,1,0:T(8,128)(2,1)S(1)} async-done(((bf16[4,16,128]{2,1,0:T(8,128)(2,1)}), bf16[4,16,128]{2,1,0:T(8,128)(2,1)S(1)}, u32[]{:S(2)}, u32[]{:S(2)}) %all-to-all-start.1) | async-done | bytes 16416 | tf_op jit(solution)/shard_map/routing/all_to_all | solution.py:340
  61.0 22.0 %all-gather.3.cloned.1.call-done = bf16[2176,2560]{1,0:T(8,128)(2,1)} async-done(((bf16[272,2560]{1,0:T(8,128)(2,1)}), bf16[2176,2560]{1,0:T(8,128)(2,1)}) %all-gather.3.cloned.1.call-update) | async-done | bytes 11141136 | tf_op jit(solution)/shard_map/section_weights/all_gather | solution.py:318
  83.0 18.3 %layers.1 = bf16[4,208,512]{2,1,0:T(8,128)(2,1)S(1)} custom-call(s32[4]{0:T(128)S(1)} %copy-done.2, bf16[4,64,512]{2,1,0:T(8,128)(2,1)S(1)} %copy-done.1, bf16[64,512]{1,0:T(8,128)(2,1)S(1)} %collective-permute-done.other_ref, s32[64,128]{1,0:T(8,128)S(1)} %get-tuple-element.11.count_ref, bf16[4,16,128]{2,1,0:T(8,128)(2,1)S(1)} %all-to-all-done.1.cot_ref, ...), custom_call_target="tpu_custom_call" | custom-call | tf_op jit(solution)/shard_map/layers/pallas_call | solution.py:344
  101.3 16.5 %all_to_all.23.got_ref = bf16[4,208,512]{2,1,0:T(8,128)(2,1)S(1)} all-to-all(bf16[4,208,512]{2,1,0:T(8,128)(2,1)S(1)} %layers.1), channel_id=1, replica_groups=mesh['segment'=4,'z'=8,'y'=8,'core'=2] {'segment'}, dimensions={0} | all-to-all | bytes 1703936 | tf_op jit(solution)/shard_map/section_exchange/all_to_all | solution.py:366
  117.8 1.3 weight_gradient.3
  119.0 1.9 %collective-permute-start.1 = (bf16[272,512]{1,0:T(8,128)(2,1)S(1)}, bf16[272,512]{1,0:T(8,128)(2,1)S(1)}, u32[]{:S(2)}, u32[]{:S(2)}) collective-permute-start(bf16[272,512]{1,0:T(8,128)(2,1)S(1)} %get-tuple-element.14.send_ref), channel_id=1, source_target_pairs={{0,1},{1,0},{2,3},{3,2},{4,5},{5,4},{6,7},{7,6},{8,9},{9,8},{10,11... | collective-permute-start | bytes 835592 | tf_op jit(solution)/shard_map/weight_gradient/ppermute | solution.py:377
  121.0 1.5 collective-permute-done.1.got_ref
  122.5 0.3 weight_gradient.4
  123.0 32.7 %all_to_all.24 = bf16[64,6,512]{2,1,0:T(8,128)(2,1)S(1)} all-to-all(bf16[64,6,512]{2,1,0:T(8,128)(2,1)S(1)} %reshape.25), channel_id=1, replica_groups=mesh['segment'=4,'z'=8,'y'=8,'core'=2] {'z','y'}, dimensions={0} | all-to-all | bytes 786432 | tf_op jit(solution)/shard_map/weight_gradient/all_to_all | solution.py:382
  155.8 0.8 weight_gradient.5
  (34 shorter events, 1.1 us)
Async XLA Ops:
  7.2 1.6 copy-start
  7.2 75.8 %all-gather.3.cloned.1.call-start = ((), (), s32[]{:S(2)}) async-start(), calls=%async_computation.4 | async-start | bytes 12533760 | tf_op jit(solution)/shard_map/section_weights/all_gather | solution.py:318
  8.8 1.0 copy-start.3
  10.2 1.3 copy-start.2
  10.2 1.3 copy-start.5
  10.2 1.3 copy-start.6
  10.2 1.3 copy-start.4
  11.5 22.0 %copy-start.1 = (bf16[4,64,512]{2,1,0:T(8,128)(2,1)S(1)}, bf16[4,64,512]{2,1,0:T(8,128)(2,1)}, u32[]{:S(2)}) copy-start(bf16[4,64,512]{2,1,0:T(8,128)(2,1)} %events_ref.1) | copy-start | bytes 786436
  16.1 33.4 %all-to-all-start = ((bf16[128,2,576]{2,1,0:T(2,128)(2,1)}), bf16[128,2,576]{2,1,0:T(2,128)(2,1)S(1)}, u32[]{:S(2)}, u32[]{:S(2)}) async-start(bf16[128,2,576]{2,1,0:T(2,128)(2,1)} %reshape.29), calls=%async_computation | async-start | bytes 655360 | tf_op jit(solution)/shard_map/routing/all_to_all | solution.py:331
  33.6 22.0 %collective-permute-start = (bf16[64,512]{1,0:T(8,128)(2,1)S(1)}, bf16[64,512]{1,0:T(8,128)(2,1)S(1)}, u32[]{:S(2)}, u32[]{:S(2)}) collective-permute-start(bf16[64,512]{1,0:T(8,128)(2,1)S(1)} %select_reduce_fusion), channel_id=1, source_target_pairs={{0,64},{16,80},{32,96},{48,112},{64,0},{80,16},{96,32},{112,48},{1... | collective-permute-start | bytes 196616 | tf_op jit(solution)/shard_map/events/ppermute | solution.py:325
  51.2 9.8 %all-to-all-start.1 = ((bf16[4,16,128]{2,1,0:T(8,128)(2,1)}), bf16[4,16,128]{2,1,0:T(8,128)(2,1)S(1)}, u32[]{:S(2)}, u32[]{:S(2)}) async-start(bf16[4,16,128]{2,1,0:T(8,128)(2,1)} %get-tuple-element.12), calls=%async_computation.1 | async-start | bytes 32768 | tf_op jit(solution)/shard_map/routing/all_to_all | solution.py:340
  119.0 3.4 %collective-permute-start.1 = (bf16[272,512]{1,0:T(8,128)(2,1)S(1)}, bf16[272,512]{1,0:T(8,128)(2,1)S(1)}, u32[]{:S(2)}, u32[]{:S(2)}) collective-permute-start(bf16[272,512]{1,0:T(8,128)(2,1)S(1)} %get-tuple-element.14.send_ref), channel_id=1, source_target_pairs={{0,1},{1,0},{2,3},{3,2},{4,5},{5,4},{6,7},{7,6},{8,9},{9,8},{10,11... | collective-permute-start | bytes 835592 | tf_op jit(solution)/shard_map/weight_gradient/ppermute | solution.py:377
Sparse Core Ops, SparseCore 0:
  11.6 71.3 all-gather.2

commit v3 on v2

--- a/solution.py
+++ b/solution.py
@@ -49,6 +49,59 @@
     return upper * DEV_HIST + lax.axis_index("segment")
 
 
+def packing_start(
+    plan_ref, routes_ref, lengths_ref, w_in_ref, w_out_ref, events_ref, bias_ref, cot_ref,
+    first_ref, second_ref, outgoing_ref, facts_ref,
+    table, sems,
+):
+    core = lax.axis_index("core")
+    half = WIDTH // 2
+    copies = []
+    for side, dest in ((core, first_ref), (1 - core, second_ref)):
+        rows = pl.ds(pl.multiple_of(side * half, half), half)
+        copies.append((w_in_ref.at[0, rows], dest.at[pl.ds(0, half), pl.ds(0, 4 * WIDTH)]))
+        copies.append((w_out_ref.at[0, rows], dest.at[pl.ds(0, half), pl.ds(4 * WIDTH, WIDTH)]))
+    partner_value = DEV_HIST + 2 * lax.axis_index("segment") - wanted_value()
+    chosen = jnp.int32(0)
+    for h in range(DEV_HIST):
+        chosen = chosen + jnp.where(plan_ref[h] == partner_value, h, 0)
+    copies.append((events_ref.at[chosen], outgoing_ref))
+    copies = [pltpu.make_async_copy(*c, sems.at[n]) for n, c in enumerate(copies)]
+    for c in copies:
+        c.start()
+
+    bias = bias_ref[0]
+    high = bias.astype(BF).astype(F32)
+    middle = (bias - high).astype(BF).astype(F32)
+    low = bias - high - middle
+    pieces = jnp.concatenate([high, middle, low, jnp.zeros((8, ROWS), F32)]).astype(BF)
+    row, head = iota((16, 32), 0), iota((16, 32), 1)
+    even = (row // 4) * 8 + 2 * (row % 4)
+    used = row < 12
+    pick_even = (used & (head == even)).astype(F32).astype(BF)
+    pick_odd = (used & (head == even + 1)).astype(F32).astype(BF)
+    distance, place = iota((ROWS, 128), 0), iota((ROWS, 128), 1)
+    to_even = (place == (128 - distance) % 128).astype(F32).astype(BF)
+    to_odd = (place == ROWS - distance).astype(F32).astype(BF)
+    base = mm(mm(pick_even, pieces).astype(BF), to_even) + mm(mm(pick_odd, pieces).astype(BF), to_odd)
+    table[...] = base.astype(BF)
+    copy = pltpu.make_async_copy(table, first_ref.at[pl.ds(half, 16), pl.ds(0, 128)], sems.at[len(copies)])
+    copy.start()
+
+    lane = iota((1, 128), 1)
+    facts = jnp.zeros((1, 128), F32)
+    for j, ref in enumerate((routes_ref, plan_ref, lengths_ref)):
+        for h in range(DEV_HIST):
+            facts = jnp.where(lane == 4 * j + h, ref[h].astype(F32), facts)
+    cot = cot_ref[0].astype(F32)
+    blocks = [cot[k : k + 1] for k in range(SLOTS)] + [facts, jnp.zeros((1, 128), F32)]
+    lines = [jnp.concatenate(blocks[k : k + 5], axis=1) for k in (0, 5)]
+    facts_ref[...] = jnp.broadcast_to(jnp.concatenate(lines).astype(BF)[None], facts_ref.shape)
+    for c in copies:
+        c.wait()
+    copy.wait()
+
+
 def whole_part(a, d):
     if d & (d - 1) == 0:
         return a // d
@@ -103,20 +156,26 @@
 
 
 def layers_kernel(
-    plan_ref, events_ref, other_ref, count_ref, cot_ref, gathered_ref,
+    plan_ref, events_ref, other_ref, count_ref, cot_ref,
+    first, second, near_a, near_b, swap_a, swap_b, far_a, far_b,
     out_ref,
     weights, tables, proj_s, dsilu_s, normed_s, rstd_s, norm_o_s, rstd_o_s, bias_s, att_s, datt_s, sems, table_sem,
 ):
     half = WIDTH // 2
-    for l in range(LAYERS):
+    segment, core = lax.axis_index("segment"), lax.axis_index("core")
+    near = lax.rem(segment + 1 + 2 * core, LAYERS)
+    swap = lax.rem(segment + 3 + 2 * core, LAYERS)
+    far = lax.rem(segment + 2, LAYERS)
+    for piece, l in ((first, segment), (near_a, near), (swap_a, swap), (far_a, far)):
         pltpu.make_async_copy(
-            gathered_ref.at[l, 0, pl.ds(half, 16), pl.ds(0, 128)], tables.at[l], table_sem.at[l]
+            piece.at[pl.ds(half, 16), pl.ds(0, 128)], tables.at[l], table_sem.at[l]
         ).start()
-    for l in range(LAYERS):
-        for c in range(2):
-            pltpu.make_async_copy(
-                gathered_ref.at[l, c, pl.ds(0, half)], weights.at[l, pl.ds(c * half, half)], sems.at[l, c]
-            ).start()
+    for piece, l, side in (
+        (first, segment, core), (second, segment, 1 - core), (near_a, near, core), (near_b, near, 1 - core),
+        (swap_a, swap, 1 - core), (swap_b, swap, core), (far_a, far, core), (far_b, far, 1 - core),
+    ):
+        rows = pl.ds(pl.multiple_of(side * half, half), half)
+        pltpu.make_async_copy(piece.at[pl.ds(0, half)], weights.at[l, rows], sems.at[l, side]).start()
 
     lane, row = iota((ROWS, 128), 1), iota((ROWS, 128), 0)
     left = (lane < HEAD_COLS).astype(F32)
@@ -284,8 +343,9 @@
     return jax.ShapeDtypeStruct(dims, dtype)
 
 
-def call(kernel, outs, scratch=(), in_specs=None, limit=48):
+def call(kernel, outs, scratch=(), in_specs=None, out_specs=None, limit=48):
     specs = {} if in_specs is None else {"in_specs": in_specs}
+    specs |= {} if out_specs is None else {"out_specs": out_specs}
     return pl.pallas_call(
         kernel,
         out_shape=outs,
@@ -299,36 +359,47 @@
     n_z, n_y, n_core = (lax.axis_size(a) for a in DP)
     n_dp = n_z * n_y * n_core
     chips = n_z * n_y
-    core = lax.axis_index("core")
     own_rows = WIDTH // n_dp
     block_rows = own_rows + 2
     half = WIDTH // 2
 
+    any_spec, vmem = pl.BlockSpec(memory_space=pl.ANY), pl.BlockSpec(memory_space=pltpu.VMEM)
+    smem = pl.BlockSpec(memory_space=pltpu.SMEM)
+    with jax.named_scope("packing"):
+        first, second, outgoing, facts = call(
+            packing_start,
+            (
+                shape((half + 16, 5 * WIDTH), BF),
+                shape((half, 5 * WIDTH), BF),
+                shape((ROWS, WIDTH), BF),
+                shape((n_dp, 2, (SLOTS + 2) * 64), BF),
+            ),
+            scratch=[pltpu.VMEM((16, 128), BF), pltpu.SemaphoreType.DMA((6,))],
+            in_specs=[smem] * 3 + [any_spec] * 3 + [vmem] * 2,
+            out_specs=(any_spec, any_spec, any_spec, vmem),
+        )(balance_plan, routes.reshape(DEV_HIST), lengths, w_uvqk, w_out, events, rel_bias, state_cotangent)
+
     with jax.named_scope("section_weights"):
-        even, odd = rel_bias[0, 0::2], rel_bias[0, 1::2]
-        base = jnp.concatenate([even[:, 0:1], odd[:, ::-1], even[:, :0:-1]], axis=1)
-        high = lax.reduce_precision(base, 8, 7)
-        middle = lax.reduce_precision(base - high, 8, 7)
-        low = base - high - middle
-        table = jnp.concatenate([a.astype(BF) for a in (high, middle, low)])
-        table = jnp.pad(table, ((0, 4), (0, 5 * WIDTH - 128)))
-        w_in = lax.dynamic_slice_in_dim(w_uvqk[0], core * half, half, 0)
-        w_back = lax.dynamic_slice_in_dim(w_out[0], core * half, half, 0)
-        mine = jnp.concatenate([jnp.concatenate([w_in, w_back], axis=1), table])
-        gathered = lax.all_gather(mine, ("segment", "core"))
-        gathered = gathered.reshape(LAYERS, 2, half + 16, 5 * WIDTH)
+        ring = [(s * 2, (s - 1) % LAYERS * 2) for s in range(LAYERS)]
+        ring += [(s * 2 + 1, (s + 1) % LAYERS * 2 + 1) for s in range(LAYERS)]
+        swap = [(0, 1), (1, 0)]
+        near_a = lax.ppermute(first, ("segment", "core"), ring)
+        near_b = lax.ppermute(second, ("segment", "core"), ring)
 
     with jax.named_scope("events"):
-        partner_value = DEV_HIST + 2 * lax.axis_index("segment") - wanted_value()
-        chosen = (balance_plan == partner_value)[:, None, None]
-        outgoing = jnp.sum(jnp.where(chosen, events, jnp.zeros((), BF)), axis=0, dtype=BF)
         other_events = lax.ppermute(outgoing, "z", [(i, (i + n_z // 2) % n_z) for i in range(n_z)])
 
     with jax.named_scope("routing"):
-        facts = jnp.concatenate([routes[:, 0], balance_plan, lengths, jnp.zeros((116,), jnp.int32)])
-        facts = jnp.concatenate([state_cotangent[0].reshape(SLOTS * 128), facts.astype(BF)])
-        facts = jnp.broadcast_to(facts[None], (n_dp, (SLOTS + 1) * 128))
         facts = lax.all_to_all(facts, DP, 0, 0, tiled=True)
+        near_a, near_b, facts = lax.optimization_barrier((near_a, near_b, facts))
+        facts = facts.reshape(n_dp, (SLOTS + 2) * 128)
+
+    with jax.named_scope("section_weights"):
+        far_a = lax.ppermute(near_a, ("segment", "core"), ring)
+        swap_a = lax.ppermute(near_a, "core", swap)
+        swap_b = lax.ppermute(near_b, "core", swap)
+
+    with jax.named_scope("routing"):
         seeds, hot, count = call(
             functools.partial(routing_kernel, block_rows, own_rows),
             (
@@ -338,8 +409,12 @@
             ),
         )(facts)
         seeds = lax.all_to_all(seeds, "segment", 0, 0, tiled=True)
-
-    any_spec, vmem = pl.BlockSpec(memory_space=pl.ANY), pl.BlockSpec(memory_space=pltpu.VMEM)
+        far_a, swap_a, swap_b, seeds, other_events = lax.optimization_barrier(
+            (far_a, swap_a, swap_b, seeds, other_events)
+        )
+    with jax.named_scope("section_weights"):
+        far_b = lax.ppermute(far_a, "core", swap)
+
     with jax.named_scope("layers"):
         message = call(
             layers_kernel,
@@ -359,12 +434,14 @@
                 pltpu.SemaphoreType.DMA((LAYERS, 2)),
                 pltpu.SemaphoreType.DMA((LAYERS,)),
             ],
-            in_specs=[pl.BlockSpec(memory_space=pltpu.SMEM)] + [vmem] * 4 + [any_spec],
-        )(balance_plan, events, other_events, count, seeds, gathered)
+            in_specs=[smem] + [vmem] * 4 + [any_spec] * 8,
+        )(
+            balance_plan, events, other_events, count, seeds,
+            first, second, near_a, near_b, swap_a, swap_b, far_a, far_b,
+        )
 
     with jax.named_scope("section_exchange"):
         arrived = lax.all_to_all(message, "segment", 0, 0, tiled=True)
-    swap = [(0, 1), (1, 0)]
     with jax.named_scope("weight_gradient"):
         grads, keep, send = call(
             functools.partial(gradient_kernel, own_rows),

time: 164 us -> 152 us (0.927)
  blocking collectives: 49.2 us -> 82.5 us
  waiting for transfers between devices: 37.3 us -> 10.2 us
  between operations: 14.3 us -> 0.81 us
  other arithmetic: 3.9 us -> 0 us
  local copies, waits for them, and re-layouts: 5.72 us -> 8.35 us
  starting transfers between devices: 31.2 us -> 29.1 us
    all_to_all x0 -> x1, blocking collectives: none -> 33.2 us  [body(): facts = lax.all_to_all(facts, DP, 0, 0, tiled=True)]
    all_gather x1 -> x0, waiting for transfers between devices: 22 us -> none  [body(): gathered = lax.all_gather(mine, ('segment', 'core'))]
    all_to_all x1 -> x0, starting transfers between devices: 17.4 us -> none  [body(): facts = lax.all_to_all(facts, DP, 0, 0, tiled=True)]
    ppermute x0 -> x6, starting transfers between devices: none -> 16.6 us  [the longest x1 4.8 us: body(): near_a = lax.ppermute(first, ('segment', 'core'), ring)]
    all_to_all x1 -> x0, waiting for transfers between devices: 8.31 us -> none  [body(): facts = lax.all_to_all(facts, DP, 0, 0, tiled=True)]
    unnamed x17 -> x25, local copies, waits for them, and re-layouts: 2.65 us -> 8.08 us
    ppermute x0 -> x6, waiting for transfers between devices: none -> 3.34 us  [the longest x1 3.33 us: body(): far_b = lax.ppermute(far_a, 'core', swap)]
    broadcast_in_dim x1 -> x0, other arithmetic: 2.47 us -> none  [body(): facts = jnp.broadcast_to(facts[None], (n_dp, (SLOTS + 1) * 128))]
  transfers between devices with their start and end apart: 5 -> 9, of which waited for: 4 -> 3; matrix products, arithmetic and copies ran while one was open for 3% -> 0% of each run, Pallas kernels for 1% -> 1%
where the time goes in v3:
time: 152 us
  blocking collectives  82.5 us (54%)
  starting transfers between devices  29.1 us (19%)
  Pallas kernels  20.8 us (14%)
  waiting for transfers between devices  10.2 us (7%)
  local copies, waits for them, and re-layouts  8.35 us (5%)
    all_to_all x1, blocking collectives, body(): facts = lax.all_to_all(facts, DP, 0, 0, tiled=True)  33.2 us
    all_to_all x1, blocking collectives, body(): lax.all_to_all(blocks.reshape(chips, block_rows, WIDTH), ('z', 'y'), 0, 0...  31.5 us
    all_to_all x1, blocking collectives, body(): arrived = lax.all_to_all(message, 'segment', 0, 0, tiled=True)  17.8 us
    pallas_call x1, Pallas kernels, body(): call(layers_kernel, shape((LAYERS, MSG, WIDTH), BF), scratch=[pltpu.VMEM(...  16 us
    unnamed x25, local copies, waits for them, and re-layouts  8.08 us
    ppermute x1, starting transfers between devices, body(): lax.ppermute(outgoing, 'z', [(i, (i + n_z // 2) % n_z) for i in range(n_z)])  7.36 us
    all_to_all x1, waiting for transfers between devices, body(): seeds = lax.all_to_all(seeds, 'segment', 0, 0, tiled=True)  5.32 us
    ppermute x1, starting transfers between devices, body(): near_a = lax.ppermute(first, ('segment', 'core'), ring)  4.8 us
  transfers between devices with their start and end apart: 9, of which 3 were waited for; matrix products, arithmetic and copies ran while one was open for 0% of the time, Pallas kernels for 1%

profile of v3, /device:TPU:8, one launch (start us, length us, event | category | flops | bytes accessed | tf_op | source)
XLA Modules:
  0.0 151.7 jit_solution(11136248255136185132)
XLA Ops:
  0.6 1.6 %copy-done = bf16[1,512,2048]{2,1,0:T(8,128)(2,1)S(1)} copy-done((bf16[1,512,2048]{2,1,0:T(8,128)(2,1)S(1)}, bf16[1,512,2048]{2,1,0:T(8,128)(2,1)}, u32[]{:S(2)}) %copy-start) | copy-done | bytes 2097176
  2.2 0.9 copy-done.2
  3.2 1.0 copy-done.4
  7.6 1.2 packing.1
  8.8 4.8 %collective-permute-start = (bf16[272,2560]{1,0:T(8,128)(2,1)S(1)}, bf16[272,2560]{1,0:T(8,128)(2,1)}, u32[]{:S(2)}, u32[]{:S(2)}) collective-permute-start(bf16[272,2560]{1,0:T(8,128)(2,1)S(1)} %get-tuple-element.23.first), channel_id=1, source_target_pairs={{0,384},{128,0},{256,128},{384,256},{1,129},{129,257},{257,385},{3... | collective-permute-start | bytes 4177928 | tf_op jit(solution)/shard_map/section_weights/ppermute | solution.py:386
  13.6 2.7 %collective-permute-start.1 = (bf16[256,2560]{1,0:T(8,128)(2,1)S(1)}, bf16[256,2560]{1,0:T(8,128)(2,1)}, u32[]{:S(2)}, u32[]{:S(2)}) collective-permute-start(bf16[256,2560]{1,0:T(8,128)(2,1)S(1)} %get-tuple-element.24.second), channel_id=1, source_target_pairs={{0,384},{128,0},{256,128},{384,256},{1,129},{129,257},{257,385},{3... | collective-permute-start | bytes 3932168 | tf_op jit(solution)/shard_map/section_weights/ppermute | solution.py:387
  16.4 33.2 %all_to_all.20 = bf16[128,2,640]{2,1,0:T(2,128)(2,1)S(1)} all-to-all(bf16[128,2,640]{2,1,0:T(2,128)(2,1)S(1)} %get-tuple-element.25), channel_id=1, replica_groups=mesh['segment'=4,'z'=8,'y'=8,'core'=2] {'z','y','core'}, dimensions={0} | all-to-all | bytes 655360 | tf_op jit(solution)/shard_map/routing/all_to_all | solution.py:393
  49.6 1.9 %collective-permute-start.3 = (bf16[272,2560]{1,0:T(8,128)(2,1)}, bf16[272,2560]{1,0:T(8,128)(2,1)}, u32[]{:S(2)}, u32[]{:S(2)}) collective-permute-start(bf16[272,2560]{1,0:T(8,128)(2,1)} %collective-permute-done.near_a), channel_id=1, source_target_pairs={{0,1},{1,0},{2,3},{3,2},{4,5},{5,4},{6,7},{7,6},{8,9},{9,8},{10,11... | collective-permute-start | bytes 4177928 | tf_op jit(solution)/shard_map/section_weights/ppermute | solution.py:399
  51.5 2.4 %collective-permute-start.2 = (bf16[272,2560]{1,0:T(8,128)(2,1)}, bf16[272,2560]{1,0:T(8,128)(2,1)}, u32[]{:S(2)}, u32[]{:S(2)}) collective-permute-start(bf16[272,2560]{1,0:T(8,128)(2,1)} %collective-permute-done.near_a), channel_id=1, source_target_pairs={{0,384},{128,0},{256,128},{384,256},{1,129},{129,257},{257,385},{3... | collective-permute-start | bytes 4177928 | tf_op jit(solution)/shard_map/section_weights/ppermute | solution.py:398
  54.0 2.8 %collective-permute-start.4 = (bf16[256,2560]{1,0:T(8,128)(2,1)}, bf16[256,2560]{1,0:T(8,128)(2,1)}, u32[]{:S(2)}, u32[]{:S(2)}) collective-permute-start(bf16[256,2560]{1,0:T(8,128)(2,1)} %collective-permute-done.1.near_b), channel_id=1, source_target_pairs={{0,1},{1,0},{2,3},{3,2},{4,5},{5,4},{6,7},{7,6},{8,9},{9,8},{10,11... | collective-permute-start | bytes 3932168 | tf_op jit(solution)/shard_map/section_weights/ppermute | solution.py:400
  56.8 7.4 %collective-permute-start.5 = (bf16[64,512]{1,0:T(8,128)(2,1)S(1)}, bf16[64,512]{1,0:T(8,128)(2,1)S(1)}, u32[]{:S(2)}, u32[]{:S(2)}) collective-permute-start(bf16[64,512]{1,0:T(8,128)(2,1)S(1)} %get-tuple-element.30), channel_id=1, source_target_pairs={{0,64},{16,80},{32,96},{48,112},{64,0},{80,16},{96,32},{112,48},{1... | collective-permute-start | bytes 196616 | tf_op jit(solution)/shard_map/events/ppermute | solution.py:390
  64.2 1.2 routing.1
  65.3 3.3 %all-to-all-start.1 = ((bf16[4,16,128]{2,1,0:T(8,128)(2,1)}), bf16[4,16,128]{2,1,0:T(8,128)(2,1)S(1)}, u32[]{:S(2)}, u32[]{:S(2)}) async-start(bf16[4,16,128]{2,1,0:T(8,128)(2,1)} %get-tuple-element.29), calls=%async_computation.1 | async-start | bytes 32768 | tf_op jit(solution)/shard_map/routing/all_to_all | solution.py:411
  68.6 5.3 %all-to-all-done.1.cot_ref = bf16[4,16,128]{2,1,0:T(8,128)(2,1)S(1)} async-done(((bf16[4,16,128]{2,1,0:T(8,128)(2,1)}), bf16[4,16,128]{2,1,0:T(8,128)(2,1)S(1)}, u32[]{:S(2)}, u32[]{:S(2)}) %all-to-all-start.1) | async-done | bytes 16416 | tf_op jit(solution)/shard_map/routing/all_to_all | solution.py:411
  73.9 1.9 %collective-permute-start.6 = (bf16[272,2560]{1,0:T(8,128)(2,1)}, bf16[272,2560]{1,0:T(8,128)(2,1)S(1)}, u32[]{:S(2)}, u32[]{:S(2)}) collective-permute-start(bf16[272,2560]{1,0:T(8,128)(2,1)} %collective-permute-done.2.far_a), channel_id=1, source_target_pairs={{0,1},{1,0},{2,3},{3,2},{4,5},{5,4},{6,7},{7,6},{8,9},{9,8},{10,11... | collective-permute-start | bytes 4177928 | tf_op jit(solution)/shard_map/section_weights/ppermute | solution.py:416
  75.9 3.3 %collective-permute-done.6.far_b = bf16[272,2560]{1,0:T(8,128)(2,1)S(1)} collective-permute-done((bf16[272,2560]{1,0:T(8,128)(2,1)}, bf16[272,2560]{1,0:T(8,128)(2,1)S(1)}, u32[]{:S(2)}, u32[]{:S(2)}) %collective-permute-start.6) | collective-permute-done | bytes 1392672 | tf_op jit(solution)/shard_map/section_weights/ppermute | solution.py:416
  79.2 1.1 copy-done.11
  80.3 16.0 %layers.1 = bf16[4,208,512]{2,1,0:T(8,128)(2,1)S(1)} custom-call(s32[4]{0:T(128)S(1)} %copy-done.8, bf16[4,64,512]{2,1,0:T(8,128)(2,1)S(1)} %copy-done.3, bf16[64,512]{1,0:T(8,128)(2,1)S(1)} %collective-permute-done.5.other_ref, s32[64,128]{1,0:T(8,128)S(1)} %get-tuple-element.32.count_ref, bf16[4,16,128]{2,1,0:T(8,128)(2,1)S(1)} %all-to-all-done.1.cot_ref, ...), custom_call_target="tpu_custom_call" | custom-call | tf_op jit(solution)/shard_map/layers/pallas_call | solution.py:419
  96.3 17.8 %all_to_all.21.got_ref = bf16[4,208,512]{2,1,0:T(8,128)(2,1)S(1)} all-to-all(bf16[4,208,512]{2,1,0:T(8,128)(2,1)S(1)} %layers.1), channel_id=1, replica_groups=mesh['segment'=4,'z'=8,'y'=8,'core'=2] {'segment'}, dimensions={0} | all-to-all | bytes 1703936 | tf_op jit(solution)/shard_map/section_exchange/all_to_all | solution.py:444
  114.2 1.3 weight_gradient.3
  115.4 1.9 %collective-permute-start.7 = (bf16[272,512]{1,0:T(8,128)(2,1)S(1)}, bf16[272,512]{1,0:T(8,128)(2,1)S(1)}, u32[]{:S(2)}, u32[]{:S(2)}) collective-permute-start(bf16[272,512]{1,0:T(8,128)(2,1)S(1)} %get-tuple-element.38.send_ref), channel_id=1, source_target_pairs={{0,1},{1,0},{2,3},{3,2},{4,5},{5,4},{6,7},{7,6},{8,9},{9,8},{10,11... | collective-permute-start | bytes 835592 | tf_op jit(solution)/shard_map/weight_gradient/ppermute | solution.py:454
  117.3 1.5 %collective-permute-done.7.got_ref = bf16[272,512]{1,0:T(8,128)(2,1)S(1)} collective-permute-done((bf16[272,512]{1,0:T(8,128)(2,1)S(1)}, bf16[272,512]{1,0:T(8,128)(2,1)S(1)}, u32[]{:S(2)}, u32[]{:S(2)}) %collective-permute-start.7) | collective-permute-done | bytes 278560 | tf_op jit(solution)/shard_map/weight_gradient/ppermute | solution.py:454
  119.3 31.5 %all_to_all.22 = bf16[64,6,512]{2,1,0:T(8,128)(2,1)S(1)} all-to-all(bf16[64,6,512]{2,1,0:T(8,128)(2,1)S(1)} %reshape.20), channel_id=1, replica_groups=mesh['segment'=4,'z'=8,'y'=8,'core'=2] {'z','y'}, dimensions={0} | all-to-all | bytes 786432 | tf_op jit(solution)/shard_map/weight_gradient/all_to_all | solution.py:459
  150.9 0.8 weight_gradient.5
  (30 shorter events, 4.0 us)
Async XLA Ops:
  0.6 1.6 %copy-start = (bf16[1,512,2048]{2,1,0:T(8,128)(2,1)S(1)}, bf16[1,512,2048]{2,1,0:T(8,128)(2,1)}, u32[]{:S(2)}) copy-start(bf16[1,512,2048]{2,1,0:T(8,128)(2,1)} %w_in_ref.1) | copy-start | bytes 6291460
  2.2 0.9 copy-start.2
  3.2 1.0 copy-start.4
  4.2 0.7 copy-start.5
  4.9 0.7 copy-start.6
  5.6 0.7 copy-start.7
  6.2 0.7 copy-start.9
  6.9 0.7 copy-start.10
  8.8 70.4 %copy-start.1 = (bf16[272,2560]{1,0:T(8,128)(2,1)}, bf16[272,2560]{1,0:T(8,128)(2,1)S(1)}, u32[]{:S(2)}) copy-start(bf16[272,2560]{1,0:T(8,128)(2,1)S(1)} %get-tuple-element.23.first) | copy-start | bytes 4177924
  8.8 71.5 %copy-start.3 = (bf16[4,64,512]{2,1,0:T(8,128)(2,1)S(1)}, bf16[4,64,512]{2,1,0:T(8,128)(2,1)}, u32[]{:S(2)}) copy-start(bf16[4,64,512]{2,1,0:T(8,128)(2,1)} %events_ref.3) | copy-start | bytes 786436
  8.8 71.5 %copy-start.8 = (s32[4]{0:T(128)S(1)}, s32[4]{0:T(128)}, u32[]{:S(2)}) copy-start(s32[4]{0:T(128)} %plan_ref.3) | copy-start | bytes 52
  8.8 40.8 %collective-permute-start = (bf16[272,2560]{1,0:T(8,128)(2,1)S(1)}, bf16[272,2560]{1,0:T(8,128)(2,1)}, u32[]{:S(2)}, u32[]{:S(2)}) collective-permute-start(bf16[272,2560]{1,0:T(8,128)(2,1)S(1)} %get-tuple-element.23.first), channel_id=1, source_target_pairs={{0,384},{128,0},{256,128},{384,256},{1,129},{129,257},{257,385},{3... | collective-permute-start | bytes 4177928 | tf_op jit(solution)/shard_map/section_weights/ppermute | solution.py:386
  13.6 36.0 %collective-permute-start.1 = (bf16[256,2560]{1,0:T(8,128)(2,1)S(1)}, bf16[256,2560]{1,0:T(8,128)(2,1)}, u32[]{:S(2)}, u32[]{:S(2)}) collective-permute-start(bf16[256,2560]{1,0:T(8,128)(2,1)S(1)} %get-tuple-element.24.second), channel_id=1, source_target_pairs={{0,384},{128,0},{256,128},{384,256},{1,129},{129,257},{257,385},{3... | collective-permute-start | bytes 3932168 | tf_op jit(solution)/shard_map/section_weights/ppermute | solution.py:387
  49.6 24.3 %collective-permute-start.3 = (bf16[272,2560]{1,0:T(8,128)(2,1)}, bf16[272,2560]{1,0:T(8,128)(2,1)}, u32[]{:S(2)}, u32[]{:S(2)}) collective-permute-start(bf16[272,2560]{1,0:T(8,128)(2,1)} %collective-permute-done.near_a), channel_id=1, source_target_pairs={{0,1},{1,0},{2,3},{3,2},{4,5},{5,4},{6,7},{7,6},{8,9},{9,8},{10,11... | collective-permute-start | bytes 4177928 | tf_op jit(solution)/shard_map/section_weights/ppermute | solution.py:399
  51.5 22.4 %collective-permute-start.2 = (bf16[272,2560]{1,0:T(8,128)(2,1)}, bf16[272,2560]{1,0:T(8,128)(2,1)}, u32[]{:S(2)}, u32[]{:S(2)}) collective-permute-start(bf16[272,2560]{1,0:T(8,128)(2,1)} %collective-permute-done.near_a), channel_id=1, source_target_pairs={{0,384},{128,0},{256,128},{384,256},{1,129},{129,257},{257,385},{3... | collective-permute-start | bytes 4177928 | tf_op jit(solution)/shard_map/section_weights/ppermute | solution.py:398
  54.0 20.0 %collective-permute-start.4 = (bf16[256,2560]{1,0:T(8,128)(2,1)}, bf16[256,2560]{1,0:T(8,128)(2,1)}, u32[]{:S(2)}, u32[]{:S(2)}) collective-permute-start(bf16[256,2560]{1,0:T(8,128)(2,1)} %collective-permute-done.1.near_b), channel_id=1, source_target_pairs={{0,1},{1,0},{2,3},{3,2},{4,5},{5,4},{6,7},{7,6},{8,9},{9,8},{10,11... | collective-permute-start | bytes 3932168 | tf_op jit(solution)/shard_map/section_weights/ppermute | solution.py:400
  56.8 11.8 %collective-permute-start.5 = (bf16[64,512]{1,0:T(8,128)(2,1)S(1)}, bf16[64,512]{1,0:T(8,128)(2,1)S(1)}, u32[]{:S(2)}, u32[]{:S(2)}) collective-permute-start(bf16[64,512]{1,0:T(8,128)(2,1)S(1)} %get-tuple-element.30), channel_id=1, source_target_pairs={{0,64},{16,80},{32,96},{48,112},{64,0},{80,16},{96,32},{112,48},{1... | collective-permute-start | bytes 196616 | tf_op jit(solution)/shard_map/events/ppermute | solution.py:390
  65.3 8.6 %all-to-all-start.1 = ((bf16[4,16,128]{2,1,0:T(8,128)(2,1)}), bf16[4,16,128]{2,1,0:T(8,128)(2,1)S(1)}, u32[]{:S(2)}, u32[]{:S(2)}) async-start(bf16[4,16,128]{2,1,0:T(8,128)(2,1)} %get-tuple-element.29), calls=%async_computation.1 | async-start | bytes 32768 | tf_op jit(solution)/shard_map/routing/all_to_all | solution.py:411
  73.9 5.3 %collective-permute-start.6 = (bf16[272,2560]{1,0:T(8,128)(2,1)}, bf16[272,2560]{1,0:T(8,128)(2,1)S(1)}, u32[]{:S(2)}, u32[]{:S(2)}) collective-permute-start(bf16[272,2560]{1,0:T(8,128)(2,1)} %collective-permute-done.2.far_a), channel_id=1, source_target_pairs={{0,1},{1,0},{2,3},{3,2},{4,5},{5,4},{6,7},{7,6},{8,9},{9,8},{10,11... | collective-permute-start | bytes 4177928 | tf_op jit(solution)/shard_map/section_weights/ppermute | solution.py:416
  79.2 1.1 copy-start.11
  115.4 3.4 %collective-permute-start.7 = (bf16[272,512]{1,0:T(8,128)(2,1)S(1)}, bf16[272,512]{1,0:T(8,128)(2,1)S(1)}, u32[]{:S(2)}, u32[]{:S(2)}) collective-permute-start(bf16[272,512]{1,0:T(8,128)(2,1)S(1)} %get-tuple-element.38.send_ref), channel_id=1, source_target_pairs={{0,1},{1,0},{2,3},{3,2},{4,5},{5,4},{6,7},{7,6},{8,9},{9,8},{10,11... | collective-permute-start | bytes 835592 | tf_op jit(solution)/shard_map/weight_gradient/ppermute | solution.py:454

commit v4 on v3

--- a/solution.py
+++ b/solution.py
@@ -52,25 +52,34 @@
 def packing_start(
     plan_ref, routes_ref, lengths_ref, w_in_ref, w_out_ref, events_ref, bias_ref, cot_ref,
     first_ref, second_ref, outgoing_ref, facts_ref,
-    table, sems,
+    plan, routes, lengths, bias_s, cot_s, table, sems,
 ):
     core = lax.axis_index("core")
     half = WIDTH // 2
+    small = [(plan_ref, plan), (routes_ref, routes), (lengths_ref, lengths), (bias_ref.at[0], bias_s), (cot_ref.at[0], cot_s)]
+    small = [pltpu.make_async_copy(*c, sems.at[n]) for n, c in enumerate(small)]
+    for c in small:
+        c.start()
     copies = []
     for side, dest in ((core, first_ref), (1 - core, second_ref)):
-        rows = pl.ds(pl.multiple_of(side * half, half), half)
-        copies.append((w_in_ref.at[0, rows], dest.at[pl.ds(0, half), pl.ds(0, 4 * WIDTH)]))
-        copies.append((w_out_ref.at[0, rows], dest.at[pl.ds(0, half), pl.ds(4 * WIDTH, WIDTH)]))
+        for part in range(2):
+            rows = pl.ds(pl.multiple_of(side * half + part * (half // 2), half // 2), half // 2)
+            to = pl.ds(part * (half // 2), half // 2)
+            copies.append((w_in_ref.at[0, rows], dest.at[to, pl.ds(0, 4 * WIDTH)]))
+            copies.append((w_out_ref.at[0, rows], dest.at[to, pl.ds(4 * WIDTH, WIDTH)]))
+    copies = [pltpu.make_async_copy(*c, sems.at[len(small) + n]) for n, c in enumerate(copies)]
+    for c in copies:
+        c.start()
+    for c in small:
+        c.wait()
     partner_value = DEV_HIST + 2 * lax.axis_index("segment") - wanted_value()
     chosen = jnp.int32(0)
     for h in range(DEV_HIST):
-        chosen = chosen + jnp.where(plan_ref[h] == partner_value, h, 0)
-    copies.append((events_ref.at[chosen], outgoing_ref))
-    copies = [pltpu.make_async_copy(*c, sems.at[n]) for n, c in enumerate(copies)]
-    for c in copies:
-        c.start()
-
-    bias = bias_ref[0]
+        chosen = chosen + jnp.where(plan[h] == partner_value, h, 0)
+    copies.append(pltpu.make_async_copy(events_ref.at[chosen], outgoing_ref, sems.at[len(small) + len(copies)]))
+    copies[-1].start()
+
+    bias = bias_s[...]
     high = bias.astype(BF).astype(F32)
     middle = (bias - high).astype(BF).astype(F32)
     low = bias - high - middle
@@ -85,15 +94,15 @@
     to_odd = (place == ROWS - distance).astype(F32).astype(BF)
     base = mm(mm(pick_even, pieces).astype(BF), to_even) + mm(mm(pick_odd, pieces).astype(BF), to_odd)
     table[...] = base.astype(BF)
-    copy = pltpu.make_async_copy(table, first_ref.at[pl.ds(half, 16), pl.ds(0, 128)], sems.at[len(copies)])
+    copy = pltpu.make_async_copy(table, first_ref.at[pl.ds(half, 16), pl.ds(0, 128)], sems.at[len(small) + len(copies)])
     copy.start()
 
     lane = iota((1, 128), 1)
     facts = jnp.zeros((1, 128), F32)
-    for j, ref in enumerate((routes_ref, plan_ref, lengths_ref)):
+    for j, ref in enumerate((routes, plan, lengths)):
         for h in range(DEV_HIST):
             facts = jnp.where(lane == 4 * j + h, ref[h].astype(F32), facts)
-    cot = cot_ref[0].astype(F32)
+    cot = cot_s[...].astype(F32)
     blocks = [cot[k : k + 1] for k in range(SLOTS)] + [facts, jnp.zeros((1, 128), F32)]
     lines = [jnp.concatenate(blocks[k : k + 5], axis=1) for k in (0, 5)]
     facts_ref[...] = jnp.broadcast_to(jnp.concatenate(lines).astype(BF)[None], facts_ref.shape)
@@ -166,16 +175,23 @@
     near = lax.rem(segment + 1 + 2 * core, LAYERS)
     swap = lax.rem(segment + 3 + 2 * core, LAYERS)
     far = lax.rem(segment + 2, LAYERS)
-    for piece, l in ((first, segment), (near_a, near), (swap_a, swap), (far_a, far)):
-        pltpu.make_async_copy(
-            piece.at[pl.ds(half, 16), pl.ds(0, 128)], tables.at[l], table_sem.at[l]
-        ).start()
-    for piece, l, side in (
-        (first, segment, core), (second, segment, 1 - core), (near_a, near, core), (near_b, near, 1 - core),
-        (swap_a, swap, 1 - core), (swap_b, swap, core), (far_a, far, core), (far_b, far, 1 - core),
-    ):
-        rows = pl.ds(pl.multiple_of(side * half, half), half)
-        pltpu.make_async_copy(piece.at[pl.ds(0, half)], weights.at[l, rows], sems.at[l, side]).start()
+    held = (
+        (segment, first, core, second, 1 - core),
+        (near, near_a, core, near_b, 1 - core),
+        (swap, swap_a, 1 - core, swap_b, core),
+        (far, far_a, core, far_b, 1 - core),
+    )
+    for l in range(LAYERS):
+        for slot, one, side, two, other_side in held:
+
+            @pl.when(slot == l)
+            def _():
+                pltpu.make_async_copy(
+                    one.at[pl.ds(half, 16), pl.ds(0, 128)], tables.at[l], table_sem.at[l]
+                ).start()
+                for piece, at in ((one, side), (two, other_side)):
+                    rows = pl.ds(pl.multiple_of(at * half, half), half)
+                    pltpu.make_async_copy(piece.at[pl.ds(0, half)], weights.at[l, rows], sems.at[l, at]).start()
 
     lane, row = iota((ROWS, 128), 1), iota((ROWS, 128), 0)
     left = (lane < HEAD_COLS).astype(F32)
@@ -183,14 +199,6 @@
     column = jnp.where(lane < HEAD_COLS, lane, lane - HEAD_COLS)
     count = count_ref[...]
     allowed = (column <= row) & (column < count)
-
-    for l in range(LAYERS):
-        pltpu.make_async_copy(tables.at[l], tables.at[l], table_sem.at[l]).wait()
-        table = tables[l].astype(F32)
-        table = table[0:4] + table[4:8] + table[8:12]
-        for p in range(PAIRS):
-            wide = jnp.broadcast_to(table[p : p + 1], (ROWS, 128))
-            bias_s[l, p] = pltpu.roll(wide, 0, 1, stride=1, stride_axis=0)
 
     def block_diagonal(a):
         return jnp.concatenate([a * left_b, a * right_b], axis=0)
@@ -220,6 +228,12 @@
         for c in range(2):
             piece = weights.at[l, pl.ds(c * half, half)]
             pltpu.make_async_copy(piece, piece, sems.at[l, c]).wait()
+        pltpu.make_async_copy(tables.at[l], tables.at[l], table_sem.at[l]).wait()
+        table = tables[l].astype(F32)
+        table = table[0:4] + table[4:8] + table[8:12]
+        for p in range(PAIRS):
+            wide = jnp.broadcast_to(table[p : p + 1], (ROWS, 128))
+            bias_s[l, p] = pltpu.roll(wide, 0, 1, stride=1, stride_axis=0)
         normed_b = normed.astype(BF)
         for kind in range(4):
             cols = pl.ds(kind * WIDTH, WIDTH)
@@ -374,9 +388,18 @@
                 shape((ROWS, WIDTH), BF),
                 shape((n_dp, 2, (SLOTS + 2) * 64), BF),
             ),
-            scratch=[pltpu.VMEM((16, 128), BF), pltpu.SemaphoreType.DMA((6,))],
-            in_specs=[smem] * 3 + [any_spec] * 3 + [vmem] * 2,
+            scratch=[
+                pltpu.SMEM((DEV_HIST,), jnp.int32),
+                pltpu.SMEM((DEV_HIST,), jnp.int32),
+                pltpu.SMEM((DEV_HIST,), jnp.int32),
+                pltpu.VMEM((8, ROWS), F32),
+                pltpu.VMEM((SLOTS, 128), BF),
+                pltpu.VMEM((16, 128), BF),
+                pltpu.SemaphoreType.DMA((15,)),
+            ],
+            in_specs=[any_spec] * 8,
             out_specs=(any_spec, any_spec, any_spec, vmem),
+            limit=58,
         )(balance_plan, routes.reshape(DEV_HIST), lengths, w_uvqk, w_out, events, rel_bias, state_cotangent)
 
     with jax.named_scope("section_weights"):
@@ -391,7 +414,8 @@
 
     with jax.named_scope("routing"):
         facts = lax.all_to_all(facts, DP, 0, 0, tiled=True)
-        near_a, near_b, facts = lax.optimization_barrier((near_a, near_b, facts))
+        near_a, other_events, facts = lax.optimization_barrier((near_a, other_events, facts))
+        near_b, facts = lax.optimization_barrier((near_b, facts))
         facts = facts.reshape(n_dp, (SLOTS + 2) * 128)
 
     with jax.named_scope("section_weights"):
@@ -409,9 +433,7 @@
             ),
         )(facts)
         seeds = lax.all_to_all(seeds, "segment", 0, 0, tiled=True)
-        far_a, swap_a, swap_b, seeds, other_events = lax.optimization_barrier(
-            (far_a, swap_a, swap_b, seeds, other_events)
-        )
+        far_a, swap_a, swap_b, seeds = lax.optimization_barrier((far_a, swap_a, swap_b, seeds))
     with jax.named_scope("section_weights"):
         far_b = lax.ppermute(far_a, "core", swap)
 
@@ -435,6 +457,7 @@
                 pltpu.SemaphoreType.DMA((LAYERS,)),
             ],
             in_specs=[smem] + [vmem] * 4 + [any_spec] * 8,
+            limit=28,
         )(
             balance_plan, events, other_events, count, seeds,
             first, second, near_a, near_b, swap_a, swap_b, far_a, far_b,

time: 152 us -> 221 us (1.45)
  Pallas kernels: 20.8 us -> 102 us
  blocking collectives: 82.5 us -> 58.8 us
  starting transfers between devices: 29.1 us -> 44.1 us
  local copies, waits for them, and re-layouts: 8.35 us -> 1.63 us
  waiting for transfers between devices: 10.2 us -> 12.7 us
    pallas_call x1, Pallas kernels: 1.21 us -> 83.4 us  [body(): call(packing_start, (shape((half + 16, 5 * WIDTH), BF), shape((half, 5 *...]
    all_to_all x1, blocking collectives: 33.2 us -> 14.2 us  [body(): seeds = lax.all_to_all(seeds, 'segment', 0, 0, tiled=True)]
    all_to_all x1, starting transfers between devices: 3.25 us -> 17.4 us  [body(): facts = lax.all_to_all(facts, DP, 0, 0, tiled=True)]
    ppermute x1, waiting for transfers between devices: 0.01 us -> 7.92 us  [body(): lax.ppermute(outgoing, 'z', [(i, (i + n_z // 2) % n_z) for i in range(n_z)])]
    unnamed x25 -> x9, local copies, waits for them, and re-layouts: 8.08 us -> 1.37 us
    all_to_all x1, waiting for transfers between devices: 5.32 us -> 0.53 us  [body(): facts = lax.all_to_all(facts, DP, 0, 0, tiled=True)]
    all_to_all x1, blocking collectives: 31.5 us -> 27.7 us  [body(): lax.all_to_all(blocks.reshape(chips, block_rows, WIDTH), ('z', 'y'), 0, 0...]
  transfers between devices with their start and end apart: 9 -> 9, of which waited for: 3 -> 4; matrix products, arithmetic and copies ran while one was open for 0% -> 0% of each run, Pallas kernels for 1% -> 0%
where the time goes in v4:
time: 221 us; the launch traced here: 220 us
  Pallas kernels  102 us (46%)
  blocking collectives  58.8 us (27%)
  starting transfers between devices  44.1 us (20%)
  waiting for transfers between devices  12.7 us (6%)
    pallas_call x1, Pallas kernels, body(): call(packing_start, (shape((half + 16, 5 * WIDTH), BF), shape((half, 5 *...  83.4 us
    all_to_all x1, blocking collectives, body(): lax.all_to_all(blocks.reshape(chips, block_rows, WIDTH), ('z', 'y'), 0, 0...  27.7 us
    all_to_all x1, starting transfers between devices, body(): facts = lax.all_to_all(facts, DP, 0, 0, tiled=True)  17.4 us
    all_to_all x1, blocking collectives, body(): arrived = lax.all_to_all(message, 'segment', 0, 0, tiled=True)  16.8 us
    pallas_call x1, Pallas kernels, body(): call(layers_kernel, shape((LAYERS, MSG, WIDTH), BF), scratch=[pltpu.VMEM(...  15.6 us
    all_to_all x1, blocking collectives, body(): seeds = lax.all_to_all(seeds, 'segment', 0, 0, tiled=True)  14.2 us
    ppermute x1, waiting for transfers between devices, body(): lax.ppermute(outgoing, 'z', [(i, (i + n_z // 2) % n_z) for i in range(n_z)])  7.92 us
    ppermute x1, starting transfers between devices, body(): lax.ppermute(outgoing, 'z', [(i, (i + n_z // 2) % n_z) for i in range(n_z)])  7.61 us
  transfers between devices with their start and end apart: 9, of which 4 were waited for; matrix products, arithmetic and copies ran while one was open for 0% of the time, Pallas kernels for 0%

profile of v4, /device:TPU:8, one launch (start us, length us, event | category | flops | bytes accessed | tf_op | source)
XLA Modules:
  0.0 220.4 jit_solution(3963622235491670909)
XLA Ops:
  0.6 83.4 %packing.1 = (bf16[272,2560]{1,0:T(8,128)(2,1)}, bf16[256,2560]{1,0:T(8,128)(2,1)}, bf16[64,512]{1,0:T(8,128)(2,1)}, bf16[128,2,640]{2,1,0:T(2,128)(2,1)}) custom-call(s32[4]{0:T(128)} %plan_ref.3, s32[4]{0:T(128)} %bitcast.8, s32[4]{0:T(128)} %lengths_ref.1, bf16[1,512,2048]{2,1,0:T(8,128)(2,1)} %w_in_ref.1, bf16[1,512,512]{2,1,0:T(8,128)(2,1)} %w_out_ref.1, ...), custom_call_target="tpu_custom_call" | custom-call | tf_op jit(solution)/shard_map/packing/pallas_call | solution.py:383
  84.0 4.8 %collective-permute-start = (bf16[272,2560]{1,0:T(8,128)(2,1)}, bf16[272,2560]{1,0:T(8,128)(2,1)S(1)}, u32[]{:S(2)}, u32[]{:S(2)}) collective-permute-start(bf16[272,2560]{1,0:T(8,128)(2,1)} %get-tuple-element.24.first), channel_id=1, source_target_pairs={{0,384},{128,0},{256,128},{384,256},{1,129},{129,257},{257,385},{3... | collective-permute-start | bytes 4177928 | tf_op jit(solution)/shard_map/section_weights/ppermute | solution.py:409
  88.8 2.7 %collective-permute-start.2 = (bf16[256,2560]{1,0:T(8,128)(2,1)}, bf16[256,2560]{1,0:T(8,128)(2,1)}, u32[]{:S(2)}, u32[]{:S(2)}) collective-permute-start(bf16[256,2560]{1,0:T(8,128)(2,1)} %get-tuple-element.28.second), channel_id=1, source_target_pairs={{0,384},{128,0},{256,128},{384,256},{1,129},{129,257},{257,385},{3... | collective-permute-start | bytes 3932168 | tf_op jit(solution)/shard_map/section_weights/ppermute | solution.py:410
  91.6 17.4 %all-to-all-start = ((bf16[128,2,640]{2,1,0:T(2,128)(2,1)}), bf16[128,2,640]{2,1,0:T(2,128)(2,1)S(1)}, u32[]{:S(2)}, u32[]{:S(2)}) async-start(bf16[128,2,640]{2,1,0:T(2,128)(2,1)} %get-tuple-element.26), calls=%async_computation | async-start | bytes 655360 | tf_op jit(solution)/shard_map/routing/all_to_all | solution.py:416
  109.0 7.6 %collective-permute-start.1 = (bf16[64,512]{1,0:T(8,128)(2,1)}, bf16[64,512]{1,0:T(8,128)(2,1)S(1)}, u32[]{:S(2)}, u32[]{:S(2)}) collective-permute-start(bf16[64,512]{1,0:T(8,128)(2,1)} %get-tuple-element.25), channel_id=1, source_target_pairs={{0,64},{16,80},{32,96},{48,112},{64,0},{80,16},{96,32},{112,48},{1... | collective-permute-start | bytes 196616 | tf_op jit(solution)/shard_map/events/ppermute | solution.py:413
  116.6 7.9 %collective-permute-done.1.other_ref = bf16[64,512]{1,0:T(8,128)(2,1)S(1)} collective-permute-done((bf16[64,512]{1,0:T(8,128)(2,1)}, bf16[64,512]{1,0:T(8,128)(2,1)S(1)}, u32[]{:S(2)}, u32[]{:S(2)}) %collective-permute-start.1) | collective-permute-done | bytes 65568 | tf_op jit(solution)/shard_map/events/ppermute | solution.py:413
  124.5 0.5 all-to-all-done
  125.0 1.9 collective-permute-start.4
  127.0 2.4 %collective-permute-start.3 = (bf16[272,2560]{1,0:T(8,128)(2,1)S(1)}, bf16[272,2560]{1,0:T(8,128)(2,1)S(1)}, u32[]{:S(2)}, u32[]{:S(2)}) collective-permute-start(bf16[272,2560]{1,0:T(8,128)(2,1)S(1)} %collective-permute-done.near_a), channel_id=1, source_target_pairs={{0,384},{128,0},{256,128},{384,256},{1,129},{129,257},{257,385},{3... | collective-permute-start | bytes 4177928 | tf_op jit(solution)/shard_map/section_weights/ppermute | solution.py:422
  129.4 2.8 %collective-permute-start.5 = (bf16[256,2560]{1,0:T(8,128)(2,1)}, bf16[256,2560]{1,0:T(8,128)(2,1)S(1)}, u32[]{:S(2)}, u32[]{:S(2)}) collective-permute-start(bf16[256,2560]{1,0:T(8,128)(2,1)} %collective-permute-done.2.near_b), channel_id=1, source_target_pairs={{0,1},{1,0},{2,3},{3,2},{4,5},{5,4},{6,7},{7,6},{8,9},{9,8},{10,11... | collective-permute-start | bytes 3932168 | tf_op jit(solution)/shard_map/section_weights/ppermute | solution.py:424
  132.3 1.0 routing.1
  133.2 14.2 %all_to_all.20.cot_ref = bf16[4,16,128]{2,1,0:T(8,128)(2,1)S(1)} all-to-all(bf16[4,16,128]{2,1,0:T(8,128)(2,1)S(1)} %get-tuple-element.34), channel_id=1, replica_groups=mesh['segment'=4,'z'=8,'y'=8,'core'=2] {'segment'}, dimensions={0} | all-to-all | bytes 32768 | tf_op jit(solution)/shard_map/routing/all_to_all | solution.py:435
  147.5 2.5 %collective-permute-start.6 = (bf16[272,2560]{1,0:T(8,128)(2,1)S(1)}, bf16[272,2560]{1,0:T(8,128)(2,1)S(1)}, u32[]{:S(2)}, u32[]{:S(2)}) collective-permute-start(bf16[272,2560]{1,0:T(8,128)(2,1)S(1)} %collective-permute-done.3.far_a), channel_id=1, source_target_pairs={{0,1},{1,0},{2,3},{3,2},{4,5},{5,4},{6,7},{7,6},{8,9},{9,8},{10,11... | collective-permute-start | bytes 4177928 | tf_op jit(solution)/shard_map/section_weights/ppermute | solution.py:438
  150.0 2.8 %collective-permute-done.6.far_b = bf16[272,2560]{1,0:T(8,128)(2,1)S(1)} collective-permute-done((bf16[272,2560]{1,0:T(8,128)(2,1)S(1)}, bf16[272,2560]{1,0:T(8,128)(2,1)S(1)}, u32[]{:S(2)}, u32[]{:S(2)}) %collective-permute-start.6) | collective-permute-done | bytes 1392672 | tf_op jit(solution)/shard_map/section_weights/ppermute | solution.py:438
  152.8 1.3 copy-done.1
  154.1 15.6 %layers.1 = bf16[4,208,512]{2,1,0:T(8,128)(2,1)S(1)} custom-call(s32[4]{0:T(128)S(1)} %copy-done.3, bf16[4,64,512]{2,1,0:T(8,128)(2,1)S(1)} %copy-done.2, bf16[64,512]{1,0:T(8,128)(2,1)S(1)} %collective-permute-done.1.other_ref, s32[64,128]{1,0:T(8,128)S(1)} %get-tuple-element.31.count_ref, bf16[4,16,128]{2,1,0:T(8,128)(2,1)S(1)} %all_to_all.20.cot_ref, ...), custom_call_target="tpu_custom_call" | custom-call | tf_op jit(solution)/shard_map/layers/pallas_call | solution.py:441
  169.7 16.8 %all_to_all.21.got_ref = bf16[4,208,512]{2,1,0:T(8,128)(2,1)S(1)} all-to-all(bf16[4,208,512]{2,1,0:T(8,128)(2,1)S(1)} %layers.1), channel_id=1, replica_groups=mesh['segment'=4,'z'=8,'y'=8,'core'=2] {'segment'}, dimensions={0} | all-to-all | bytes 1703936 | tf_op jit(solution)/shard_map/section_exchange/all_to_all | solution.py:467
  186.5 1.3 weight_gradient.3
  187.8 1.9 collective-permute-start.7
  189.7 1.5 collective-permute-done.7.got_ref
  191.2 0.3 weight_gradient.4
  191.7 27.7 %all_to_all.22 = bf16[64,6,512]{2,1,0:T(8,128)(2,1)S(1)} all-to-all(bf16[64,6,512]{2,1,0:T(8,128)(2,1)S(1)} %reshape.20), channel_id=1, replica_groups=mesh['segment'=4,'z'=8,'y'=8,'core'=2] {'z','y'}, dimensions={0} | all-to-all | bytes 786432 | tf_op jit(solution)/shard_map/weight_gradient/all_to_all | solution.py:482
  219.4 0.1 reshape.21.got_ref
  219.6 0.8 weight_gradient.5
  (14 shorter events, 0.2 us)
Async XLA Ops:
  84.0 68.8 %copy-start = (bf16[272,2560]{1,0:T(8,128)(2,1)S(1)}, bf16[272,2560]{1,0:T(8,128)(2,1)}, u32[]{:S(2)}) copy-start(bf16[272,2560]{1,0:T(8,128)(2,1)} %get-tuple-element.24.first) | copy-start | bytes 4177924
  84.0 68.8 %copy-start.2 = (bf16[4,64,512]{2,1,0:T(8,128)(2,1)S(1)}, bf16[4,64,512]{2,1,0:T(8,128)(2,1)}, u32[]{:S(2)}) copy-start(bf16[4,64,512]{2,1,0:T(8,128)(2,1)} %events_ref.3) | copy-start | bytes 786436
  84.0 68.7 %copy-start.3 = (s32[4]{0:T(128)S(1)}, s32[4]{0:T(128)}, u32[]{:S(2)}) copy-start(s32[4]{0:T(128)} %plan_ref.3) | copy-start | bytes 52
  84.0 41.0 %collective-permute-start = (bf16[272,2560]{1,0:T(8,128)(2,1)}, bf16[272,2560]{1,0:T(8,128)(2,1)S(1)}, u32[]{:S(2)}, u32[]{:S(2)}) collective-permute-start(bf16[272,2560]{1,0:T(8,128)(2,1)} %get-tuple-element.24.first), channel_id=1, source_target_pairs={{0,384},{128,0},{256,128},{384,256},{1,129},{129,257},{257,385},{3... | collective-permute-start | bytes 4177928 | tf_op jit(solution)/shard_map/section_weights/ppermute | solution.py:409
  88.8 40.6 %collective-permute-start.2 = (bf16[256,2560]{1,0:T(8,128)(2,1)}, bf16[256,2560]{1,0:T(8,128)(2,1)}, u32[]{:S(2)}, u32[]{:S(2)}) collective-permute-start(bf16[256,2560]{1,0:T(8,128)(2,1)} %get-tuple-element.28.second), channel_id=1, source_target_pairs={{0,384},{128,0},{256,128},{384,256},{1,129},{129,257},{257,385},{3... | collective-permute-start | bytes 3932168 | tf_op jit(solution)/shard_map/section_weights/ppermute | solution.py:410
  91.6 33.4 %all-to-all-start = ((bf16[128,2,640]{2,1,0:T(2,128)(2,1)}), bf16[128,2,640]{2,1,0:T(2,128)(2,1)S(1)}, u32[]{:S(2)}, u32[]{:S(2)}) async-start(bf16[128,2,640]{2,1,0:T(2,128)(2,1)} %get-tuple-element.26), calls=%async_computation | async-start | bytes 655360 | tf_op jit(solution)/shard_map/routing/all_to_all | solution.py:416
  109.0 15.5 %collective-permute-start.1 = (bf16[64,512]{1,0:T(8,128)(2,1)}, bf16[64,512]{1,0:T(8,128)(2,1)S(1)}, u32[]{:S(2)}, u32[]{:S(2)}) collective-permute-start(bf16[64,512]{1,0:T(8,128)(2,1)} %get-tuple-element.25), channel_id=1, source_target_pairs={{0,64},{16,80},{32,96},{48,112},{64,0},{80,16},{96,32},{112,48},{1... | collective-permute-start | bytes 196616 | tf_op jit(solution)/shard_map/events/ppermute | solution.py:413
  125.0 22.4 %collective-permute-start.4 = (bf16[272,2560]{1,0:T(8,128)(2,1)S(1)}, bf16[272,2560]{1,0:T(8,128)(2,1)S(1)}, u32[]{:S(2)}, u32[]{:S(2)}) collective-permute-start(bf16[272,2560]{1,0:T(8,128)(2,1)S(1)} %collective-permute-done.near_a), channel_id=1, source_target_pairs={{0,1},{1,0},{2,3},{3,2},{4,5},{5,4},{6,7},{7,6},{8,9},{9,8},{10,11... | collective-permute-start | bytes 4177928 | tf_op jit(solution)/shard_map/section_weights/ppermute | solution.py:423
  127.0 20.5 %collective-permute-start.3 = (bf16[272,2560]{1,0:T(8,128)(2,1)S(1)}, bf16[272,2560]{1,0:T(8,128)(2,1)S(1)}, u32[]{:S(2)}, u32[]{:S(2)}) collective-permute-start(bf16[272,2560]{1,0:T(8,128)(2,1)S(1)} %collective-permute-done.near_a), channel_id=1, source_target_pairs={{0,384},{128,0},{256,128},{384,256},{1,129},{129,257},{257,385},{3... | collective-permute-start | bytes 4177928 | tf_op jit(solution)/shard_map/section_weights/ppermute | solution.py:422
  129.4 18.1 %collective-permute-start.5 = (bf16[256,2560]{1,0:T(8,128)(2,1)}, bf16[256,2560]{1,0:T(8,128)(2,1)S(1)}, u32[]{:S(2)}, u32[]{:S(2)}) collective-permute-start(bf16[256,2560]{1,0:T(8,128)(2,1)} %collective-permute-done.2.near_b), channel_id=1, source_target_pairs={{0,1},{1,0},{2,3},{3,2},{4,5},{5,4},{6,7},{7,6},{8,9},{9,8},{10,11... | collective-permute-start | bytes 3932168 | tf_op jit(solution)/shard_map/section_weights/ppermute | solution.py:424
  147.5 5.3 %collective-permute-start.6 = (bf16[272,2560]{1,0:T(8,128)(2,1)S(1)}, bf16[272,2560]{1,0:T(8,128)(2,1)S(1)}, u32[]{:S(2)}, u32[]{:S(2)}) collective-permute-start(bf16[272,2560]{1,0:T(8,128)(2,1)S(1)} %collective-permute-done.3.far_a), channel_id=1, source_target_pairs={{0,1},{1,0},{2,3},{3,2},{4,5},{5,4},{6,7},{7,6},{8,9},{9,8},{10,11... | collective-permute-start | bytes 4177928 | tf_op jit(solution)/shard_map/section_weights/ppermute | solution.py:438
  152.8 1.3 copy-start.1
  187.8 3.4 %collective-permute-start.7 = (bf16[272,512]{1,0:T(8,128)(2,1)S(1)}, bf16[272,512]{1,0:T(8,128)(2,1)S(1)}, u32[]{:S(2)}, u32[]{:S(2)}) collective-permute-start(bf16[272,512]{1,0:T(8,128)(2,1)S(1)} %get-tuple-element.40.send_ref), channel_id=1, source_target_pairs={{0,1},{1,0},{2,3},{3,2},{4,5},{5,4},{6,7},{7,6},{8,9},{9,8},{10,11... | collective-permute-start | bytes 835592 | tf_op jit(solution)/shard_map/weight_gradient/ppermute | solution.py:477

commit v5 on v4

--- a/solution.py
+++ b/solution.py
@@ -52,7 +52,7 @@
 def packing_start(
     plan_ref, routes_ref, lengths_ref, w_in_ref, w_out_ref, events_ref, bias_ref, cot_ref,
     first_ref, second_ref, outgoing_ref, facts_ref,
-    plan, routes, lengths, bias_s, cot_s, table, sems,
+    plan, routes, lengths, bias_s, cot_s, sems,
 ):
     core = lax.axis_index("core")
     half = WIDTH // 2
@@ -93,9 +93,8 @@
     to_even = (place == (128 - distance) % 128).astype(F32).astype(BF)
     to_odd = (place == ROWS - distance).astype(F32).astype(BF)
     base = mm(mm(pick_even, pieces).astype(BF), to_even) + mm(mm(pick_odd, pieces).astype(BF), to_odd)
-    table[...] = base.astype(BF)
-    copy = pltpu.make_async_copy(table, first_ref.at[pl.ds(half, 16), pl.ds(0, 128)], sems.at[len(small) + len(copies)])
-    copy.start()
+    first_ref[half : half + 16, 0:128] = base.astype(BF)
+    first_ref[half : half + 16, 128 : 5 * WIDTH] = jnp.zeros((16, 5 * WIDTH - 128), BF)
 
     lane = iota((1, 128), 1)
     facts = jnp.zeros((1, 128), F32)
@@ -108,7 +107,6 @@
     facts_ref[...] = jnp.broadcast_to(jnp.concatenate(lines).astype(BF)[None], facts_ref.shape)
     for c in copies:
         c.wait()
-    copy.wait()
 
 
 def whole_part(a, d):
@@ -394,11 +392,9 @@
                 pltpu.SMEM((DEV_HIST,), jnp.int32),
                 pltpu.VMEM((8, ROWS), F32),
                 pltpu.VMEM((SLOTS, 128), BF),
-                pltpu.VMEM((16, 128), BF),
-                pltpu.SemaphoreType.DMA((15,)),
+                pltpu.SemaphoreType.DMA((14,)),
             ],
             in_specs=[any_spec] * 8,
-            out_specs=(any_spec, any_spec, any_spec, vmem),
             limit=58,
         )(balance_plan, routes.reshape(DEV_HIST), lengths, w_uvqk, w_out, events, rel_bias, state_cotangent)
 

time: 221 us -> 141 us (0.64)
  Pallas kernels: 102 us -> 22.5 us
    pallas_call x1, Pallas kernels: 83.4 us -> 3.57 us  [body(): call(packing_start, (shape((half + 16, 5 * WIDTH), BF), shape((half, 5 *...]
  transfers between devices with their start and end apart: 9 -> 9, of which waited for: 4 -> 4; matrix products, arithmetic and copies ran while one was open for 0% -> 0% of each run, Pallas kernels for 0% -> 1%
where the time goes in v5:
time: 141 us
  blocking collectives  58.8 us (42%)
  starting transfers between devices  44.1 us (31%)
  Pallas kernels  22.5 us (16%)
  waiting for transfers between devices  12.7 us (9%)
  local copies, waits for them, and re-layouts  1.63 us (1%)
    all_to_all x1, blocking collectives, body(): lax.all_to_all(blocks.reshape(chips, block_rows, WIDTH), ('z', 'y'), 0, 0...  27.7 us
    all_to_all x1, starting transfers between devices, body(): facts = lax.all_to_all(facts, DP, 0, 0, tiled=True)  17.4 us
    all_to_all x1, blocking collectives, body(): arrived = lax.all_to_all(message, 'segment', 0, 0, tiled=True)  16.8 us
    pallas_call x1, Pallas kernels, body(): call(layers_kernel, shape((LAYERS, MSG, WIDTH), BF), scratch=[pltpu.VMEM(...  15.6 us
    all_to_all x1, blocking collectives, body(): seeds = lax.all_to_all(seeds, 'segment', 0, 0, tiled=True)  14.2 us
    ppermute x1, waiting for transfers between devices, body(): lax.ppermute(outgoing, 'z', [(i, (i + n_z // 2) % n_z) for i in range(n_z)])  7.92 us
    ppermute x1, starting transfers between devices, body(): lax.ppermute(outgoing, 'z', [(i, (i + n_z // 2) % n_z) for i in range(n_z)])  7.61 us
    ppermute x1, starting transfers between devices, body(): near_a = lax.ppermute(first, ('segment', 'core'), ring)  4.8 us
  transfers between devices with their start and end apart: 9, of which 4 were waited for; matrix products, arithmetic and copies ran while one was open for 0% of the time, Pallas kernels for 1%

profile of v5, /device:TPU:8, one launch (start us, length us, event | category | flops | bytes accessed | tf_op | source)
XLA Modules:
  0.0 140.6 jit_solution(2770110807137154975)
XLA Ops:
  0.6 3.6 %packing.1 = (bf16[272,2560]{1,0:T(8,128)(2,1)}, bf16[256,2560]{1,0:T(8,128)(2,1)}, bf16[64,512]{1,0:T(8,128)(2,1)}, bf16[128,2,640]{2,1,0:T(2,128)(2,1)}) custom-call(s32[4]{0:T(128)} %plan_ref.3, s32[4]{0:T(128)} %bitcast.8, s32[4]{0:T(128)} %lengths_ref.1, bf16[1,512,2048]{2,1,0:T(8,128)(2,1)} %w_in_ref.1, bf16[1,512,512]{2,1,0:T(8,128)(2,1)} %w_out_ref.1, ...), custom_call_target="tpu_custom_call" | custom-call | tf_op jit(solution)/shard_map/packing/pallas_call | solution.py:381
  4.2 4.8 %collective-permute-start = (bf16[272,2560]{1,0:T(8,128)(2,1)}, bf16[272,2560]{1,0:T(8,128)(2,1)S(1)}, u32[]{:S(2)}, u32[]{:S(2)}) collective-permute-start(bf16[272,2560]{1,0:T(8,128)(2,1)} %get-tuple-element.24.first), channel_id=1, source_target_pairs={{0,384},{128,0},{256,128},{384,256},{1,129},{129,257},{257,385},{3... | collective-permute-start | bytes 4177928 | tf_op jit(solution)/shard_map/section_weights/ppermute | solution.py:405
  9.0 2.7 %collective-permute-start.2 = (bf16[256,2560]{1,0:T(8,128)(2,1)}, bf16[256,2560]{1,0:T(8,128)(2,1)}, u32[]{:S(2)}, u32[]{:S(2)}) collective-permute-start(bf16[256,2560]{1,0:T(8,128)(2,1)} %get-tuple-element.28.second), channel_id=1, source_target_pairs={{0,384},{128,0},{256,128},{384,256},{1,129},{129,257},{257,385},{3... | collective-permute-start | bytes 3932168 | tf_op jit(solution)/shard_map/section_weights/ppermute | solution.py:406
  11.8 17.4 %all-to-all-start = ((bf16[128,2,640]{2,1,0:T(2,128)(2,1)}), bf16[128,2,640]{2,1,0:T(2,128)(2,1)S(1)}, u32[]{:S(2)}, u32[]{:S(2)}) async-start(bf16[128,2,640]{2,1,0:T(2,128)(2,1)} %get-tuple-element.26), calls=%async_computation | async-start | bytes 655360 | tf_op jit(solution)/shard_map/routing/all_to_all | solution.py:412
  29.2 7.6 %collective-permute-start.1 = (bf16[64,512]{1,0:T(8,128)(2,1)}, bf16[64,512]{1,0:T(8,128)(2,1)S(1)}, u32[]{:S(2)}, u32[]{:S(2)}) collective-permute-start(bf16[64,512]{1,0:T(8,128)(2,1)} %get-tuple-element.25), channel_id=1, source_target_pairs={{0,64},{16,80},{32,96},{48,112},{64,0},{80,16},{96,32},{112,48},{1... | collective-permute-start | bytes 196616 | tf_op jit(solution)/shard_map/events/ppermute | solution.py:409
  36.8 7.9 %collective-permute-done.1.other_ref = bf16[64,512]{1,0:T(8,128)(2,1)S(1)} collective-permute-done((bf16[64,512]{1,0:T(8,128)(2,1)}, bf16[64,512]{1,0:T(8,128)(2,1)S(1)}, u32[]{:S(2)}, u32[]{:S(2)}) %collective-permute-start.1) | collective-permute-done | bytes 65568 | tf_op jit(solution)/shard_map/events/ppermute | solution.py:409
  44.7 0.5 all-to-all-done
  45.2 1.9 %collective-permute-start.4 = (bf16[272,2560]{1,0:T(8,128)(2,1)S(1)}, bf16[272,2560]{1,0:T(8,128)(2,1)S(1)}, u32[]{:S(2)}, u32[]{:S(2)}) collective-permute-start(bf16[272,2560]{1,0:T(8,128)(2,1)S(1)} %collective-permute-done.near_a), channel_id=1, source_target_pairs={{0,1},{1,0},{2,3},{3,2},{4,5},{5,4},{6,7},{7,6},{8,9},{9,8},{10,11... | collective-permute-start | bytes 4177928 | tf_op jit(solution)/shard_map/section_weights/ppermute | solution.py:419
  47.2 2.4 %collective-permute-start.3 = (bf16[272,2560]{1,0:T(8,128)(2,1)S(1)}, bf16[272,2560]{1,0:T(8,128)(2,1)S(1)}, u32[]{:S(2)}, u32[]{:S(2)}) collective-permute-start(bf16[272,2560]{1,0:T(8,128)(2,1)S(1)} %collective-permute-done.near_a), channel_id=1, source_target_pairs={{0,384},{128,0},{256,128},{384,256},{1,129},{129,257},{257,385},{3... | collective-permute-start | bytes 4177928 | tf_op jit(solution)/shard_map/section_weights/ppermute | solution.py:418
  49.6 2.8 %collective-permute-start.5 = (bf16[256,2560]{1,0:T(8,128)(2,1)}, bf16[256,2560]{1,0:T(8,128)(2,1)S(1)}, u32[]{:S(2)}, u32[]{:S(2)}) collective-permute-start(bf16[256,2560]{1,0:T(8,128)(2,1)} %collective-permute-done.2.near_b), channel_id=1, source_target_pairs={{0,1},{1,0},{2,3},{3,2},{4,5},{5,4},{6,7},{7,6},{8,9},{9,8},{10,11... | collective-permute-start | bytes 3932168 | tf_op jit(solution)/shard_map/section_weights/ppermute | solution.py:420
  52.5 1.0 routing.1
  53.4 14.2 %all_to_all.20.cot_ref = bf16[4,16,128]{2,1,0:T(8,128)(2,1)S(1)} all-to-all(bf16[4,16,128]{2,1,0:T(8,128)(2,1)S(1)} %get-tuple-element.34), channel_id=1, replica_groups=mesh['segment'=4,'z'=8,'y'=8,'core'=2] {'segment'}, dimensions={0} | all-to-all | bytes 32768 | tf_op jit(solution)/shard_map/routing/all_to_all | solution.py:431
  67.7 2.5 %collective-permute-start.6 = (bf16[272,2560]{1,0:T(8,128)(2,1)S(1)}, bf16[272,2560]{1,0:T(8,128)(2,1)S(1)}, u32[]{:S(2)}, u32[]{:S(2)}) collective-permute-start(bf16[272,2560]{1,0:T(8,128)(2,1)S(1)} %collective-permute-done.3.far_a), channel_id=1, source_target_pairs={{0,1},{1,0},{2,3},{3,2},{4,5},{5,4},{6,7},{7,6},{8,9},{9,8},{10,11... | collective-permute-start | bytes 4177928 | tf_op jit(solution)/shard_map/section_weights/ppermute | solution.py:434
  70.2 2.8 %collective-permute-done.6.far_b = bf16[272,2560]{1,0:T(8,128)(2,1)S(1)} collective-permute-done((bf16[272,2560]{1,0:T(8,128)(2,1)S(1)}, bf16[272,2560]{1,0:T(8,128)(2,1)S(1)}, u32[]{:S(2)}, u32[]{:S(2)}) %collective-permute-start.6) | collective-permute-done | bytes 1392672 | tf_op jit(solution)/shard_map/section_weights/ppermute | solution.py:434
  73.0 1.3 copy-done.1
  74.3 15.6 %layers.1 = bf16[4,208,512]{2,1,0:T(8,128)(2,1)S(1)} custom-call(s32[4]{0:T(128)S(1)} %copy-done.3, bf16[4,64,512]{2,1,0:T(8,128)(2,1)S(1)} %copy-done.2, bf16[64,512]{1,0:T(8,128)(2,1)S(1)} %collective-permute-done.1.other_ref, s32[64,128]{1,0:T(8,128)S(1)} %get-tuple-element.31.count_ref, bf16[4,16,128]{2,1,0:T(8,128)(2,1)S(1)} %all_to_all.20.cot_ref, ...), custom_call_target="tpu_custom_call" | custom-call | tf_op jit(solution)/shard_map/layers/pallas_call | solution.py:437
  89.9 16.8 %all_to_all.21.got_ref = bf16[4,208,512]{2,1,0:T(8,128)(2,1)S(1)} all-to-all(bf16[4,208,512]{2,1,0:T(8,128)(2,1)S(1)} %layers.1), channel_id=1, replica_groups=mesh['segment'=4,'z'=8,'y'=8,'core'=2] {'segment'}, dimensions={0} | all-to-all | bytes 1703936 | tf_op jit(solution)/shard_map/section_exchange/all_to_all | solution.py:463
  106.7 1.3 weight_gradient.3
  108.0 1.9 %collective-permute-start.7 = (bf16[272,512]{1,0:T(8,128)(2,1)S(1)}, bf16[272,512]{1,0:T(8,128)(2,1)S(1)}, u32[]{:S(2)}, u32[]{:S(2)}) collective-permute-start(bf16[272,512]{1,0:T(8,128)(2,1)S(1)} %get-tuple-element.40.send_ref), channel_id=1, source_target_pairs={{0,1},{1,0},{2,3},{3,2},{4,5},{5,4},{6,7},{7,6},{8,9},{9,8},{10,11... | collective-permute-start | bytes 835592 | tf_op jit(solution)/shard_map/weight_gradient/ppermute | solution.py:473
  109.9 1.5 %collective-permute-done.7.got_ref = bf16[272,512]{1,0:T(8,128)(2,1)S(1)} collective-permute-done((bf16[272,512]{1,0:T(8,128)(2,1)S(1)}, bf16[272,512]{1,0:T(8,128)(2,1)S(1)}, u32[]{:S(2)}, u32[]{:S(2)}) %collective-permute-start.7) | collective-permute-done | bytes 278560 | tf_op jit(solution)/shard_map/weight_gradient/ppermute | solution.py:473
  111.4 0.3 weight_gradient.4
  111.9 27.7 %all_to_all.22 = bf16[64,6,512]{2,1,0:T(8,128)(2,1)S(1)} all-to-all(bf16[64,6,512]{2,1,0:T(8,128)(2,1)S(1)} %reshape.20), channel_id=1, replica_groups=mesh['segment'=4,'z'=8,'y'=8,'core'=2] {'z','y'}, dimensions={0} | all-to-all | bytes 786432 | tf_op jit(solution)/shard_map/weight_gradient/all_to_all | solution.py:478
  139.6 0.1 reshape.21.got_ref
  139.8 0.8 weight_gradient.5
  (14 shorter events, 0.2 us)
Async XLA Ops:
  4.2 68.8 %copy-start = (bf16[272,2560]{1,0:T(8,128)(2,1)S(1)}, bf16[272,2560]{1,0:T(8,128)(2,1)}, u32[]{:S(2)}) copy-start(bf16[272,2560]{1,0:T(8,128)(2,1)} %get-tuple-element.24.first) | copy-start | bytes 4177924
  4.2 68.8 %copy-start.2 = (bf16[4,64,512]{2,1,0:T(8,128)(2,1)S(1)}, bf16[4,64,512]{2,1,0:T(8,128)(2,1)}, u32[]{:S(2)}) copy-start(bf16[4,64,512]{2,1,0:T(8,128)(2,1)} %events_ref.3) | copy-start | bytes 786436
  4.2 68.7 %copy-start.3 = (s32[4]{0:T(128)S(1)}, s32[4]{0:T(128)}, u32[]{:S(2)}) copy-start(s32[4]{0:T(128)} %plan_ref.3) | copy-start | bytes 52
  4.2 41.0 %collective-permute-start = (bf16[272,2560]{1,0:T(8,128)(2,1)}, bf16[272,2560]{1,0:T(8,128)(2,1)S(1)}, u32[]{:S(2)}, u32[]{:S(2)}) collective-permute-start(bf16[272,2560]{1,0:T(8,128)(2,1)} %get-tuple-element.24.first), channel_id=1, source_target_pairs={{0,384},{128,0},{256,128},{384,256},{1,129},{129,257},{257,385},{3... | collective-permute-start | bytes 4177928 | tf_op jit(solution)/shard_map/section_weights/ppermute | solution.py:405
  9.0 40.6 %collective-permute-start.2 = (bf16[256,2560]{1,0:T(8,128)(2,1)}, bf16[256,2560]{1,0:T(8,128)(2,1)}, u32[]{:S(2)}, u32[]{:S(2)}) collective-permute-start(bf16[256,2560]{1,0:T(8,128)(2,1)} %get-tuple-element.28.second), channel_id=1, source_target_pairs={{0,384},{128,0},{256,128},{384,256},{1,129},{129,257},{257,385},{3... | collective-permute-start | bytes 3932168 | tf_op jit(solution)/shard_map/section_weights/ppermute | solution.py:406
  11.8 33.4 %all-to-all-start = ((bf16[128,2,640]{2,1,0:T(2,128)(2,1)}), bf16[128,2,640]{2,1,0:T(2,128)(2,1)S(1)}, u32[]{:S(2)}, u32[]{:S(2)}) async-start(bf16[128,2,640]{2,1,0:T(2,128)(2,1)} %get-tuple-element.26), calls=%async_computation | async-start | bytes 655360 | tf_op jit(solution)/shard_map/routing/all_to_all | solution.py:412
  29.2 15.5 %collective-permute-start.1 = (bf16[64,512]{1,0:T(8,128)(2,1)}, bf16[64,512]{1,0:T(8,128)(2,1)S(1)}, u32[]{:S(2)}, u32[]{:S(2)}) collective-permute-start(bf16[64,512]{1,0:T(8,128)(2,1)} %get-tuple-element.25), channel_id=1, source_target_pairs={{0,64},{16,80},{32,96},{48,112},{64,0},{80,16},{96,32},{112,48},{1... | collective-permute-start | bytes 196616 | tf_op jit(solution)/shard_map/events/ppermute | solution.py:409
  45.2 22.4 %collective-permute-start.4 = (bf16[272,2560]{1,0:T(8,128)(2,1)S(1)}, bf16[272,2560]{1,0:T(8,128)(2,1)S(1)}, u32[]{:S(2)}, u32[]{:S(2)}) collective-permute-start(bf16[272,2560]{1,0:T(8,128)(2,1)S(1)} %collective-permute-done.near_a), channel_id=1, source_target_pairs={{0,1},{1,0},{2,3},{3,2},{4,5},{5,4},{6,7},{7,6},{8,9},{9,8},{10,11... | collective-permute-start | bytes 4177928 | tf_op jit(solution)/shard_map/section_weights/ppermute | solution.py:419
  47.2 20.5 %collective-permute-start.3 = (bf16[272,2560]{1,0:T(8,128)(2,1)S(1)}, bf16[272,2560]{1,0:T(8,128)(2,1)S(1)}, u32[]{:S(2)}, u32[]{:S(2)}) collective-permute-start(bf16[272,2560]{1,0:T(8,128)(2,1)S(1)} %collective-permute-done.near_a), channel_id=1, source_target_pairs={{0,384},{128,0},{256,128},{384,256},{1,129},{129,257},{257,385},{3... | collective-permute-start | bytes 4177928 | tf_op jit(solution)/shard_map/section_weights/ppermute | solution.py:418
  49.6 18.1 %collective-permute-start.5 = (bf16[256,2560]{1,0:T(8,128)(2,1)}, bf16[256,2560]{1,0:T(8,128)(2,1)S(1)}, u32[]{:S(2)}, u32[]{:S(2)}) collective-permute-start(bf16[256,2560]{1,0:T(8,128)(2,1)} %collective-permute-done.2.near_b), channel_id=1, source_target_pairs={{0,1},{1,0},{2,3},{3,2},{4,5},{5,4},{6,7},{7,6},{8,9},{9,8},{10,11... | collective-permute-start | bytes 3932168 | tf_op jit(solution)/shard_map/section_weights/ppermute | solution.py:420
  67.7 5.3 %collective-permute-start.6 = (bf16[272,2560]{1,0:T(8,128)(2,1)S(1)}, bf16[272,2560]{1,0:T(8,128)(2,1)S(1)}, u32[]{:S(2)}, u32[]{:S(2)}) collective-permute-start(bf16[272,2560]{1,0:T(8,128)(2,1)S(1)} %collective-permute-done.3.far_a), channel_id=1, source_target_pairs={{0,1},{1,0},{2,3},{3,2},{4,5},{5,4},{6,7},{7,6},{8,9},{9,8},{10,11... | collective-permute-start | bytes 4177928 | tf_op jit(solution)/shard_map/section_weights/ppermute | solution.py:434
  73.0 1.3 copy-start.1
  108.0 3.4 %collective-permute-start.7 = (bf16[272,512]{1,0:T(8,128)(2,1)S(1)}, bf16[272,512]{1,0:T(8,128)(2,1)S(1)}, u32[]{:S(2)}, u32[]{:S(2)}) collective-permute-start(bf16[272,512]{1,0:T(8,128)(2,1)S(1)} %get-tuple-element.40.send_ref), channel_id=1, source_target_pairs={{0,1},{1,0},{2,3},{3,2},{4,5},{5,4},{6,7},{7,6},{8,9},{9,8},{10,11... | collective-permute-start | bytes 835592 | tf_op jit(solution)/shard_map/weight_gradient/ppermute | solution.py:473

commit v6 on v5

--- a/solution.py
+++ b/solution.py
@@ -14,7 +14,8 @@
 ROWS = 64
 WIDTH = 512
 HEAD_COLS = 64
-PAIRS = 4
+GROUP = 256
+GROUPS = WIDTH // GROUP
 LAYERS = 4
 SLOTS = 8
 MSG = 208
@@ -109,13 +110,7 @@
         c.wait()
 
 
-def whole_part(a, d):
-    if d & (d - 1) == 0:
-        return a // d
-    return jnp.floor((a.astype(F32) + 0.5) * (1.0 / d)).astype(jnp.int32)
-
-
-def routing_kernel(block_rows, own_rows, table_ref, seeds_ref, hot_ref, count_ref):
+def routing_kernel(own_rows, table_ref, seeds_ref, hot_ref, count_ref):
     n_dp = table_ref.shape[0]
     hist = n_dp * DEV_HIST
     me = dp_place()
@@ -143,11 +138,11 @@
     hot = jnp.where(place_of == iota((16, hist), 0).astype(F32), hit, 0.0).astype(BF)
     total = hot_ref.shape[2]
     place, history = iota((hist, total), 1), iota((hist, total), 0)
-    chip = whole_part(place, block_rows)
-    within = place - chip * block_rows - own_rows
-    first = (chip * 2 + within) * DEV_HIST
-    valid = (within >= 0) & (within < 2)
+    chip = place // own_rows
+    within = place - chip * own_rows
+    first = (chip * 2 + within // 2) * DEV_HIST
     for h in range(DEV_HIST):
+        valid = (within < 4) & (within % 2 == h // 2)
         move = jnp.where(valid & (history == first + h), 1.0, 0.0).astype(BF)
         hot_ref[h] = mm(hot, move).astype(BF)
 
@@ -164,9 +159,9 @@
 
 def layers_kernel(
     plan_ref, events_ref, other_ref, count_ref, cot_ref,
-    first, second, near_a, near_b, swap_a, swap_b, far_a, far_b,
+    first, w_in_ref, w_out_ref, near_a, near_b, swap_a, swap_b, far_a, far_b,
     out_ref,
-    weights, tables, proj_s, dsilu_s, normed_s, rstd_s, norm_o_s, rstd_o_s, bias_s, att_s, datt_s, sems, table_sem,
+    weights, tables, proj_s, dsilu_s, normed_s, rstd_s, norm_o_s, rstd_o_s, att_s, datt_s, sems, table_sem,
 ):
     half = WIDTH // 2
     segment, core = lax.axis_index("segment"), lax.axis_index("core")
@@ -174,12 +169,20 @@
     swap = lax.rem(segment + 3 + 2 * core, LAYERS)
     far = lax.rem(segment + 2, LAYERS)
     held = (
-        (segment, first, core, second, 1 - core),
         (near, near_a, core, near_b, 1 - core),
         (swap, swap_a, 1 - core, swap_b, core),
         (far, far_a, core, far_b, 1 - core),
     )
     for l in range(LAYERS):
+
+        @pl.when(segment == l)
+        def _():
+            pltpu.make_async_copy(first.at[pl.ds(half, 16), pl.ds(0, 128)], tables.at[l], table_sem.at[l]).start()
+            for at in range(2):
+                rows = pl.ds(at * half, half)
+                for piece, cols in ((w_in_ref, pl.ds(0, 4 * WIDTH)), (w_out_ref, pl.ds(4 * WIDTH, WIDTH))):
+                    pltpu.make_async_copy(piece.at[0, rows], weights.at[l, rows, cols], sems.at[l, at]).start()
+
         for slot, one, side, two, other_side in held:
 
             @pl.when(slot == l)
@@ -191,21 +194,24 @@
                     rows = pl.ds(pl.multiple_of(at * half, half), half)
                     pltpu.make_async_copy(piece.at[pl.ds(0, half)], weights.at[l, rows], sems.at[l, at]).start()
 
-    lane, row = iota((ROWS, 128), 1), iota((ROWS, 128), 0)
-    left = (lane < HEAD_COLS).astype(F32)
-    left_b, right_b = left.astype(BF), (1.0 - left).astype(BF)
-    column = jnp.where(lane < HEAD_COLS, lane, lane - HEAD_COLS)
+    row, lane = iota((ROWS, GROUP), 0), iota((ROWS, GROUP), 1)
+    head = lane // HEAD_COLS
+    column = lane - head * HEAD_COLS
+    own_head = [(head == h).astype(F32).astype(BF) for h in range(GROUP // HEAD_COLS)]
     count = count_ref[...]
-    allowed = (column <= row) & (column < count)
+    allowed = (column <= row) & (column < count[:, 0:1])
 
     def block_diagonal(a):
-        return jnp.concatenate([a * left_b, a * right_b], axis=0)
+        return jnp.concatenate([a * mask for mask in own_head], axis=0)
 
     def merge(a):
-        return jnp.where(lane < HEAD_COLS, a[:ROWS], a[ROWS:])
-
-    def part(kind, p):
-        return pl.ds(kind * WIDTH + p * 128, 128)
+        total = a[:ROWS]
+        for h in range(1, GROUP // HEAD_COLS):
+            total = jnp.where(head == h, a[h * ROWS : (h + 1) * ROWS], total)
+        return total
+
+    def part(kind, g):
+        return pl.ds(kind * WIDTH + g * GROUP, GROUP)
 
     value = wanted_value()
     found = jnp.int32(0)
@@ -229,9 +235,10 @@
         pltpu.make_async_copy(tables.at[l], tables.at[l], table_sem.at[l]).wait()
         table = tables[l].astype(F32)
         table = table[0:4] + table[4:8] + table[8:12]
-        for p in range(PAIRS):
-            wide = jnp.broadcast_to(table[p : p + 1], (ROWS, 128))
-            bias_s[l, p] = pltpu.roll(wide, 0, 1, stride=1, stride_axis=0)
+        bias = []
+        for g in range(GROUPS):
+            tiles = [jnp.broadcast_to(table[p : p + 1], (ROWS, 128)) for p in (2 * g, 2 * g + 1)]
+            bias.append(jnp.concatenate([pltpu.roll(t, 0, 1, stride=1, stride_axis=0) for t in tiles], axis=1))
         normed_b = normed.astype(BF)
         for kind in range(4):
             cols = pl.ds(kind * WIDTH, WIDTH)
@@ -240,16 +247,17 @@
             silu = pre * gated
             proj_s[l, :, cols] = silu.astype(BF)
             dsilu_s[l, :, cols] = gated + silu * (1.0 - gated)
+        keys = [block_diagonal(proj_s[l, :, part(3, g)]) for g in range(GROUPS)]
+        values = [block_diagonal(proj_s[l, :, part(1, g)]) for g in range(GROUPS)]
+        scores = [mm(proj_s[l, :, part(2, g)], keys[g], NT) * 0.125 + bias[g] for g in range(GROUPS)]
         outs = []
-        for p in range(PAIRS):
-            keys = block_diagonal(proj_s[l, :, part(3, p)])
-            score = mm(proj_s[l, :, part(2, p)], keys, NT) * 0.125 + bias_s[l, p]
-            gated = sigmoid(score)
-            silu = score * gated
+        for g in range(GROUPS):
+            gated = sigmoid(scores[g])
+            silu = scores[g] * gated
             att = jnp.where(allowed, silu, 0.0).astype(BF)
-            att_s[l, p] = att
-            datt_s[l, p] = jnp.where(allowed, gated + silu * (1.0 - gated), 0.0) * 0.125
-            outs.append(mm(att, block_diagonal(proj_s[l, :, part(1, p)])))
+            att_s[l, g] = att
+            datt_s[l, g] = jnp.where(allowed, gated + silu * (1.0 - gated), 0.0) * 0.125
+            outs.append(mm(att, values[g]))
         mixed = jnp.concatenate(outs, axis=1)
         centred = mixed - row_mean(mixed)
         rstd = lax.rsqrt(row_mean(centred * centred) + 1e-6)
@@ -276,14 +284,12 @@
         d_norm = d_branch * proj_s[l, :, pl.ds(0, WIDTH)].astype(F32)
         d_mixed = rstd_o_s[l][:, 0:1] * (d_norm - row_mean(d_norm) - norm_o * row_mean(d_norm * norm_o))
         d_mixed = d_mixed.astype(BF)
-        d_value, d_query, d_key = [], [], []
-        for p in range(PAIRS):
-            d_out = d_mixed[:, 128 * p : 128 * p + 128]
-            d_att = mm(d_out, block_diagonal(proj_s[l, :, part(1, p)]), NT).astype(BF).astype(F32)
-            d_value.append(merge(mm(att_s[l, p], d_out, TN)))
-            d_score = (d_att * datt_s[l, p]).astype(BF)
-            d_query.append(mm(d_score, block_diagonal(proj_s[l, :, part(3, p)])))
-            d_key.append(merge(mm(d_score, proj_s[l, :, part(2, p)], TN)))
+        d_outs = [d_mixed[:, g * GROUP : (g + 1) * GROUP] for g in range(GROUPS)]
+        d_atts = [mm(d_outs[g], block_diagonal(proj_s[l, :, part(1, g)]), NT) for g in range(GROUPS)]
+        d_value = [merge(mm(att_s[l, g], d_outs[g], TN)) for g in range(GROUPS)]
+        d_scores = [(d_atts[g].astype(BF).astype(F32) * datt_s[l, g]).astype(BF) for g in range(GROUPS)]
+        d_query = [mm(d_scores[g], block_diagonal(proj_s[l, :, part(3, g)])) for g in range(GROUPS)]
+        d_key = [merge(mm(d_scores[g], proj_s[l, :, part(2, g)], TN)) for g in range(GROUPS)]
         d_normed = jnp.zeros((ROWS, WIDTH), F32)
         for kind, pieces in enumerate(([d_gate], d_value, d_query, d_key)):
             cols = pl.ds(kind * WIDTH, WIDTH)
@@ -316,38 +322,31 @@
     send_ref[half : half + 16, :] = jnp.concatenate(states, axis=1)
 
 
-def packing_kernel(block_rows, own_rows, keep_ref, send_ref, got_ref, out_ref):
+def packing_kernel(own_rows, keep_ref, send_ref, got_ref, out_ref):
     half = WIDTH // 2
     core = lax.axis_index("core")
-    total = (keep_ref[...] + got_ref[0:half, :].astype(F32)).astype(BF)
-    rows = out_ref.shape[0]
-    place, source = iota((rows, half), 0), iota((rows, half), 1)
-    chip = whole_part(place, block_rows)
-    within = place - chip * block_rows
-    pick = (within < own_rows) & (source == chip * own_rows + within)
-    laid = mm(pick.astype(F32).astype(BF), total)
     own = send_ref[half : half + 16, :].astype(F32)[0:1]
     other = got_ref[half : half + 16, :].astype(F32)[0:1]
     first = jnp.where(core == 0, own, other)
     second = jnp.where(core == 0, other, own)
-    place = iota((rows, WIDTH), 0)
-    at = place - whole_part(place, block_rows) * block_rows
-    laid = laid + jnp.where(at == own_rows, first, 0.0) + jnp.where(at == own_rows + 1, second, 0.0)
-    out_ref[...] = laid.astype(BF)
-
-
-def result_kernel(block_rows, got_ref, hot_ref, served_ref, weight_ref):
+    at = iota((half, half), 0) % own_rows
+    states = jnp.zeros((half, half), F32)
+    for r, quarter in enumerate((first[:, :half], first[:, half:], second[:, :half], second[:, half:])):
+        states = jnp.where(at == r, quarter, states)
+    out_ref[:, 0:WIDTH] = (keep_ref[...] + got_ref[0:half, :].astype(F32)).astype(BF)
+    out_ref[:, WIDTH : WIDTH + half] = states.astype(BF)
+
+
+def result_kernel(got_ref, hot_ref, served_ref, weight_ref):
     rows = got_ref.shape[0]
-    out_rows = weight_ref.shape[0]
-    lead = max(16, out_rows)
-    place = iota((lead, rows), 1)
-    within = place - whole_part(place, block_rows) * block_rows
-    pick = ((within == iota((lead, rows), 0)) & (within < out_rows)).astype(F32).astype(BF)
-    got = got_ref[...]
-    weight_ref[...] = mm(pick, got)[0:out_rows]
+    own_rows = weight_ref.shape[0]
+    lead = max(16, own_rows)
+    pick = (iota((lead, rows), 1) % own_rows == iota((lead, rows), 0)).astype(F32).astype(BF)
+    weight_ref[...] = mm(pick, got_ref[:, 0:WIDTH])[0:own_rows]
     served = jnp.zeros((16, 128), F32)
     for h in range(DEV_HIST):
-        served = served + mm(hot_ref[h], got[:, 128 * h : 128 * h + 128])
+        at = WIDTH + 128 * (h % 2)
+        served = served + mm(hot_ref[h], got_ref[:, at : at + 128])
     served_ref[...] = served[0:SLOTS].astype(BF)
 
 
@@ -372,7 +371,6 @@
     n_dp = n_z * n_y * n_core
     chips = n_z * n_y
     own_rows = WIDTH // n_dp
-    block_rows = own_rows + 2
     half = WIDTH // 2
 
     any_spec, vmem = pl.BlockSpec(memory_space=pl.ANY), pl.BlockSpec(memory_space=pltpu.VMEM)
@@ -421,10 +419,10 @@
 
     with jax.named_scope("routing"):
         seeds, hot, count = call(
-            functools.partial(routing_kernel, block_rows, own_rows),
+            functools.partial(routing_kernel, own_rows),
             (
                 shape((LAYERS, 16, 128), BF),
-                shape((DEV_HIST, 16, chips * block_rows), BF),
+                shape((DEV_HIST, 16, half), BF),
                 shape((ROWS, 128), jnp.int32),
             ),
         )(facts)
@@ -446,17 +444,16 @@
                 pltpu.VMEM((LAYERS, ROWS, 128), F32),
                 pltpu.VMEM((LAYERS, ROWS, WIDTH), F32),
                 pltpu.VMEM((LAYERS, ROWS, 128), F32),
-                pltpu.VMEM((LAYERS, PAIRS, ROWS, 128), F32),
-                pltpu.VMEM((LAYERS, PAIRS, ROWS, 128), BF),
-                pltpu.VMEM((LAYERS, PAIRS, ROWS, 128), F32),
+                pltpu.VMEM((LAYERS, GROUPS, ROWS, GROUP), BF),
+                pltpu.VMEM((LAYERS, GROUPS, ROWS, GROUP), F32),
                 pltpu.SemaphoreType.DMA((LAYERS, 2)),
                 pltpu.SemaphoreType.DMA((LAYERS,)),
             ],
-            in_specs=[smem] + [vmem] * 4 + [any_spec] * 8,
+            in_specs=[smem] + [vmem] * 4 + [any_spec] * 9,
             limit=28,
         )(
             balance_plan, events, other_events, count, seeds,
-            first, second, near_a, near_b, swap_a, swap_b, far_a, far_b,
+            first, w_uvqk, w_out, near_a, near_b, swap_a, swap_b, far_a, far_b,
         )
 
     with jax.named_scope("section_exchange"):
@@ -472,16 +469,15 @@
         )(arrived)
         partner = lax.ppermute(send, "core", swap)
         blocks = call(
-            functools.partial(packing_kernel, block_rows, own_rows),
-            shape((chips * block_rows, WIDTH), BF),
+            functools.partial(packing_kernel, own_rows),
+            shape((half, WIDTH + half), BF),
         )(keep, send, partner)
-        blocks = lax.all_to_all(
-            blocks.reshape(chips, block_rows, WIDTH), ("z", "y"), 0, 0, tiled=True
-        )
+        blocks = blocks.reshape(chips, own_rows, WIDTH + half)
+        blocks = lax.all_to_all(blocks, ("z", "y"), 0, 0, tiled=True)
         served, weight = call(
-            functools.partial(result_kernel, block_rows),
+            result_kernel,
             (shape((SLOTS, 128), BF), shape((own_rows, WIDTH), F32)),
-        )(blocks.reshape(chips * block_rows, WIDTH), hot)
+        )(blocks.reshape(half, WIDTH + half), hot)
     return served[None], grads[None], weight[None]
 
 

time: 141 us -> 136 us (0.965)
  Pallas kernels: 22.5 us -> 19 us
  blocking collectives: 58.8 us -> 56.9 us
    pallas_call x1, Pallas kernels: 15.6 us -> 12.3 us  [body(): call(layers_kernel, shape((LAYERS, MSG, WIDTH), BF), scratch=[pltpu.VMEM(...]
    all_to_all x1, blocking collectives: 27.7 us -> 25.3 us  [body(): blocks = lax.all_to_all(blocks, ('z', 'y'), 0, 0, tiled=True)]
where the time goes in v6:
time: 136 us; the launch traced here: 135 us
  blocking collectives  56.9 us (42%)
  starting transfers between devices  44.1 us (32%)
  Pallas kernels  19 us (14%)
  waiting for transfers between devices  12.7 us (9%)
  local copies, waits for them, and re-layouts  1.59 us (1%)
    all_to_all x1, blocking collectives, body(): blocks = lax.all_to_all(blocks, ('z', 'y'), 0, 0, tiled=True)  25.3 us
    all_to_all x1, starting transfers between devices, body(): facts = lax.all_to_all(facts, DP, 0, 0, tiled=True)  17.4 us
    all_to_all x1, blocking collectives, body(): arrived = lax.all_to_all(message, 'segment', 0, 0, tiled=True)  16.8 us
    all_to_all x1, blocking collectives, body(): seeds = lax.all_to_all(seeds, 'segment', 0, 0, tiled=True)  14.7 us
    pallas_call x1, Pallas kernels, body(): call(layers_kernel, shape((LAYERS, MSG, WIDTH), BF), scratch=[pltpu.VMEM(...  12.3 us
    ppermute x1, waiting for transfers between devices, body(): lax.ppermute(outgoing, 'z', [(i, (i + n_z // 2) % n_z) for i in range(n_z)])  7.92 us
    ppermute x1, starting transfers between devices, body(): lax.ppermute(outgoing, 'z', [(i, (i + n_z // 2) % n_z) for i in range(n_z)])  7.61 us
    ppermute x1, starting transfers between devices, body(): near_a = lax.ppermute(first, ('segment', 'core'), ring)  4.8 us
  transfers between devices with their start and end apart: 9, of which 4 were waited for; matrix products, arithmetic and copies ran while one was open for 0% of the time, Pallas kernels for 1%

profile of v6, /device:TPU:8, one launch (start us, length us, event | category | flops | bytes accessed | tf_op | source)
XLA Modules:
  0.0 135.0 jit_solution(2060993104728268067)
XLA Ops:
  0.6 3.7 %packing.1 = (bf16[272,2560]{1,0:T(8,128)(2,1)}, bf16[256,2560]{1,0:T(8,128)(2,1)}, bf16[64,512]{1,0:T(8,128)(2,1)}, bf16[128,2,640]{2,1,0:T(2,128)(2,1)}) custom-call(s32[4]{0:T(128)} %plan_ref.3, s32[4]{0:T(128)} %bitcast.8, s32[4]{0:T(128)} %lengths_ref.1, bf16[1,512,2048]{2,1,0:T(8,128)(2,1)} %w_in_ref.3, bf16[1,512,512]{2,1,0:T(8,128)(2,1)} %w_out_ref.3, ...), custom_call_target="tpu_custom_call" | custom-call | tf_op jit(solution)/shard_map/packing/pallas_call | solution.py:379
  4.4 4.8 %collective-permute-start = (bf16[272,2560]{1,0:T(8,128)(2,1)}, bf16[272,2560]{1,0:T(8,128)(2,1)}, u32[]{:S(2)}, u32[]{:S(2)}) collective-permute-start(bf16[272,2560]{1,0:T(8,128)(2,1)} %get-tuple-element.24.first), channel_id=1, source_target_pairs={{0,384},{128,0},{256,128},{384,256},{1,129},{129,257},{257,385},{3... | collective-permute-start | bytes 4177928 | tf_op jit(solution)/shard_map/section_weights/ppermute | solution.py:403
  9.2 2.7 %collective-permute-start.2 = (bf16[256,2560]{1,0:T(8,128)(2,1)}, bf16[256,2560]{1,0:T(8,128)(2,1)}, u32[]{:S(2)}, u32[]{:S(2)}) collective-permute-start(bf16[256,2560]{1,0:T(8,128)(2,1)} %get-tuple-element.28), channel_id=1, source_target_pairs={{0,384},{128,0},{256,128},{384,256},{1,129},{129,257},{257,385},{3... | collective-permute-start | bytes 3932168 | tf_op jit(solution)/shard_map/section_weights/ppermute | solution.py:404
  12.0 17.4 %all-to-all-start = ((bf16[128,2,640]{2,1,0:T(2,128)(2,1)}), bf16[128,2,640]{2,1,0:T(2,128)(2,1)S(1)}, u32[]{:S(2)}, u32[]{:S(2)}) async-start(bf16[128,2,640]{2,1,0:T(2,128)(2,1)} %get-tuple-element.26), calls=%async_computation | async-start | bytes 655360 | tf_op jit(solution)/shard_map/routing/all_to_all | solution.py:410
  29.4 7.6 %collective-permute-start.1 = (bf16[64,512]{1,0:T(8,128)(2,1)}, bf16[64,512]{1,0:T(8,128)(2,1)S(1)}, u32[]{:S(2)}, u32[]{:S(2)}) collective-permute-start(bf16[64,512]{1,0:T(8,128)(2,1)} %get-tuple-element.25), channel_id=1, source_target_pairs={{0,64},{16,80},{32,96},{48,112},{64,0},{80,16},{96,32},{112,48},{1... | collective-permute-start | bytes 196616 | tf_op jit(solution)/shard_map/events/ppermute | solution.py:407
  37.0 7.9 %collective-permute-done.1.other_ref = bf16[64,512]{1,0:T(8,128)(2,1)S(1)} collective-permute-done((bf16[64,512]{1,0:T(8,128)(2,1)}, bf16[64,512]{1,0:T(8,128)(2,1)S(1)}, u32[]{:S(2)}, u32[]{:S(2)}) %collective-permute-start.1) | collective-permute-done | bytes 65568 | tf_op jit(solution)/shard_map/events/ppermute | solution.py:407
  44.9 0.5 all-to-all-done
  45.4 1.9 %collective-permute-start.4 = (bf16[272,2560]{1,0:T(8,128)(2,1)}, bf16[272,2560]{1,0:T(8,128)(2,1)S(1)}, u32[]{:S(2)}, u32[]{:S(2)}) collective-permute-start(bf16[272,2560]{1,0:T(8,128)(2,1)} %collective-permute-done.near_a), channel_id=1, source_target_pairs={{0,1},{1,0},{2,3},{3,2},{4,5},{5,4},{6,7},{7,6},{8,9},{9,8},{10,11... | collective-permute-start | bytes 4177928 | tf_op jit(solution)/shard_map/section_weights/ppermute | solution.py:417
  47.4 2.4 %collective-permute-start.3 = (bf16[272,2560]{1,0:T(8,128)(2,1)}, bf16[272,2560]{1,0:T(8,128)(2,1)S(1)}, u32[]{:S(2)}, u32[]{:S(2)}) collective-permute-start(bf16[272,2560]{1,0:T(8,128)(2,1)} %collective-permute-done.near_a), channel_id=1, source_target_pairs={{0,384},{128,0},{256,128},{384,256},{1,129},{129,257},{257,385},{3... | collective-permute-start | bytes 4177928 | tf_op jit(solution)/shard_map/section_weights/ppermute | solution.py:416
  49.8 2.8 %collective-permute-start.5 = (bf16[256,2560]{1,0:T(8,128)(2,1)}, bf16[256,2560]{1,0:T(8,128)(2,1)S(1)}, u32[]{:S(2)}, u32[]{:S(2)}) collective-permute-start(bf16[256,2560]{1,0:T(8,128)(2,1)} %collective-permute-done.2.near_b), channel_id=1, source_target_pairs={{0,1},{1,0},{2,3},{3,2},{4,5},{5,4},{6,7},{7,6},{8,9},{9,8},{10,11... | collective-permute-start | bytes 3932168 | tf_op jit(solution)/shard_map/section_weights/ppermute | solution.py:418
  52.7 0.7 routing.1
  53.4 14.7 %all_to_all.20.cot_ref = bf16[4,16,128]{2,1,0:T(8,128)(2,1)S(1)} all-to-all(bf16[4,16,128]{2,1,0:T(8,128)(2,1)S(1)} %get-tuple-element.34), channel_id=1, replica_groups=mesh['segment'=4,'z'=8,'y'=8,'core'=2] {'segment'}, dimensions={0} | all-to-all | bytes 32768 | tf_op jit(solution)/shard_map/routing/all_to_all | solution.py:429
  68.1 2.5 %collective-permute-start.6 = (bf16[272,2560]{1,0:T(8,128)(2,1)S(1)}, bf16[272,2560]{1,0:T(8,128)(2,1)S(1)}, u32[]{:S(2)}, u32[]{:S(2)}) collective-permute-start(bf16[272,2560]{1,0:T(8,128)(2,1)S(1)} %collective-permute-done.3.far_a), channel_id=1, source_target_pairs={{0,1},{1,0},{2,3},{3,2},{4,5},{5,4},{6,7},{7,6},{8,9},{9,8},{10,11... | collective-permute-start | bytes 4177928 | tf_op jit(solution)/shard_map/section_weights/ppermute | solution.py:432
  70.6 2.8 %collective-permute-done.6.far_b = bf16[272,2560]{1,0:T(8,128)(2,1)S(1)} collective-permute-done((bf16[272,2560]{1,0:T(8,128)(2,1)S(1)}, bf16[272,2560]{1,0:T(8,128)(2,1)S(1)}, u32[]{:S(2)}, u32[]{:S(2)}) %collective-permute-start.6) | collective-permute-done | bytes 1392672 | tf_op jit(solution)/shard_map/section_weights/ppermute | solution.py:432
  73.4 1.3 copy-done.2
  74.7 12.3 %layers.1 = bf16[4,208,512]{2,1,0:T(8,128)(2,1)S(1)} custom-call(s32[4]{0:T(128)S(1)} %copy-done.4, bf16[4,64,512]{2,1,0:T(8,128)(2,1)S(1)} %copy-done.3, bf16[64,512]{1,0:T(8,128)(2,1)S(1)} %collective-permute-done.1.other_ref, s32[64,128]{1,0:T(8,128)S(1)} %get-tuple-element.31.count_ref, bf16[4,16,128]{2,1,0:T(8,128)(2,1)S(1)} %all_to_all.20.cot_ref, ...), custom_call_target="tpu_custom_call" | custom-call | tf_op jit(solution)/shard_map/layers/pallas_call | solution.py:435
  87.1 16.8 %all_to_all.21.got_ref = bf16[4,208,512]{2,1,0:T(8,128)(2,1)S(1)} all-to-all(bf16[4,208,512]{2,1,0:T(8,128)(2,1)S(1)} %layers.1), channel_id=1, replica_groups=mesh['segment'=4,'z'=8,'y'=8,'core'=2] {'segment'}, dimensions={0} | all-to-all | bytes 1703936 | tf_op jit(solution)/shard_map/section_exchange/all_to_all | solution.py:460
  103.9 1.3 weight_gradient.3
  105.2 1.9 %collective-permute-start.7 = (bf16[272,512]{1,0:T(8,128)(2,1)S(1)}, bf16[272,512]{1,0:T(8,128)(2,1)S(1)}, u32[]{:S(2)}, u32[]{:S(2)}) collective-permute-start(bf16[272,512]{1,0:T(8,128)(2,1)S(1)} %get-tuple-element.40.send_ref), channel_id=1, source_target_pairs={{0,1},{1,0},{2,3},{3,2},{4,5},{5,4},{6,7},{7,6},{8,9},{9,8},{10,11... | collective-permute-start | bytes 835592 | tf_op jit(solution)/shard_map/weight_gradient/ppermute | solution.py:470
  107.1 1.5 %collective-permute-done.7.got_ref = bf16[272,512]{1,0:T(8,128)(2,1)S(1)} collective-permute-done((bf16[272,512]{1,0:T(8,128)(2,1)S(1)}, bf16[272,512]{1,0:T(8,128)(2,1)S(1)}, u32[]{:S(2)}, u32[]{:S(2)}) %collective-permute-start.7) | collective-permute-done | bytes 278560 | tf_op jit(solution)/shard_map/weight_gradient/ppermute | solution.py:470
  108.6 0.1 weight_gradient.4
  108.7 0.1 reshape.20
  108.8 25.3 %all_to_all.22 = bf16[64,4,768]{2,1,0:T(4,128)(2,1)S(1)} all-to-all(bf16[64,4,768]{2,1,0:T(4,128)(2,1)S(1)} %reshape.20), channel_id=1, replica_groups=mesh['segment'=4,'z'=8,'y'=8,'core'=2] {'z','y'}, dimensions={0} | all-to-all | bytes 786432 | tf_op jit(solution)/shard_map/weight_gradient/all_to_all | solution.py:476
  134.3 0.8 weight_gradient.5
  (16 shorter events, 0.2 us)
Async XLA Ops:
  0.6 72.7 %copy-start = (bf16[1,512,2048]{2,1,0:T(8,128)(2,1)S(1)}, bf16[1,512,2048]{2,1,0:T(8,128)(2,1)}, u32[]{:S(2)}) copy-start(bf16[1,512,2048]{2,1,0:T(8,128)(2,1)} %w_in_ref.3) | copy-start | bytes 6291460
  4.4 69.0 %copy-start.1 = (bf16[1,512,512]{2,1,0:T(8,128)(2,1)S(1)}, bf16[1,512,512]{2,1,0:T(8,128)(2,1)}, u32[]{:S(2)}) copy-start(bf16[1,512,512]{2,1,0:T(8,128)(2,1)} %w_out_ref.3) | copy-start | bytes 1572868
  4.4 69.0 %copy-start.3 = (bf16[4,64,512]{2,1,0:T(8,128)(2,1)S(1)}, bf16[4,64,512]{2,1,0:T(8,128)(2,1)}, u32[]{:S(2)}) copy-start(bf16[4,64,512]{2,1,0:T(8,128)(2,1)} %events_ref.3) | copy-start | bytes 786436
  4.4 69.0 %copy-start.4 = (s32[4]{0:T(128)S(1)}, s32[4]{0:T(128)}, u32[]{:S(2)}) copy-start(s32[4]{0:T(128)} %plan_ref.3) | copy-start | bytes 52
  4.4 41.0 %collective-permute-start = (bf16[272,2560]{1,0:T(8,128)(2,1)}, bf16[272,2560]{1,0:T(8,128)(2,1)}, u32[]{:S(2)}, u32[]{:S(2)}) collective-permute-start(bf16[272,2560]{1,0:T(8,128)(2,1)} %get-tuple-element.24.first), channel_id=1, source_target_pairs={{0,384},{128,0},{256,128},{384,256},{1,129},{129,257},{257,385},{3... | collective-permute-start | bytes 4177928 | tf_op jit(solution)/shard_map/section_weights/ppermute | solution.py:403
  9.2 40.6 %collective-permute-start.2 = (bf16[256,2560]{1,0:T(8,128)(2,1)}, bf16[256,2560]{1,0:T(8,128)(2,1)}, u32[]{:S(2)}, u32[]{:S(2)}) collective-permute-start(bf16[256,2560]{1,0:T(8,128)(2,1)} %get-tuple-element.28), channel_id=1, source_target_pairs={{0,384},{128,0},{256,128},{384,256},{1,129},{129,257},{257,385},{3... | collective-permute-start | bytes 3932168 | tf_op jit(solution)/shard_map/section_weights/ppermute | solution.py:404
  12.0 33.4 %all-to-all-start = ((bf16[128,2,640]{2,1,0:T(2,128)(2,1)}), bf16[128,2,640]{2,1,0:T(2,128)(2,1)S(1)}, u32[]{:S(2)}, u32[]{:S(2)}) async-start(bf16[128,2,640]{2,1,0:T(2,128)(2,1)} %get-tuple-element.26), calls=%async_computation | async-start | bytes 655360 | tf_op jit(solution)/shard_map/routing/all_to_all | solution.py:410
  29.4 15.5 %collective-permute-start.1 = (bf16[64,512]{1,0:T(8,128)(2,1)}, bf16[64,512]{1,0:T(8,128)(2,1)S(1)}, u32[]{:S(2)}, u32[]{:S(2)}) collective-permute-start(bf16[64,512]{1,0:T(8,128)(2,1)} %get-tuple-element.25), channel_id=1, source_target_pairs={{0,64},{16,80},{32,96},{48,112},{64,0},{80,16},{96,32},{112,48},{1... | collective-permute-start | bytes 196616 | tf_op jit(solution)/shard_map/events/ppermute | solution.py:407
  45.4 22.6 %collective-permute-start.4 = (bf16[272,2560]{1,0:T(8,128)(2,1)}, bf16[272,2560]{1,0:T(8,128)(2,1)S(1)}, u32[]{:S(2)}, u32[]{:S(2)}) collective-permute-start(bf16[272,2560]{1,0:T(8,128)(2,1)} %collective-permute-done.near_a), channel_id=1, source_target_pairs={{0,1},{1,0},{2,3},{3,2},{4,5},{5,4},{6,7},{7,6},{8,9},{9,8},{10,11... | collective-permute-start | bytes 4177928 | tf_op jit(solution)/shard_map/section_weights/ppermute | solution.py:417
  47.4 20.7 %collective-permute-start.3 = (bf16[272,2560]{1,0:T(8,128)(2,1)}, bf16[272,2560]{1,0:T(8,128)(2,1)S(1)}, u32[]{:S(2)}, u32[]{:S(2)}) collective-permute-start(bf16[272,2560]{1,0:T(8,128)(2,1)} %collective-permute-done.near_a), channel_id=1, source_target_pairs={{0,384},{128,0},{256,128},{384,256},{1,129},{129,257},{257,385},{3... | collective-permute-start | bytes 4177928 | tf_op jit(solution)/shard_map/section_weights/ppermute | solution.py:416
  49.8 18.3 %collective-permute-start.5 = (bf16[256,2560]{1,0:T(8,128)(2,1)}, bf16[256,2560]{1,0:T(8,128)(2,1)S(1)}, u32[]{:S(2)}, u32[]{:S(2)}) collective-permute-start(bf16[256,2560]{1,0:T(8,128)(2,1)} %collective-permute-done.2.near_b), channel_id=1, source_target_pairs={{0,1},{1,0},{2,3},{3,2},{4,5},{5,4},{6,7},{7,6},{8,9},{9,8},{10,11... | collective-permute-start | bytes 3932168 | tf_op jit(solution)/shard_map/section_weights/ppermute | solution.py:418
  68.1 5.3 %collective-permute-start.6 = (bf16[272,2560]{1,0:T(8,128)(2,1)S(1)}, bf16[272,2560]{1,0:T(8,128)(2,1)S(1)}, u32[]{:S(2)}, u32[]{:S(2)}) collective-permute-start(bf16[272,2560]{1,0:T(8,128)(2,1)S(1)} %collective-permute-done.3.far_a), channel_id=1, source_target_pairs={{0,1},{1,0},{2,3},{3,2},{4,5},{5,4},{6,7},{7,6},{8,9},{9,8},{10,11... | collective-permute-start | bytes 4177928 | tf_op jit(solution)/shard_map/section_weights/ppermute | solution.py:432
  73.4 1.3 copy-start.2
  105.2 3.4 %collective-permute-start.7 = (bf16[272,512]{1,0:T(8,128)(2,1)S(1)}, bf16[272,512]{1,0:T(8,128)(2,1)S(1)}, u32[]{:S(2)}, u32[]{:S(2)}) collective-permute-start(bf16[272,512]{1,0:T(8,128)(2,1)S(1)} %get-tuple-element.40.send_ref), channel_id=1, source_target_pairs={{0,1},{1,0},{2,3},{3,2},{4,5},{5,4},{6,7},{7,6},{8,9},{9,8},{10,11... | collective-permute-start | bytes 835592 | tf_op jit(solution)/shard_map/weight_gradient/ppermute | solution.py:470

commit v7 on v6

--- a/solution.py
+++ b/solution.py
@@ -50,17 +50,9 @@
     return upper * DEV_HIST + lax.axis_index("segment")
 
 
-def packing_start(
-    plan_ref, routes_ref, lengths_ref, w_in_ref, w_out_ref, events_ref, bias_ref, cot_ref,
-    first_ref, second_ref, outgoing_ref, facts_ref,
-    plan, routes, lengths, bias_s, cot_s, sems,
-):
+def weights_kernel(w_in_ref, w_out_ref, first_ref, second_ref, sems):
     core = lax.axis_index("core")
     half = WIDTH // 2
-    small = [(plan_ref, plan), (routes_ref, routes), (lengths_ref, lengths), (bias_ref.at[0], bias_s), (cot_ref.at[0], cot_s)]
-    small = [pltpu.make_async_copy(*c, sems.at[n]) for n, c in enumerate(small)]
-    for c in small:
-        c.start()
     copies = []
     for side, dest in ((core, first_ref), (1 - core, second_ref)):
         for part in range(2):
@@ -68,19 +60,14 @@
             to = pl.ds(part * (half // 2), half // 2)
             copies.append((w_in_ref.at[0, rows], dest.at[to, pl.ds(0, 4 * WIDTH)]))
             copies.append((w_out_ref.at[0, rows], dest.at[to, pl.ds(4 * WIDTH, WIDTH)]))
-    copies = [pltpu.make_async_copy(*c, sems.at[len(small) + n]) for n, c in enumerate(copies)]
+    copies = [pltpu.make_async_copy(*c, sems.at[n]) for n, c in enumerate(copies)]
     for c in copies:
         c.start()
-    for c in small:
+    for c in copies:
         c.wait()
-    partner_value = DEV_HIST + 2 * lax.axis_index("segment") - wanted_value()
-    chosen = jnp.int32(0)
-    for h in range(DEV_HIST):
-        chosen = chosen + jnp.where(plan[h] == partner_value, h, 0)
-    copies.append(pltpu.make_async_copy(events_ref.at[chosen], outgoing_ref, sems.at[len(small) + len(copies)]))
-    copies[-1].start()
-
-    bias = bias_s[...]
+
+
+def bias_rows(bias):
     high = bias.astype(BF).astype(F32)
     middle = (bias - high).astype(BF).astype(F32)
     low = bias - high - middle
@@ -93,10 +80,25 @@
     distance, place = iota((ROWS, 128), 0), iota((ROWS, 128), 1)
     to_even = (place == (128 - distance) % 128).astype(F32).astype(BF)
     to_odd = (place == ROWS - distance).astype(F32).astype(BF)
-    base = mm(mm(pick_even, pieces).astype(BF), to_even) + mm(mm(pick_odd, pieces).astype(BF), to_odd)
-    first_ref[half : half + 16, 0:128] = base.astype(BF)
-    first_ref[half : half + 16, 128 : 5 * WIDTH] = jnp.zeros((16, 5 * WIDTH - 128), BF)
-
+    return mm(mm(pick_even, pieces).astype(BF), to_even) + mm(mm(pick_odd, pieces).astype(BF), to_odd)
+
+
+def facts_kernel(
+    plan_ref, routes_ref, lengths_ref, events_ref, cot_ref, outgoing_ref, facts_ref,
+    plan, routes, lengths, cot_s, sems,
+):
+    small = [(plan_ref, plan), (routes_ref, routes), (lengths_ref, lengths), (cot_ref.at[0], cot_s)]
+    small = [pltpu.make_async_copy(*c, sems.at[n]) for n, c in enumerate(small)]
+    for c in small:
+        c.start()
+    for c in small:
+        c.wait()
+    partner_value = DEV_HIST + 2 * lax.axis_index("segment") - wanted_value()
+    chosen = jnp.int32(0)
+    for h in range(DEV_HIST):
+        chosen = chosen + jnp.where(plan[h] == partner_value, h, 0)
+    copy = pltpu.make_async_copy(events_ref.at[chosen], outgoing_ref, sems.at[len(small)])
+    copy.start()
     lane = iota((1, 128), 1)
     facts = jnp.zeros((1, 128), F32)
     for j, ref in enumerate((routes, plan, lengths)):
@@ -106,11 +108,10 @@
     blocks = [cot[k : k + 1] for k in range(SLOTS)] + [facts, jnp.zeros((1, 128), F32)]
     lines = [jnp.concatenate(blocks[k : k + 5], axis=1) for k in (0, 5)]
     facts_ref[...] = jnp.broadcast_to(jnp.concatenate(lines).astype(BF)[None], facts_ref.shape)
-    for c in copies:
-        c.wait()
-
-
-def routing_kernel(own_rows, table_ref, seeds_ref, hot_ref, count_ref):
+    copy.wait()
+
+
+def routing_kernel(own_rows, table_ref, bias_ref, seeds_ref, hot_ref, count_ref):
     n_dp = table_ref.shape[0]
     hist = n_dp * DEV_HIST
     me = dp_place()
@@ -129,8 +130,10 @@
     for k in range(SLOTS):
         pick = jnp.where((source == route) & (slot == float(k)), 1.0, 0.0).astype(BF)
         seeds = seeds + mm(pick, table_ref[:, 128 * k : 128 * k + 128])
+    bias = bias_rows(bias_ref[0]).astype(BF)
     for q in range(LAYERS):
-        seeds_ref[q] = jnp.broadcast_to(seeds[q : q + 1], (16, 128)).astype(BF)
+        seeds_ref[q, 0:16, :] = jnp.broadcast_to(seeds[q : q + 1], (16, 128)).astype(BF)
+        seeds_ref[q, 16:32, :] = bias
 
     hit = jnp.broadcast_to((routes == me.astype(F32)).astype(F32), (16, hist))
     earlier = (iota((hist, hist), 0) < iota((hist, hist), 1)).astype(F32).astype(BF)
@@ -159,9 +162,9 @@
 
 def layers_kernel(
     plan_ref, events_ref, other_ref, count_ref, cot_ref,
-    first, w_in_ref, w_out_ref, near_a, near_b, swap_a, swap_b, far_a, far_b,
+    w_in_ref, w_out_ref, near_a, near_b, swap_a, swap_b, far_a, far_b,
     out_ref,
-    weights, tables, proj_s, dsilu_s, normed_s, rstd_s, norm_o_s, rstd_o_s, att_s, datt_s, sems, table_sem,
+    weights, proj_s, dsilu_s, normed_s, rstd_s, norm_o_s, rstd_o_s, att_s, datt_s, sems,
 ):
     half = WIDTH // 2
     segment, core = lax.axis_index("segment"), lax.axis_index("core")
@@ -177,7 +180,6 @@
 
         @pl.when(segment == l)
         def _():
-            pltpu.make_async_copy(first.at[pl.ds(half, 16), pl.ds(0, 128)], tables.at[l], table_sem.at[l]).start()
             for at in range(2):
                 rows = pl.ds(at * half, half)
                 for piece, cols in ((w_in_ref, pl.ds(0, 4 * WIDTH)), (w_out_ref, pl.ds(4 * WIDTH, WIDTH))):
@@ -187,12 +189,9 @@
 
             @pl.when(slot == l)
             def _():
-                pltpu.make_async_copy(
-                    one.at[pl.ds(half, 16), pl.ds(0, 128)], tables.at[l], table_sem.at[l]
-                ).start()
                 for piece, at in ((one, side), (two, other_side)):
                     rows = pl.ds(pl.multiple_of(at * half, half), half)
-                    pltpu.make_async_copy(piece.at[pl.ds(0, half)], weights.at[l, rows], sems.at[l, at]).start()
+                    pltpu.make_async_copy(piece, weights.at[l, rows], sems.at[l, at]).start()
 
     row, lane = iota((ROWS, GROUP), 0), iota((ROWS, GROUP), 1)
     head = lane // HEAD_COLS
@@ -232,8 +231,7 @@
         for c in range(2):
             piece = weights.at[l, pl.ds(c * half, half)]
             pltpu.make_async_copy(piece, piece, sems.at[l, c]).wait()
-        pltpu.make_async_copy(tables.at[l], tables.at[l], table_sem.at[l]).wait()
-        table = tables[l].astype(F32)
+        table = cot_ref[l, 16:32, :].astype(F32)
         table = table[0:4] + table[4:8] + table[8:12]
         bias = []
         for g in range(GROUPS):
@@ -273,7 +271,7 @@
     for q in range(LAYERS):
         quarter = jnp.broadcast_to(state[:, 128 * q : 128 * q + 128], (16, 128))
         out_ref[q, 192:208, :] = jnp.concatenate([quarter] * 4, axis=1).astype(BF)
-    seed = jnp.concatenate([cot_ref[q].astype(F32)[0:1] for q in range(LAYERS)], axis=1)
+    seed = jnp.concatenate([cot_ref[q, 0:16, :].astype(F32)[0:1] for q in range(LAYERS)], axis=1)
     cot = jnp.where(last, jnp.broadcast_to(seed, (ROWS, WIDTH)), 0.0).astype(BF)
 
     for l in reversed(range(LAYERS)):
@@ -376,25 +374,26 @@
     any_spec, vmem = pl.BlockSpec(memory_space=pl.ANY), pl.BlockSpec(memory_space=pltpu.VMEM)
     smem = pl.BlockSpec(memory_space=pltpu.SMEM)
     with jax.named_scope("packing"):
-        first, second, outgoing, facts = call(
-            packing_start,
-            (
-                shape((half + 16, 5 * WIDTH), BF),
-                shape((half, 5 * WIDTH), BF),
-                shape((ROWS, WIDTH), BF),
-                shape((n_dp, 2, (SLOTS + 2) * 64), BF),
-            ),
+        first, second = call(
+            weights_kernel,
+            (shape((half, 5 * WIDTH), BF), shape((half, 5 * WIDTH), BF)),
+            scratch=[pltpu.SemaphoreType.DMA((8,))],
+            in_specs=[any_spec] * 2,
+            limit=58,
+        )(w_uvqk, w_out)
+        outgoing, facts = call(
+            facts_kernel,
+            (shape((ROWS, WIDTH), BF), shape((n_dp, 2, (SLOTS + 2) * 64), BF)),
             scratch=[
                 pltpu.SMEM((DEV_HIST,), jnp.int32),
                 pltpu.SMEM((DEV_HIST,), jnp.int32),
                 pltpu.SMEM((DEV_HIST,), jnp.int32),
-                pltpu.VMEM((8, ROWS), F32),
                 pltpu.VMEM((SLOTS, 128), BF),
-                pltpu.SemaphoreType.DMA((14,)),
+                pltpu.SemaphoreType.DMA((5,)),
             ],
-            in_specs=[any_spec] * 8,
+            in_specs=[any_spec] * 5,
             limit=58,
-        )(balance_plan, routes.reshape(DEV_HIST), lengths, w_uvqk, w_out, events, rel_bias, state_cotangent)
+        )(balance_plan, routes.reshape(DEV_HIST), lengths, events, state_cotangent)
 
     with jax.named_scope("section_weights"):
         ring = [(s * 2, (s - 1) % LAYERS * 2) for s in range(LAYERS)]
@@ -421,11 +420,11 @@
         seeds, hot, count = call(
             functools.partial(routing_kernel, own_rows),
             (
-                shape((LAYERS, 16, 128), BF),
+                shape((LAYERS, 32, 128), BF),
                 shape((DEV_HIST, 16, half), BF),
                 shape((ROWS, 128), jnp.int32),
             ),
-        )(facts)
+        )(facts, rel_bias)
         seeds = lax.all_to_all(seeds, "segment", 0, 0, tiled=True)
         far_a, swap_a, swap_b, seeds = lax.optimization_barrier((far_a, swap_a, swap_b, seeds))
     with jax.named_scope("section_weights"):
@@ -437,7 +436,6 @@
             shape((LAYERS, MSG, WIDTH), BF),
             scratch=[
                 pltpu.VMEM((LAYERS, WIDTH, 5 * WIDTH), BF),
-                pltpu.VMEM((LAYERS, 16, 128), BF),
                 pltpu.VMEM((LAYERS, ROWS, 4 * WIDTH), BF),
                 pltpu.VMEM((LAYERS, ROWS, 4 * WIDTH), F32),
                 pltpu.VMEM((LAYERS, ROWS, WIDTH), F32),
@@ -447,13 +445,12 @@
                 pltpu.VMEM((LAYERS, GROUPS, ROWS, GROUP), BF),
                 pltpu.VMEM((LAYERS, GROUPS, ROWS, GROUP), F32),
                 pltpu.SemaphoreType.DMA((LAYERS, 2)),
-                pltpu.SemaphoreType.DMA((LAYERS,)),
             ],
-            in_specs=[smem] + [vmem] * 4 + [any_spec] * 9,
+            in_specs=[smem] + [vmem] * 4 + [any_spec] * 8,
             limit=28,
         )(
             balance_plan, events, other_events, count, seeds,
-            first, w_uvqk, w_out, near_a, near_b, swap_a, swap_b, far_a, far_b,
+            w_uvqk, w_out, near_a, near_b, swap_a, swap_b, far_a, far_b,
         )
 
     with jax.named_scope("section_exchange"):

time: 136 us -> 135 us (level)
  Pallas kernels: 19 us -> 21.2 us
    pallas_call x2 -> x3, Pallas kernels: 4.46 us -> 6.74 us  [the longest x1 3.37 us: body(): call(weights_kernel, (shape((half, 5 * WIDTH), BF), shape((half, 5 * WIDT...]
  transfers between devices with their start and end apart: 9 -> 9, of which waited for: 4 -> 4; matrix products, arithmetic and copies ran while one was open for 0% -> 0% of each run, Pallas kernels for 1% -> 2%
where the time goes in v7:
time: 135 us
  blocking collectives  55.8 us (41%)
  starting transfers between devices  44.1 us (33%)
  Pallas kernels  21.2 us (16%)
  waiting for transfers between devices  12.6 us (9%)
    all_to_all x1, blocking collectives, body(): blocks = lax.all_to_all(blocks, ('z', 'y'), 0, 0, tiled=True)  25.3 us
    all_to_all x1, starting transfers between devices, body(): facts = lax.all_to_all(facts, DP, 0, 0, tiled=True)  17.4 us
    all_to_all x1, blocking collectives, body(): arrived = lax.all_to_all(message, 'segment', 0, 0, tiled=True)  16.8 us
    all_to_all x1, blocking collectives, body(): seeds = lax.all_to_all(seeds, 'segment', 0, 0, tiled=True)  13.6 us
    pallas_call x1, Pallas kernels, body(): call(layers_kernel, shape((LAYERS, MSG, WIDTH), BF), scratch=[pltpu.VMEM(...  12.3 us
    ppermute x1, waiting for transfers between devices, body(): lax.ppermute(outgoing, 'z', [(i, (i + n_z // 2) % n_z) for i in range(n_z)])  7.92 us
    ppermute x1, starting transfers between devices, body(): lax.ppermute(outgoing, 'z', [(i, (i + n_z // 2) % n_z) for i in range(n_z)])  7.61 us
    ppermute x1, starting transfers between devices, body(): near_a = lax.ppermute(first, ('segment', 'core'), ring)  4.8 us
  transfers between devices with their start and end apart: 9, of which 4 were waited for; matrix products, arithmetic and copies ran while one was open for 0% of the time, Pallas kernels for 2%

profile of v7, /device:TPU:8, one launch (start us, length us, event | category | flops | bytes accessed | tf_op | source)
XLA Modules:
  0.0 134.8 jit_solution(5583018797740865428)
XLA Ops:
  0.6 3.4 %packing.2 = (bf16[256,2560]{1,0:T(8,128)(2,1)}, bf16[256,2560]{1,0:T(8,128)(2,1)}) custom-call(bf16[1,512,2048]{2,1,0:T(8,128)(2,1)} %w_in_ref.3, bf16[1,512,512]{2,1,0:T(8,128)(2,1)} %w_out_ref.3), custom_call_target="tpu_custom_call" | custom-call | tf_op jit(solution)/shard_map/packing/pallas_call | solution.py:377
  4.1 4.8 %collective-permute-start = (bf16[256,2560]{1,0:T(8,128)(2,1)}, bf16[256,2560]{1,0:T(8,128)(2,1)}, u32[]{:S(2)}, u32[]{:S(2)}) collective-permute-start(bf16[256,2560]{1,0:T(8,128)(2,1)} %get-tuple-element.24), channel_id=1, source_target_pairs={{0,384},{128,0},{256,128},{384,256},{1,129},{129,257},{257,385},{3... | collective-permute-start | bytes 3932168 | tf_op jit(solution)/shard_map/section_weights/ppermute | solution.py:402
  8.9 2.7 %collective-permute-start.2 = (bf16[256,2560]{1,0:T(8,128)(2,1)}, bf16[256,2560]{1,0:T(8,128)(2,1)}, u32[]{:S(2)}, u32[]{:S(2)}) collective-permute-start(bf16[256,2560]{1,0:T(8,128)(2,1)} %get-tuple-element.28), channel_id=1, source_target_pairs={{0,384},{128,0},{256,128},{384,256},{1,129},{129,257},{257,385},{3... | collective-permute-start | bytes 3932168 | tf_op jit(solution)/shard_map/section_weights/ppermute | solution.py:403
  11.6 2.3 %packing.3 = (bf16[64,512]{1,0:T(8,128)(2,1)}, bf16[128,2,640]{2,1,0:T(2,128)(2,1)}) custom-call(s32[4]{0:T(128)} %plan_ref.3, s32[4]{0:T(128)} %bitcast.8, s32[4]{0:T(128)} %lengths_ref.1, bf16[4,64,512]{2,1,0:T(8,128)(2,1)} %events_ref.3, bf16[1,8,128]{2,1,0:T(8,128)(2,1)} %cot_ref.1), custom_call_target="tpu_custom_call" | custom-call | tf_op jit(solution)/shard_map/packing/pallas_call | solution.py:384
  14.0 17.4 %all-to-all-start = ((bf16[128,2,640]{2,1,0:T(2,128)(2,1)}), bf16[128,2,640]{2,1,0:T(2,128)(2,1)S(1)}, u32[]{:S(2)}, u32[]{:S(2)}) async-start(bf16[128,2,640]{2,1,0:T(2,128)(2,1)} %get-tuple-element.26), calls=%async_computation | async-start | bytes 655360 | tf_op jit(solution)/shard_map/routing/all_to_all | solution.py:409
  31.4 7.6 %collective-permute-start.1 = (bf16[64,512]{1,0:T(8,128)(2,1)}, bf16[64,512]{1,0:T(8,128)(2,1)S(1)}, u32[]{:S(2)}, u32[]{:S(2)}) collective-permute-start(bf16[64,512]{1,0:T(8,128)(2,1)} %get-tuple-element.25), channel_id=1, source_target_pairs={{0,64},{16,80},{32,96},{48,112},{64,0},{80,16},{96,32},{112,48},{1... | collective-permute-start | bytes 196616 | tf_op jit(solution)/shard_map/events/ppermute | solution.py:406
  39.0 7.9 %collective-permute-done.1.other_ref = bf16[64,512]{1,0:T(8,128)(2,1)S(1)} collective-permute-done((bf16[64,512]{1,0:T(8,128)(2,1)}, bf16[64,512]{1,0:T(8,128)(2,1)S(1)}, u32[]{:S(2)}, u32[]{:S(2)}) %collective-permute-start.1) | collective-permute-done | bytes 65568 | tf_op jit(solution)/shard_map/events/ppermute | solution.py:406
  46.9 0.5 all-to-all-done
  47.4 1.9 %collective-permute-start.4 = (bf16[256,2560]{1,0:T(8,128)(2,1)}, bf16[256,2560]{1,0:T(8,128)(2,1)S(1)}, u32[]{:S(2)}, u32[]{:S(2)}) collective-permute-start(bf16[256,2560]{1,0:T(8,128)(2,1)} %collective-permute-done.near_a), channel_id=1, source_target_pairs={{0,1},{1,0},{2,3},{3,2},{4,5},{5,4},{6,7},{7,6},{8,9},{9,8},{10,11... | collective-permute-start | bytes 3932168 | tf_op jit(solution)/shard_map/section_weights/ppermute | solution.py:416
  49.3 2.4 %collective-permute-start.3 = (bf16[256,2560]{1,0:T(8,128)(2,1)}, bf16[256,2560]{1,0:T(8,128)(2,1)S(1)}, u32[]{:S(2)}, u32[]{:S(2)}) collective-permute-start(bf16[256,2560]{1,0:T(8,128)(2,1)} %collective-permute-done.near_a), channel_id=1, source_target_pairs={{0,384},{128,0},{256,128},{384,256},{1,129},{129,257},{257,385},{3... | collective-permute-start | bytes 3932168 | tf_op jit(solution)/shard_map/section_weights/ppermute | solution.py:415
  51.8 2.8 %collective-permute-start.5 = (bf16[256,2560]{1,0:T(8,128)(2,1)}, bf16[256,2560]{1,0:T(8,128)(2,1)S(1)}, u32[]{:S(2)}, u32[]{:S(2)}) collective-permute-start(bf16[256,2560]{1,0:T(8,128)(2,1)} %collective-permute-done.2.near_b), channel_id=1, source_target_pairs={{0,1},{1,0},{2,3},{3,2},{4,5},{5,4},{6,7},{7,6},{8,9},{9,8},{10,11... | collective-permute-start | bytes 3932168 | tf_op jit(solution)/shard_map/section_weights/ppermute | solution.py:417
  54.7 1.0 routing.1
  55.7 13.6 %all_to_all.20.cot_ref = bf16[4,32,128]{2,1,0:T(8,128)(2,1)S(1)} all-to-all(bf16[4,32,128]{2,1,0:T(8,128)(2,1)S(1)} %get-tuple-element.34), channel_id=1, replica_groups=mesh['segment'=4,'z'=8,'y'=8,'core'=2] {'segment'}, dimensions={0} | all-to-all | bytes 65536 | tf_op jit(solution)/shard_map/routing/all_to_all | solution.py:428
  69.3 2.6 %collective-permute-start.6 = (bf16[256,2560]{1,0:T(8,128)(2,1)S(1)}, bf16[256,2560]{1,0:T(8,128)(2,1)S(1)}, u32[]{:S(2)}, u32[]{:S(2)}) collective-permute-start(bf16[256,2560]{1,0:T(8,128)(2,1)S(1)} %collective-permute-done.3.far_a), channel_id=1, source_target_pairs={{0,1},{1,0},{2,3},{3,2},{4,5},{5,4},{6,7},{7,6},{8,9},{9,8},{10,11... | collective-permute-start | bytes 3932168 | tf_op jit(solution)/shard_map/section_weights/ppermute | solution.py:431
  71.9 2.6 %collective-permute-done.6.far_b = bf16[256,2560]{1,0:T(8,128)(2,1)S(1)} collective-permute-done((bf16[256,2560]{1,0:T(8,128)(2,1)S(1)}, bf16[256,2560]{1,0:T(8,128)(2,1)S(1)}, u32[]{:S(2)}, u32[]{:S(2)}) %collective-permute-start.6) | collective-permute-done | bytes 1310752 | tf_op jit(solution)/shard_map/section_weights/ppermute | solution.py:431
  74.5 12.3 %layers.1 = bf16[4,208,512]{2,1,0:T(8,128)(2,1)S(1)} custom-call(s32[4]{0:T(128)S(1)} %copy-done.4, bf16[4,64,512]{2,1,0:T(8,128)(2,1)S(1)} %copy-done.2, bf16[64,512]{1,0:T(8,128)(2,1)S(1)} %collective-permute-done.1.other_ref, s32[64,128]{1,0:T(8,128)S(1)} %get-tuple-element.31.count_ref, bf16[4,32,128]{2,1,0:T(8,128)(2,1)S(1)} %all_to_all.20.cot_ref, ...), custom_call_target="tpu_custom_call" | custom-call | tf_op jit(solution)/shard_map/layers/pallas_call | solution.py:434
  86.8 16.8 %all_to_all.21.got_ref = bf16[4,208,512]{2,1,0:T(8,128)(2,1)S(1)} all-to-all(bf16[4,208,512]{2,1,0:T(8,128)(2,1)S(1)} %layers.1), channel_id=1, replica_groups=mesh['segment'=4,'z'=8,'y'=8,'core'=2] {'segment'}, dimensions={0} | all-to-all | bytes 1703936 | tf_op jit(solution)/shard_map/section_exchange/all_to_all | solution.py:457
  103.7 1.3 weight_gradient.3
  105.0 1.9 %collective-permute-start.7 = (bf16[272,512]{1,0:T(8,128)(2,1)S(1)}, bf16[272,512]{1,0:T(8,128)(2,1)S(1)}, u32[]{:S(2)}, u32[]{:S(2)}) collective-permute-start(bf16[272,512]{1,0:T(8,128)(2,1)S(1)} %get-tuple-element.40.send_ref), channel_id=1, source_target_pairs={{0,1},{1,0},{2,3},{3,2},{4,5},{5,4},{6,7},{7,6},{8,9},{9,8},{10,11... | collective-permute-start | bytes 835592 | tf_op jit(solution)/shard_map/weight_gradient/ppermute | solution.py:467
  106.9 1.5 %collective-permute-done.7.got_ref = bf16[272,512]{1,0:T(8,128)(2,1)S(1)} collective-permute-done((bf16[272,512]{1,0:T(8,128)(2,1)S(1)}, bf16[272,512]{1,0:T(8,128)(2,1)S(1)}, u32[]{:S(2)}, u32[]{:S(2)}) %collective-permute-start.7) | collective-permute-done | bytes 278560 | tf_op jit(solution)/shard_map/weight_gradient/ppermute | solution.py:467
  108.4 0.1 weight_gradient.4
  108.5 0.1 reshape.20
  108.6 25.3 %all_to_all.22 = bf16[64,4,768]{2,1,0:T(4,128)(2,1)S(1)} all-to-all(bf16[64,4,768]{2,1,0:T(4,128)(2,1)S(1)} %reshape.20), channel_id=1, replica_groups=mesh['segment'=4,'z'=8,'y'=8,'core'=2] {'z','y'}, dimensions={0} | all-to-all | bytes 786432 | tf_op jit(solution)/shard_map/weight_gradient/all_to_all | solution.py:473
  134.0 0.8 weight_gradient.5
  (17 shorter events, 0.2 us)
Async XLA Ops:
  0.6 73.9 %copy-start = (bf16[1,512,2048]{2,1,0:T(8,128)(2,1)S(1)}, bf16[1,512,2048]{2,1,0:T(8,128)(2,1)}, u32[]{:S(2)}) copy-start(bf16[1,512,2048]{2,1,0:T(8,128)(2,1)} %w_in_ref.3) | copy-start | bytes 6291460
  4.0 50.6 %copy-start.3 = (f32[1,8,64]{2,1,0:T(8,128)S(1)}, f32[1,8,64]{2,1,0:T(8,128)}, u32[]{:S(2)}) copy-start(f32[1,8,64]{2,1,0:T(8,128)} %bias_ref.1) | copy-start | bytes 6148
  4.0 70.5 %copy-start.1 = (bf16[1,512,512]{2,1,0:T(8,128)(2,1)S(1)}, bf16[1,512,512]{2,1,0:T(8,128)(2,1)}, u32[]{:S(2)}) copy-start(bf16[1,512,512]{2,1,0:T(8,128)(2,1)} %w_out_ref.3) | copy-start | bytes 1572868
  4.0 70.5 %copy-start.2 = (bf16[4,64,512]{2,1,0:T(8,128)(2,1)S(1)}, bf16[4,64,512]{2,1,0:T(8,128)(2,1)}, u32[]{:S(2)}) copy-start(bf16[4,64,512]{2,1,0:T(8,128)(2,1)} %events_ref.3) | copy-start | bytes 786436
  4.1 70.5 %copy-start.4 = (s32[4]{0:T(128)S(1)}, s32[4]{0:T(128)}, u32[]{:S(2)}) copy-start(s32[4]{0:T(128)} %plan_ref.3) | copy-start | bytes 52
  4.1 43.4 %collective-permute-start = (bf16[256,2560]{1,0:T(8,128)(2,1)}, bf16[256,2560]{1,0:T(8,128)(2,1)}, u32[]{:S(2)}, u32[]{:S(2)}) collective-permute-start(bf16[256,2560]{1,0:T(8,128)(2,1)} %get-tuple-element.24), channel_id=1, source_target_pairs={{0,384},{128,0},{256,128},{384,256},{1,129},{129,257},{257,385},{3... | collective-permute-start | bytes 3932168 | tf_op jit(solution)/shard_map/section_weights/ppermute | solution.py:402
  8.9 42.9 %collective-permute-start.2 = (bf16[256,2560]{1,0:T(8,128)(2,1)}, bf16[256,2560]{1,0:T(8,128)(2,1)}, u32[]{:S(2)}, u32[]{:S(2)}) collective-permute-start(bf16[256,2560]{1,0:T(8,128)(2,1)} %get-tuple-element.28), channel_id=1, source_target_pairs={{0,384},{128,0},{256,128},{384,256},{1,129},{129,257},{257,385},{3... | collective-permute-start | bytes 3932168 | tf_op jit(solution)/shard_map/section_weights/ppermute | solution.py:403
  14.0 33.4 %all-to-all-start = ((bf16[128,2,640]{2,1,0:T(2,128)(2,1)}), bf16[128,2,640]{2,1,0:T(2,128)(2,1)S(1)}, u32[]{:S(2)}, u32[]{:S(2)}) async-start(bf16[128,2,640]{2,1,0:T(2,128)(2,1)} %get-tuple-element.26), calls=%async_computation | async-start | bytes 655360 | tf_op jit(solution)/shard_map/routing/all_to_all | solution.py:409
  31.4 15.5 %collective-permute-start.1 = (bf16[64,512]{1,0:T(8,128)(2,1)}, bf16[64,512]{1,0:T(8,128)(2,1)S(1)}, u32[]{:S(2)}, u32[]{:S(2)}) collective-permute-start(bf16[64,512]{1,0:T(8,128)(2,1)} %get-tuple-element.25), channel_id=1, source_target_pairs={{0,64},{16,80},{32,96},{48,112},{64,0},{80,16},{96,32},{112,48},{1... | collective-permute-start | bytes 196616 | tf_op jit(solution)/shard_map/events/ppermute | solution.py:406
  47.4 21.9 %collective-permute-start.4 = (bf16[256,2560]{1,0:T(8,128)(2,1)}, bf16[256,2560]{1,0:T(8,128)(2,1)S(1)}, u32[]{:S(2)}, u32[]{:S(2)}) collective-permute-start(bf16[256,2560]{1,0:T(8,128)(2,1)} %collective-permute-done.near_a), channel_id=1, source_target_pairs={{0,1},{1,0},{2,3},{3,2},{4,5},{5,4},{6,7},{7,6},{8,9},{9,8},{10,11... | collective-permute-start | bytes 3932168 | tf_op jit(solution)/shard_map/section_weights/ppermute | solution.py:416
  49.3 20.0 %collective-permute-start.3 = (bf16[256,2560]{1,0:T(8,128)(2,1)}, bf16[256,2560]{1,0:T(8,128)(2,1)S(1)}, u32[]{:S(2)}, u32[]{:S(2)}) collective-permute-start(bf16[256,2560]{1,0:T(8,128)(2,1)} %collective-permute-done.near_a), channel_id=1, source_target_pairs={{0,384},{128,0},{256,128},{384,256},{1,129},{129,257},{257,385},{3... | collective-permute-start | bytes 3932168 | tf_op jit(solution)/shard_map/section_weights/ppermute | solution.py:415
  51.8 17.5 %collective-permute-start.5 = (bf16[256,2560]{1,0:T(8,128)(2,1)}, bf16[256,2560]{1,0:T(8,128)(2,1)S(1)}, u32[]{:S(2)}, u32[]{:S(2)}) collective-permute-start(bf16[256,2560]{1,0:T(8,128)(2,1)} %collective-permute-done.2.near_b), channel_id=1, source_target_pairs={{0,1},{1,0},{2,3},{3,2},{4,5},{5,4},{6,7},{7,6},{8,9},{9,8},{10,11... | collective-permute-start | bytes 3932168 | tf_op jit(solution)/shard_map/section_weights/ppermute | solution.py:417
  69.3 5.2 %collective-permute-start.6 = (bf16[256,2560]{1,0:T(8,128)(2,1)S(1)}, bf16[256,2560]{1,0:T(8,128)(2,1)S(1)}, u32[]{:S(2)}, u32[]{:S(2)}) collective-permute-start(bf16[256,2560]{1,0:T(8,128)(2,1)S(1)} %collective-permute-done.3.far_a), channel_id=1, source_target_pairs={{0,1},{1,0},{2,3},{3,2},{4,5},{5,4},{6,7},{7,6},{8,9},{9,8},{10,11... | collective-permute-start | bytes 3932168 | tf_op jit(solution)/shard_map/section_weights/ppermute | solution.py:431
  105.0 3.4 %collective-permute-start.7 = (bf16[272,512]{1,0:T(8,128)(2,1)S(1)}, bf16[272,512]{1,0:T(8,128)(2,1)S(1)}, u32[]{:S(2)}, u32[]{:S(2)}) collective-permute-start(bf16[272,512]{1,0:T(8,128)(2,1)S(1)} %get-tuple-element.40.send_ref), channel_id=1, source_target_pairs={{0,1},{1,0},{2,3},{3,2},{4,5},{5,4},{6,7},{7,6},{8,9},{9,8},{10,11... | collective-permute-start | bytes 835592 | tf_op jit(solution)/shard_map/weight_gradient/ppermute | solution.py:467

commit v8 on v7

--- a/solution.py
+++ b/solution.py
@@ -50,17 +50,19 @@
     return upper * DEV_HIST + lax.axis_index("segment")
 
 
-def weights_kernel(w_in_ref, w_out_ref, first_ref, second_ref, sems):
-    core = lax.axis_index("core")
-    half = WIDTH // 2
+def weight_copies(w_in_ref, w_out_ref, dest_ref, start, sems):
+    rows = dest_ref.shape[0] // 2
     copies = []
-    for side, dest in ((core, first_ref), (1 - core, second_ref)):
-        for part in range(2):
-            rows = pl.ds(pl.multiple_of(side * half + part * (half // 2), half // 2), half // 2)
-            to = pl.ds(part * (half // 2), half // 2)
-            copies.append((w_in_ref.at[0, rows], dest.at[to, pl.ds(0, 4 * WIDTH)]))
-            copies.append((w_out_ref.at[0, rows], dest.at[to, pl.ds(4 * WIDTH, WIDTH)]))
-    copies = [pltpu.make_async_copy(*c, sems.at[n]) for n, c in enumerate(copies)]
+    for part in range(2):
+        source = pl.ds(pl.multiple_of(start + part * rows, rows), rows)
+        to = pl.ds(part * rows, rows)
+        copies.append((w_in_ref.at[0, source], dest_ref.at[to, pl.ds(0, 4 * WIDTH)]))
+        copies.append((w_out_ref.at[0, source], dest_ref.at[to, pl.ds(4 * WIDTH, WIDTH)]))
+    return [pltpu.make_async_copy(*c, sems.at[n]) for n, c in enumerate(copies)]
+
+
+def weights_kernel(w_in_ref, w_out_ref, first_ref, sems):
+    copies = weight_copies(w_in_ref, w_out_ref, first_ref, lax.axis_index("core") * (WIDTH // 2), sems)
     for c in copies:
         c.start()
     for c in copies:
@@ -84,12 +86,15 @@
 
 
 def facts_kernel(
-    plan_ref, routes_ref, lengths_ref, events_ref, cot_ref, outgoing_ref, facts_ref,
-    plan, routes, lengths, cot_s, sems,
+    plan_ref, routes_ref, lengths_ref, events_ref, cot_ref, w_in_ref, w_out_ref, second_ref, outgoing_ref, facts_ref,
+    plan, routes, lengths, cot_s, sems, weight_sems,
 ):
+    quarter = WIDTH // 4
+    start = (1 - lax.axis_index("core")) * (2 * quarter) + lax.rem(lax.axis_index("y"), 2) * quarter
+    copies = weight_copies(w_in_ref, w_out_ref, second_ref, start, weight_sems)
     small = [(plan_ref, plan), (routes_ref, routes), (lengths_ref, lengths), (cot_ref.at[0], cot_s)]
     small = [pltpu.make_async_copy(*c, sems.at[n]) for n, c in enumerate(small)]
-    for c in small:
+    for c in small + copies:
         c.start()
     for c in small:
         c.wait()
@@ -108,6 +113,8 @@
     blocks = [cot[k : k + 1] for k in range(SLOTS)] + [facts, jnp.zeros((1, 128), F32)]
     lines = [jnp.concatenate(blocks[k : k + 5], axis=1) for k in (0, 5)]
     facts_ref[...] = jnp.broadcast_to(jnp.concatenate(lines).astype(BF)[None], facts_ref.shape)
+    for c in copies:
+        c.wait()
     copy.wait()
 
 
@@ -162,7 +169,7 @@
 
 def layers_kernel(
     plan_ref, events_ref, other_ref, count_ref, cot_ref,
-    w_in_ref, w_out_ref, near_a, near_b, swap_a, swap_b, far_a, far_b,
+    w_in_ref, w_out_ref, near_a, near_b, near_y, swap_a, swap_b, swap_y, far_a, far_b,
     out_ref,
     weights, proj_s, dsilu_s, normed_s, rstd_s, norm_o_s, rstd_o_s, att_s, datt_s, sems,
 ):
@@ -171,10 +178,13 @@
     near = lax.rem(segment + 1 + 2 * core, LAYERS)
     swap = lax.rem(segment + 3 + 2 * core, LAYERS)
     far = lax.rem(segment + 2, LAYERS)
+    quarter = half // 2
+    side = lax.rem(lax.axis_index("y"), 2) * quarter
+    mine, others = core * half, (1 - core) * half
     held = (
-        (near, near_a, core, near_b, 1 - core),
-        (swap, swap_a, 1 - core, swap_b, core),
-        (far, far_a, core, far_b, 1 - core),
+        (near, ((near_a, mine, core), (near_b, others + side, 1 - core), (near_y, others + quarter - side, 1 - core))),
+        (swap, ((swap_a, others, 1 - core), (swap_b, mine + side, core), (swap_y, mine + quarter - side, core))),
+        (far, ((far_a, mine, core), (far_b, others, 1 - core))),
     )
     for l in range(LAYERS):
 
@@ -185,13 +195,13 @@
                 for piece, cols in ((w_in_ref, pl.ds(0, 4 * WIDTH)), (w_out_ref, pl.ds(4 * WIDTH, WIDTH))):
                     pltpu.make_async_copy(piece.at[0, rows], weights.at[l, rows, cols], sems.at[l, at]).start()
 
-        for slot, one, side, two, other_side in held:
+        for slot, pieces in held:
 
             @pl.when(slot == l)
             def _():
-                for piece, at in ((one, side), (two, other_side)):
-                    rows = pl.ds(pl.multiple_of(at * half, half), half)
-                    pltpu.make_async_copy(piece, weights.at[l, rows], sems.at[l, at]).start()
+                for piece, at, which in pieces:
+                    rows = pl.ds(pl.multiple_of(at, quarter), piece.shape[0])
+                    pltpu.make_async_copy(piece, weights.at[l, rows], sems.at[l, which]).start()
 
     row, lane = iota((ROWS, GROUP), 0), iota((ROWS, GROUP), 1)
     head = lane // HEAD_COLS
@@ -352,7 +362,7 @@
     return jax.ShapeDtypeStruct(dims, dtype)
 
 
-def call(kernel, outs, scratch=(), in_specs=None, out_specs=None, limit=48):
+def call(kernel, outs, scratch=(), in_specs=None, out_specs=None, limit=24):
     specs = {} if in_specs is None else {"in_specs": in_specs}
     specs |= {} if out_specs is None else {"out_specs": out_specs}
     return pl.pallas_call(
@@ -374,26 +384,31 @@
     any_spec, vmem = pl.BlockSpec(memory_space=pl.ANY), pl.BlockSpec(memory_space=pltpu.VMEM)
     smem = pl.BlockSpec(memory_space=pltpu.SMEM)
     with jax.named_scope("packing"):
-        first, second = call(
+        first = call(
             weights_kernel,
-            (shape((half, 5 * WIDTH), BF), shape((half, 5 * WIDTH), BF)),
-            scratch=[pltpu.SemaphoreType.DMA((8,))],
+            shape((half, 5 * WIDTH), BF),
+            scratch=[pltpu.SemaphoreType.DMA((4,))],
             in_specs=[any_spec] * 2,
             limit=58,
         )(w_uvqk, w_out)
-        outgoing, facts = call(
+        second, outgoing, facts = call(
             facts_kernel,
-            (shape((ROWS, WIDTH), BF), shape((n_dp, 2, (SLOTS + 2) * 64), BF)),
+            (
+                shape((half // 2, 5 * WIDTH), BF),
+                shape((ROWS, WIDTH), BF),
+                shape((n_dp, 2, (SLOTS + 2) * 64), BF),
+            ),
             scratch=[
                 pltpu.SMEM((DEV_HIST,), jnp.int32),
                 pltpu.SMEM((DEV_HIST,), jnp.int32),
                 pltpu.SMEM((DEV_HIST,), jnp.int32),
                 pltpu.VMEM((SLOTS, 128), BF),
                 pltpu.SemaphoreType.DMA((5,)),
+                pltpu.SemaphoreType.DMA((4,)),
             ],
-            in_specs=[any_spec] * 5,
+            in_specs=[any_spec] * 7,
             limit=58,
-        )(balance_plan, routes.reshape(DEV_HIST), lengths, events, state_cotangent)
+        )(balance_plan, routes.reshape(DEV_HIST), lengths, events, state_cotangent, w_uvqk, w_out)
 
     with jax.named_scope("section_weights"):
         ring = [(s * 2, (s - 1) % LAYERS * 2) for s in range(LAYERS)]
@@ -407,11 +422,11 @@
 
     with jax.named_scope("routing"):
         facts = lax.all_to_all(facts, DP, 0, 0, tiled=True)
-        near_a, other_events, facts = lax.optimization_barrier((near_a, other_events, facts))
-        near_b, facts = lax.optimization_barrier((near_b, facts))
+        near_a, near_b, other_events, facts = lax.optimization_barrier((near_a, near_b, other_events, facts))
         facts = facts.reshape(n_dp, (SLOTS + 2) * 128)
 
     with jax.named_scope("section_weights"):
+        near_y = lax.ppermute(near_b, "y", [(i, i ^ 1) for i in range(n_y)])
         far_a = lax.ppermute(near_a, ("segment", "core"), ring)
         swap_a = lax.ppermute(near_a, "core", swap)
         swap_b = lax.ppermute(near_b, "core", swap)
@@ -426,8 +441,9 @@
             ),
         )(facts, rel_bias)
         seeds = lax.all_to_all(seeds, "segment", 0, 0, tiled=True)
-        far_a, swap_a, swap_b, seeds = lax.optimization_barrier((far_a, swap_a, swap_b, seeds))
+        far_a, swap_a, swap_b, near_y, seeds = lax.optimization_barrier((far_a, swap_a, swap_b, near_y, seeds))
     with jax.named_scope("section_weights"):
+        swap_y = lax.ppermute(near_y, "core", swap)
         far_b = lax.ppermute(far_a, "core", swap)
 
     with jax.named_scope("layers"):
@@ -446,11 +462,11 @@
                 pltpu.VMEM((LAYERS, GROUPS, ROWS, GROUP), F32),
                 pltpu.SemaphoreType.DMA((LAYERS, 2)),
             ],
-            in_specs=[smem] + [vmem] * 4 + [any_spec] * 8,
+            in_specs=[smem] + [vmem] * 4 + [any_spec] * 10,
             limit=28,
         )(
             balance_plan, events, other_events, count, seeds,
-            w_uvqk, w_out, near_a, near_b, swap_a, swap_b, far_a, far_b,
+            w_uvqk, w_out, near_a, near_b, near_y, swap_a, swap_b, swap_y, far_a, far_b,
         )
 
     with jax.named_scope("section_exchange"):

time: 135 us -> 140 us (1.037)
  starting transfers between devices: 44.1 us -> 48.8 us
  blocking collectives: 55.8 us -> 52.2 us
  local copies, waits for them, and re-layouts: 0.26 us -> 2.7 us
    ppermute x0 -> x2, starting transfers between devices: none -> 5.21 us  [the longest x1 2.82 us: body(): near_y = lax.ppermute(near_b, 'y', [(i, i ^ 1) for i in range(n_y)])]
    ppermute x0 -> x2, waiting for transfers between devices: none -> 3.59 us  [the longest x1 1.89 us: body(): near_y = lax.ppermute(near_b, 'y', [(i, i ^ 1) for i in range(n_y)])]
    all_to_all x1, blocking collectives: 13.6 us -> 10.1 us  [body(): seeds = lax.all_to_all(seeds, 'segment', 0, 0, tiled=True)]
    ppermute x1, waiting for transfers between devices: 2.64 us -> 0.01 us  [body(): far_b = lax.ppermute(far_a, 'core', swap)]
    unnamed x11 -> x19, local copies, waits for them, and re-layouts: 0.07 us -> 2.51 us
  transfers between devices with their start and end apart: 9 -> 11, of which waited for: 4 -> 4; matrix products, arithmetic and copies ran while one was open for 0% -> 1% of each run, Pallas kernels for 2% -> 3%
where the time goes in v8:
time: 140 us; the launch traced here: 139 us
  blocking collectives  52.2 us (37%)
  starting transfers between devices  48.8 us (35%)
  Pallas kernels  21.4 us (15%)
  waiting for transfers between devices  12.9 us (9%)
  local copies, waits for them, and re-layouts  2.7 us (2%)
    all_to_all x1, blocking collectives, body(): blocks = lax.all_to_all(blocks, ('z', 'y'), 0, 0, tiled=True)  25.9 us
    all_to_all x1, starting transfers between devices, body(): facts = lax.all_to_all(facts, DP, 0, 0, tiled=True)  17.8 us
    all_to_all x1, blocking collectives, body(): arrived = lax.all_to_all(message, 'segment', 0, 0, tiled=True)  16.2 us
    pallas_call x1, Pallas kernels, body(): call(layers_kernel, shape((LAYERS, MSG, WIDTH), BF), scratch=[pltpu.VMEM(...  13.1 us
    all_to_all x1, blocking collectives, body(): seeds = lax.all_to_all(seeds, 'segment', 0, 0, tiled=True)  10.1 us
    ppermute x1, waiting for transfers between devices, body(): lax.ppermute(outgoing, 'z', [(i, (i + n_z // 2) % n_z) for i in range(n_z)])  7.75 us
    ppermute x1, starting transfers between devices, body(): lax.ppermute(outgoing, 'z', [(i, (i + n_z // 2) % n_z) for i in range(n_z)])  7.61 us
    ppermute x1, starting transfers between devices, body(): near_a = lax.ppermute(first, ('segment', 'core'), ring)  4.67 us
  transfers between devices with their start and end apart: 11, of which 4 were waited for; matrix products, arithmetic and copies ran while one was open for 1% of the time, Pallas kernels for 3%

profile of v8, /device:TPU:8, one launch (start us, length us, event | category | flops | bytes accessed | tf_op | source)
XLA Modules:
  0.0 138.9 jit_solution(8209510621480322690)
XLA Ops:
  0.6 2.4 %packing.2 = bf16[256,2560]{1,0:T(8,128)(2,1)} custom-call(bf16[1,512,2048]{2,1,0:T(8,128)(2,1)} %w_in_ref.5, bf16[1,512,512]{2,1,0:T(8,128)(2,1)} %w_out_ref.5), custom_call_target="tpu_custom_call" | custom-call | tf_op jit(solution)/shard_map/packing/pallas_call | solution.py:387
  3.0 4.7 %collective-permute-start = (bf16[256,2560]{1,0:T(8,128)(2,1)}, bf16[256,2560]{1,0:T(8,128)(2,1)}, u32[]{:S(2)}, u32[]{:S(2)}) collective-permute-start(bf16[256,2560]{1,0:T(8,128)(2,1)} %packing.2), channel_id=1, source_target_pairs={{0,384},{128,0},{256,128},{384,256},{1,129},{129,257},{257,385},{3... | collective-permute-start | bytes 3932168 | tf_op jit(solution)/shard_map/section_weights/ppermute | solution.py:417
  7.7 2.8 %packing.3 = (bf16[128,2560]{1,0:T(8,128)(2,1)}, bf16[64,512]{1,0:T(8,128)(2,1)}, bf16[128,2,640]{2,1,0:T(2,128)(2,1)}) custom-call(s32[4]{0:T(128)} %plan_ref.3, s32[4]{0:T(128)} %bitcast.7, s32[4]{0:T(128)} %lengths_ref.1, bf16[4,64,512]{2,1,0:T(8,128)(2,1)} %events_ref.3, bf16[1,8,128]{2,1,0:T(8,128)(2,1)} %cot_ref.1, bf16[1,512,2048]{2,1,0:T(8,128)(2,1)} %w_in_ref.5, ...), custom_call_target="tpu_custom_call" | custom-call | tf_op jit(solution)/shard_map/packing/pallas_call | solution.py:394
  10.5 2.9 %collective-permute-start.1 = (bf16[128,2560]{1,0:T(8,128)(2,1)}, bf16[128,2560]{1,0:T(8,128)(2,1)S(1)}, u32[]{:S(2)}, u32[]{:S(2)}) collective-permute-start(bf16[128,2560]{1,0:T(8,128)(2,1)} %get-tuple-element.23), channel_id=1, source_target_pairs={{0,384},{128,0},{256,128},{384,256},{1,129},{129,257},{257,385},{3... | collective-permute-start | bytes 1966088 | tf_op jit(solution)/shard_map/section_weights/ppermute | solution.py:418
  13.4 17.8 %all-to-all-start = ((bf16[128,2,640]{2,1,0:T(2,128)(2,1)}), bf16[128,2,640]{2,1,0:T(2,128)(2,1)}, u32[]{:S(2)}, u32[]{:S(2)}) async-start(bf16[128,2,640]{2,1,0:T(2,128)(2,1)} %get-tuple-element.25), calls=%async_computation | async-start | bytes 655360 | tf_op jit(solution)/shard_map/routing/all_to_all | solution.py:424
  31.2 7.6 %collective-permute-start.2 = (bf16[64,512]{1,0:T(8,128)(2,1)}, bf16[64,512]{1,0:T(8,128)(2,1)S(1)}, u32[]{:S(2)}, u32[]{:S(2)}) collective-permute-start(bf16[64,512]{1,0:T(8,128)(2,1)} %get-tuple-element.24), channel_id=1, source_target_pairs={{0,64},{16,80},{32,96},{48,112},{64,0},{80,16},{96,32},{112,48},{1... | collective-permute-start | bytes 196616 | tf_op jit(solution)/shard_map/events/ppermute | solution.py:421
  38.8 7.8 %collective-permute-done.2.other_ref = bf16[64,512]{1,0:T(8,128)(2,1)S(1)} collective-permute-done((bf16[64,512]{1,0:T(8,128)(2,1)}, bf16[64,512]{1,0:T(8,128)(2,1)S(1)}, u32[]{:S(2)}, u32[]{:S(2)}) %collective-permute-start.2) | collective-permute-done | bytes 65568 | tf_op jit(solution)/shard_map/events/ppermute | solution.py:421
  47.2 1.9 %collective-permute-start.4 = (bf16[256,2560]{1,0:T(8,128)(2,1)}, bf16[256,2560]{1,0:T(8,128)(2,1)S(1)}, u32[]{:S(2)}, u32[]{:S(2)}) collective-permute-start(bf16[256,2560]{1,0:T(8,128)(2,1)} %collective-permute-done.near_a), channel_id=1, source_target_pairs={{0,1},{1,0},{2,3},{3,2},{4,5},{5,4},{6,7},{7,6},{8,9},{9,8},{10,11... | collective-permute-start | bytes 3932168 | tf_op jit(solution)/shard_map/section_weights/ppermute | solution.py:431
  49.1 2.4 %collective-permute-start.3 = (bf16[256,2560]{1,0:T(8,128)(2,1)}, bf16[256,2560]{1,0:T(8,128)(2,1)S(1)}, u32[]{:S(2)}, u32[]{:S(2)}) collective-permute-start(bf16[256,2560]{1,0:T(8,128)(2,1)} %collective-permute-done.near_a), channel_id=1, source_target_pairs={{0,384},{128,0},{256,128},{384,256},{1,129},{129,257},{257,385},{3... | collective-permute-start | bytes 3932168 | tf_op jit(solution)/shard_map/section_weights/ppermute | solution.py:430
  51.6 2.8 %collective-permute-start.6 = (bf16[128,2560]{1,0:T(8,128)(2,1)S(1)}, bf16[128,2560]{1,0:T(8,128)(2,1)S(1)}, u32[]{:S(2)}, u32[]{:S(2)}) collective-permute-start(bf16[128,2560]{1,0:T(8,128)(2,1)S(1)} %collective-permute-done.1.near_b), channel_id=1, source_target_pairs={{0,2},{2,0},{4,6},{6,4},{8,10},{10,8},{12,14},{14,12},{1,3},{3,1},... | collective-permute-start | bytes 1966088 | tf_op jit(solution)/shard_map/section_weights/ppermute | solution.py:429
  54.4 2.5 %collective-permute-start.5 = (bf16[128,2560]{1,0:T(8,128)(2,1)S(1)}, bf16[128,2560]{1,0:T(8,128)(2,1)S(1)}, u32[]{:S(2)}, u32[]{:S(2)}) collective-permute-start(bf16[128,2560]{1,0:T(8,128)(2,1)S(1)} %collective-permute-done.1.near_b), channel_id=1, source_target_pairs={{0,1},{1,0},{2,3},{3,2},{4,5},{5,4},{6,7},{7,6},{8,9},{9,8},{10,11... | collective-permute-start | bytes 1966088 | tf_op jit(solution)/shard_map/section_weights/ppermute | solution.py:432
  56.9 1.0 copy.11
  58.0 1.0 routing.1
  59.0 10.1 %all_to_all.20.cot_ref = bf16[4,32,128]{2,1,0:T(8,128)(2,1)S(1)} all-to-all(bf16[4,32,128]{2,1,0:T(8,128)(2,1)S(1)} %get-tuple-element.31), channel_id=1, replica_groups=mesh['segment'=4,'z'=8,'y'=8,'core'=2] {'segment'}, dimensions={0} | all-to-all | bytes 65536 | tf_op jit(solution)/shard_map/routing/all_to_all | solution.py:443
  69.1 1.9 %collective-permute-done.6.near_y = bf16[128,2560]{1,0:T(8,128)(2,1)S(1)} collective-permute-done((bf16[128,2560]{1,0:T(8,128)(2,1)S(1)}, bf16[128,2560]{1,0:T(8,128)(2,1)S(1)}, u32[]{:S(2)}, u32[]{:S(2)}) %collective-permute-start.6) | collective-permute-done | bytes 655392 | tf_op jit(solution)/shard_map/section_weights/ppermute | solution.py:429
  71.0 1.9 %collective-permute-start.8 = (bf16[256,2560]{1,0:T(8,128)(2,1)S(1)}, bf16[256,2560]{1,0:T(8,128)(2,1)S(1)}, u32[]{:S(2)}, u32[]{:S(2)}) collective-permute-start(bf16[256,2560]{1,0:T(8,128)(2,1)S(1)} %collective-permute-done.3.far_a), channel_id=1, source_target_pairs={{0,1},{1,0},{2,3},{3,2},{4,5},{5,4},{6,7},{7,6},{8,9},{9,8},{10,11... | collective-permute-start | bytes 3932168 | tf_op jit(solution)/shard_map/section_weights/ppermute | solution.py:447
  73.0 2.4 %collective-permute-start.7 = (bf16[128,2560]{1,0:T(8,128)(2,1)S(1)}, bf16[128,2560]{1,0:T(8,128)(2,1)S(1)}, u32[]{:S(2)}, u32[]{:S(2)}) collective-permute-start(bf16[128,2560]{1,0:T(8,128)(2,1)S(1)} %collective-permute-done.6.near_y), channel_id=1, source_target_pairs={{0,1},{1,0},{2,3},{3,2},{4,5},{5,4},{6,7},{7,6},{8,9},{9,8},{10,11... | collective-permute-start | bytes 1966088 | tf_op jit(solution)/shard_map/section_weights/ppermute | solution.py:446
  75.4 1.7 %collective-permute-done.7.swap_y = bf16[128,2560]{1,0:T(8,128)(2,1)S(1)} collective-permute-done((bf16[128,2560]{1,0:T(8,128)(2,1)S(1)}, bf16[128,2560]{1,0:T(8,128)(2,1)S(1)}, u32[]{:S(2)}, u32[]{:S(2)}) %collective-permute-start.7) | collective-permute-done | bytes 655392 | tf_op jit(solution)/shard_map/section_weights/ppermute | solution.py:446
  77.9 13.1 %layers.1 = bf16[4,208,512]{2,1,0:T(8,128)(2,1)S(1)} custom-call(s32[4]{0:T(128)S(1)} %copy-done.8, bf16[4,64,512]{2,1,0:T(8,128)(2,1)S(1)} %copy-done.2, bf16[64,512]{1,0:T(8,128)(2,1)S(1)} %copy-done.4, s32[64,128]{1,0:T(8,128)S(1)} %get-tuple-element.28.count_ref, bf16[4,32,128]{2,1,0:T(8,128)(2,1)S(1)} %all_to_all.20.cot_ref, ...), custom_call_target="tpu_custom_call" | custom-call | tf_op jit(solution)/shard_map/layers/pallas_call | solution.py:450
  91.0 16.2 %all_to_all.21.got_ref = bf16[4,208,512]{2,1,0:T(8,128)(2,1)S(1)} all-to-all(bf16[4,208,512]{2,1,0:T(8,128)(2,1)S(1)} %layers.1), channel_id=1, replica_groups=mesh['segment'=4,'z'=8,'y'=8,'core'=2] {'segment'}, dimensions={0} | all-to-all | bytes 1703936 | tf_op jit(solution)/shard_map/section_exchange/all_to_all | solution.py:473
  107.2 1.3 weight_gradient.3
  108.5 1.9 %collective-permute-start.9 = (bf16[272,512]{1,0:T(8,128)(2,1)S(1)}, bf16[272,512]{1,0:T(8,128)(2,1)S(1)}, u32[]{:S(2)}, u32[]{:S(2)}) collective-permute-start(bf16[272,512]{1,0:T(8,128)(2,1)S(1)} %get-tuple-element.38.send_ref), channel_id=1, source_target_pairs={{0,1},{1,0},{2,3},{3,2},{4,5},{5,4},{6,7},{7,6},{8,9},{9,8},{10,11... | collective-permute-start | bytes 835592 | tf_op jit(solution)/shard_map/weight_gradient/ppermute | solution.py:483
  110.4 1.5 %collective-permute-done.9.got_ref = bf16[272,512]{1,0:T(8,128)(2,1)S(1)} collective-permute-done((bf16[272,512]{1,0:T(8,128)(2,1)S(1)}, bf16[272,512]{1,0:T(8,128)(2,1)S(1)}, u32[]{:S(2)}, u32[]{:S(2)}) %collective-permute-start.9) | collective-permute-done | bytes 278560 | tf_op jit(solution)/shard_map/weight_gradient/ppermute | solution.py:483
  112.2 25.9 %all_to_all.22 = bf16[64,4,768]{2,1,0:T(4,128)(2,1)S(1)} all-to-all(bf16[64,4,768]{2,1,0:T(4,128)(2,1)S(1)} %reshape.20), channel_id=1, replica_groups=mesh['segment'=4,'z'=8,'y'=8,'core'=2] {'z','y'}, dimensions={0} | all-to-all | bytes 786432 | tf_op jit(solution)/shard_map/weight_gradient/all_to_all | solution.py:489
  (29 shorter events, 2.6 us)
Async XLA Ops:
  3.0 44.2 %collective-permute-start = (bf16[256,2560]{1,0:T(8,128)(2,1)}, bf16[256,2560]{1,0:T(8,128)(2,1)}, u32[]{:S(2)}, u32[]{:S(2)}) collective-permute-start(bf16[256,2560]{1,0:T(8,128)(2,1)} %packing.2), channel_id=1, source_target_pairs={{0,384},{128,0},{256,128},{384,256},{1,129},{129,257},{257,385},{3... | collective-permute-start | bytes 3932168 | tf_op jit(solution)/shard_map/section_weights/ppermute | solution.py:417
  7.7 69.4 %copy-start = (bf16[1,512,2048]{2,1,0:T(8,128)(2,1)S(1)}, bf16[1,512,2048]{2,1,0:T(8,128)(2,1)}, u32[]{:S(2)}) copy-start(bf16[1,512,2048]{2,1,0:T(8,128)(2,1)} %w_in_ref.5) | copy-start | bytes 6291460
  10.5 47.5 %copy-start.7 = (f32[1,8,64]{2,1,0:T(8,128)S(1)}, f32[1,8,64]{2,1,0:T(8,128)}, u32[]{:S(2)}) copy-start(f32[1,8,64]{2,1,0:T(8,128)} %bias_ref.1) | copy-start | bytes 6148
  10.5 66.6 %copy-start.1 = (bf16[1,512,512]{2,1,0:T(8,128)(2,1)S(1)}, bf16[1,512,512]{2,1,0:T(8,128)(2,1)}, u32[]{:S(2)}) copy-start(bf16[1,512,512]{2,1,0:T(8,128)(2,1)} %w_out_ref.5) | copy-start | bytes 1572868
  10.5 66.6 %copy-start.2 = (bf16[4,64,512]{2,1,0:T(8,128)(2,1)S(1)}, bf16[4,64,512]{2,1,0:T(8,128)(2,1)}, u32[]{:S(2)}) copy-start(bf16[4,64,512]{2,1,0:T(8,128)(2,1)} %events_ref.3) | copy-start | bytes 786436
  10.5 66.6 %copy-start.8 = (s32[4]{0:T(128)S(1)}, s32[4]{0:T(128)}, u32[]{:S(2)}) copy-start(s32[4]{0:T(128)} %plan_ref.3) | copy-start | bytes 52
  10.5 36.7 %collective-permute-start.1 = (bf16[128,2560]{1,0:T(8,128)(2,1)}, bf16[128,2560]{1,0:T(8,128)(2,1)S(1)}, u32[]{:S(2)}, u32[]{:S(2)}) collective-permute-start(bf16[128,2560]{1,0:T(8,128)(2,1)} %get-tuple-element.23), channel_id=1, source_target_pairs={{0,384},{128,0},{256,128},{384,256},{1,129},{129,257},{257,385},{3... | collective-permute-start | bytes 1966088 | tf_op jit(solution)/shard_map/section_weights/ppermute | solution.py:418
  13.4 33.8 %all-to-all-start = ((bf16[128,2,640]{2,1,0:T(2,128)(2,1)}), bf16[128,2,640]{2,1,0:T(2,128)(2,1)}, u32[]{:S(2)}, u32[]{:S(2)}) async-start(bf16[128,2,640]{2,1,0:T(2,128)(2,1)} %get-tuple-element.25), calls=%async_computation | async-start | bytes 655360 | tf_op jit(solution)/shard_map/routing/all_to_all | solution.py:424
  31.2 15.4 %collective-permute-start.2 = (bf16[64,512]{1,0:T(8,128)(2,1)}, bf16[64,512]{1,0:T(8,128)(2,1)S(1)}, u32[]{:S(2)}, u32[]{:S(2)}) collective-permute-start(bf16[64,512]{1,0:T(8,128)(2,1)} %get-tuple-element.24), channel_id=1, source_target_pairs={{0,64},{16,80},{32,96},{48,112},{64,0},{80,16},{96,32},{112,48},{1... | collective-permute-start | bytes 196616 | tf_op jit(solution)/shard_map/events/ppermute | solution.py:421
  46.6 0.6 copy-start.3
  47.2 23.8 %collective-permute-start.4 = (bf16[256,2560]{1,0:T(8,128)(2,1)}, bf16[256,2560]{1,0:T(8,128)(2,1)S(1)}, u32[]{:S(2)}, u32[]{:S(2)}) collective-permute-start(bf16[256,2560]{1,0:T(8,128)(2,1)} %collective-permute-done.near_a), channel_id=1, source_target_pairs={{0,1},{1,0},{2,3},{3,2},{4,5},{5,4},{6,7},{7,6},{8,9},{9,8},{10,11... | collective-permute-start | bytes 3932168 | tf_op jit(solution)/shard_map/section_weights/ppermute | solution.py:431
  49.1 21.9 %collective-permute-start.3 = (bf16[256,2560]{1,0:T(8,128)(2,1)}, bf16[256,2560]{1,0:T(8,128)(2,1)S(1)}, u32[]{:S(2)}, u32[]{:S(2)}) collective-permute-start(bf16[256,2560]{1,0:T(8,128)(2,1)} %collective-permute-done.near_a), channel_id=1, source_target_pairs={{0,384},{128,0},{256,128},{384,256},{1,129},{129,257},{257,385},{3... | collective-permute-start | bytes 3932168 | tf_op jit(solution)/shard_map/section_weights/ppermute | solution.py:430
  51.6 19.4 %collective-permute-start.6 = (bf16[128,2560]{1,0:T(8,128)(2,1)S(1)}, bf16[128,2560]{1,0:T(8,128)(2,1)S(1)}, u32[]{:S(2)}, u32[]{:S(2)}) collective-permute-start(bf16[128,2560]{1,0:T(8,128)(2,1)S(1)} %collective-permute-done.1.near_b), channel_id=1, source_target_pairs={{0,2},{2,0},{4,6},{6,4},{8,10},{10,8},{12,14},{14,12},{1,3},{3,1},... | collective-permute-start | bytes 1966088 | tf_op jit(solution)/shard_map/section_weights/ppermute | solution.py:429
  54.4 16.6 %collective-permute-start.5 = (bf16[128,2560]{1,0:T(8,128)(2,1)S(1)}, bf16[128,2560]{1,0:T(8,128)(2,1)S(1)}, u32[]{:S(2)}, u32[]{:S(2)}) collective-permute-start(bf16[128,2560]{1,0:T(8,128)(2,1)S(1)} %collective-permute-done.1.near_b), channel_id=1, source_target_pairs={{0,1},{1,0},{2,3},{3,2},{4,5},{5,4},{6,7},{7,6},{8,9},{9,8},{10,11... | collective-permute-start | bytes 1966088 | tf_op jit(solution)/shard_map/section_weights/ppermute | solution.py:432
  59.0 32.0 %copy-start.5 = (bf16[4,16,256]{2,1,0:T(8,128)(2,1)}, bf16[4,16,256]{2,1,0:T(8,128)(2,1)S(1)}, u32[]{:S(2)}) copy-start(bf16[4,16,256]{2,1,0:T(8,128)(2,1)S(1)} %get-tuple-element.39.hot_ref) | copy-start | bytes 98308
  71.0 6.0 %collective-permute-start.8 = (bf16[256,2560]{1,0:T(8,128)(2,1)S(1)}, bf16[256,2560]{1,0:T(8,128)(2,1)S(1)}, u32[]{:S(2)}, u32[]{:S(2)}) collective-permute-start(bf16[256,2560]{1,0:T(8,128)(2,1)S(1)} %collective-permute-done.3.far_a), channel_id=1, source_target_pairs={{0,1},{1,0},{2,3},{3,2},{4,5},{5,4},{6,7},{7,6},{8,9},{9,8},{10,11... | collective-permute-start | bytes 3932168 | tf_op jit(solution)/shard_map/section_weights/ppermute | solution.py:447
  73.0 4.1 %collective-permute-start.7 = (bf16[128,2560]{1,0:T(8,128)(2,1)S(1)}, bf16[128,2560]{1,0:T(8,128)(2,1)S(1)}, u32[]{:S(2)}, u32[]{:S(2)}) collective-permute-start(bf16[128,2560]{1,0:T(8,128)(2,1)S(1)} %collective-permute-done.6.near_y), channel_id=1, source_target_pairs={{0,1},{1,0},{2,3},{3,2},{4,5},{5,4},{6,7},{7,6},{8,9},{9,8},{10,11... | collective-permute-start | bytes 1966088 | tf_op jit(solution)/shard_map/section_weights/ppermute | solution.py:446
  77.1 0.8 copy-start.4
  108.5 3.4 %collective-permute-start.9 = (bf16[272,512]{1,0:T(8,128)(2,1)S(1)}, bf16[272,512]{1,0:T(8,128)(2,1)S(1)}, u32[]{:S(2)}, u32[]{:S(2)}) collective-permute-start(bf16[272,512]{1,0:T(8,128)(2,1)S(1)} %get-tuple-element.38.send_ref), channel_id=1, source_target_pairs={{0,1},{1,0},{2,3},{3,2},{4,5},{5,4},{6,7},{7,6},{8,9},{9,8},{10,11... | collective-permute-start | bytes 835592 | tf_op jit(solution)/shard_map/weight_gradient/ppermute | solution.py:483
  112.1 26.1 %copy-start.6 = (bf16[4,16,256]{2,1,0:T(8,128)(2,1)S(1)}, bf16[4,16,256]{2,1,0:T(8,128)(2,1)}, u32[]{:S(2)}) copy-start(bf16[4,16,256]{2,1,0:T(8,128)(2,1)} %copy-done.5) | copy-start | bytes 98308

commit v9 on v8

--- a/solution.py
+++ b/solution.py
@@ -89,8 +89,7 @@
     plan_ref, routes_ref, lengths_ref, events_ref, cot_ref, w_in_ref, w_out_ref, second_ref, outgoing_ref, facts_ref,
     plan, routes, lengths, cot_s, sems, weight_sems,
 ):
-    quarter = WIDTH // 4
-    start = (1 - lax.axis_index("core")) * (2 * quarter) + lax.rem(lax.axis_index("y"), 2) * quarter
+    start = (1 - lax.axis_index("core")) * (WIDTH // 2)
     copies = weight_copies(w_in_ref, w_out_ref, second_ref, start, weight_sems)
     small = [(plan_ref, plan), (routes_ref, routes), (lengths_ref, lengths), (cot_ref.at[0], cot_s)]
     small = [pltpu.make_async_copy(*c, sems.at[n]) for n, c in enumerate(small)]
@@ -169,7 +168,7 @@
 
 def layers_kernel(
     plan_ref, events_ref, other_ref, count_ref, cot_ref,
-    w_in_ref, w_out_ref, near_a, near_b, near_y, swap_a, swap_b, swap_y, far_a, far_b,
+    w_in_ref, w_out_ref, near_a, near_b, swap_a, swap_b, far_a, far_b,
     out_ref,
     weights, proj_s, dsilu_s, normed_s, rstd_s, norm_o_s, rstd_o_s, att_s, datt_s, sems,
 ):
@@ -178,12 +177,10 @@
     near = lax.rem(segment + 1 + 2 * core, LAYERS)
     swap = lax.rem(segment + 3 + 2 * core, LAYERS)
     far = lax.rem(segment + 2, LAYERS)
-    quarter = half // 2
-    side = lax.rem(lax.axis_index("y"), 2) * quarter
     mine, others = core * half, (1 - core) * half
     held = (
-        (near, ((near_a, mine, core), (near_b, others + side, 1 - core), (near_y, others + quarter - side, 1 - core))),
-        (swap, ((swap_a, others, 1 - core), (swap_b, mine + side, core), (swap_y, mine + quarter - side, core))),
+        (near, ((near_a, mine, core), (near_b, others, 1 - core))),
+        (swap, ((swap_a, others, 1 - core), (swap_b, mine, core))),
         (far, ((far_a, mine, core), (far_b, others, 1 - core))),
     )
     for l in range(LAYERS):
@@ -200,7 +197,7 @@
             @pl.when(slot == l)
             def _():
                 for piece, at, which in pieces:
-                    rows = pl.ds(pl.multiple_of(at, quarter), piece.shape[0])
+                    rows = pl.ds(pl.multiple_of(at, half), half)
                     pltpu.make_async_copy(piece, weights.at[l, rows], sems.at[l, which]).start()
 
     row, lane = iota((ROWS, GROUP), 0), iota((ROWS, GROUP), 1)
@@ -394,7 +391,7 @@
         second, outgoing, facts = call(
             facts_kernel,
             (
-                shape((half // 2, 5 * WIDTH), BF),
+                shape((half, 5 * WIDTH), BF),
                 shape((ROWS, WIDTH), BF),
                 shape((n_dp, 2, (SLOTS + 2) * 64), BF),
             ),
@@ -422,11 +419,11 @@
 
     with jax.named_scope("routing"):
         facts = lax.all_to_all(facts, DP, 0, 0, tiled=True)
-        near_a, near_b, other_events, facts = lax.optimization_barrier((near_a, near_b, other_events, facts))
+        near_a, other_events, facts = lax.optimization_barrier((near_a, other_events, facts))
+        near_b, facts = lax.optimization_barrier((near_b, facts))
         facts = facts.reshape(n_dp, (SLOTS + 2) * 128)
 
     with jax.named_scope("section_weights"):
-        near_y = lax.ppermute(near_b, "y", [(i, i ^ 1) for i in range(n_y)])
         far_a = lax.ppermute(near_a, ("segment", "core"), ring)
         swap_a = lax.ppermute(near_a, "core", swap)
         swap_b = lax.ppermute(near_b, "core", swap)
@@ -441,9 +438,8 @@
             ),
         )(facts, rel_bias)
         seeds = lax.all_to_all(seeds, "segment", 0, 0, tiled=True)
-        far_a, swap_a, swap_b, near_y, seeds = lax.optimization_barrier((far_a, swap_a, swap_b, near_y, seeds))
+        far_a, swap_b, seeds = lax.optimization_barrier((far_a, swap_b, seeds))
     with jax.named_scope("section_weights"):
-        swap_y = lax.ppermute(near_y, "core", swap)
         far_b = lax.ppermute(far_a, "core", swap)
 
     with jax.named_scope("layers"):
@@ -462,11 +458,11 @@
                 pltpu.VMEM((LAYERS, GROUPS, ROWS, GROUP), F32),
                 pltpu.SemaphoreType.DMA((LAYERS, 2)),
             ],
-            in_specs=[smem] + [vmem] * 4 + [any_spec] * 10,
+            in_specs=[smem] + [vmem] * 4 + [any_spec] * 8,
             limit=28,
         )(
             balance_plan, events, other_events, count, seeds,
-            w_uvqk, w_out, near_a, near_b, near_y, swap_a, swap_b, swap_y, far_a, far_b,
+            w_uvqk, w_out, near_a, near_b, swap_a, swap_b, far_a, far_b,
         )
 
     with jax.named_scope("section_exchange"):

time: 140 us -> 135 us (0.964)
  blocking collectives: 52.2 us -> 43.5 us
  waiting for transfers between devices: 12.9 us -> 21.3 us
  local copies, waits for them, and re-layouts: 2.7 us -> 0.26 us
  starting transfers between devices: 48.8 us -> 46.8 us
    all_to_all x1 -> x0, blocking collectives: 10.1 us -> none  [body(): seeds = lax.all_to_all(seeds, 'segment', 0, 0, tiled=True)]
    all_to_all x0 -> x1, waiting for transfers between devices: none -> 8.12 us  [body(): seeds = lax.all_to_all(seeds, 'segment', 0, 0, tiled=True)]
    ppermute x2 -> x0, starting transfers between devices: 5.21 us -> none  [the longest x1 2.82 us: body(): near_y = lax.ppermute(near_b, 'y', [(i, i ^ 1) for i in range(n_y)])]
    all_to_all x0 -> x1, starting transfers between devices: none -> 3.75 us  [body(): seeds = lax.all_to_all(seeds, 'segment', 0, 0, tiled=True)]
    ppermute x2 -> x0, waiting for transfers between devices: 3.59 us -> none  [the longest x1 1.89 us: body(): near_y = lax.ppermute(near_b, 'y', [(i, i ^ 1) for i in range(n_y)])]
    ppermute x1, waiting for transfers between devices: 0.01 us -> 3.19 us  [body(): far_b = lax.ppermute(far_a, 'core', swap)]
    unnamed x19 -> x11, local copies, waits for them, and re-layouts: 2.51 us -> 0.07 us
    all_to_all x1, blocking collectives: 16.2 us -> 18.2 us  [body(): arrived = lax.all_to_all(message, 'segment', 0, 0, tiled=True)]
  transfers between devices with their start and end apart: 11 -> 10, of which waited for: 4 -> 5; matrix products, arithmetic and copies ran while one was open for 1% -> 0% of each run, Pallas kernels for 3% -> 3%
where the time goes in v9:
time: 135 us; the launch traced here: 134 us
  starting transfers between devices  46.8 us (35%)
  blocking collectives  43.5 us (32%)
  waiting for transfers between devices  21.3 us (16%)
  Pallas kernels  21.2 us (16%)
    all_to_all x1, blocking collectives, body(): blocks = lax.all_to_all(blocks, ('z', 'y'), 0, 0, tiled=True)  25.3 us
    all_to_all x1, blocking collectives, body(): arrived = lax.all_to_all(message, 'segment', 0, 0, tiled=True)  18.2 us
    all_to_all x1, starting transfers between devices, body(): facts = lax.all_to_all(facts, DP, 0, 0, tiled=True)  17.4 us
    pallas_call x1, Pallas kernels, body(): call(layers_kernel, shape((LAYERS, MSG, WIDTH), BF), scratch=[pltpu.VMEM(...  12 us
    all_to_all x1, waiting for transfers between devices, body(): seeds = lax.all_to_all(seeds, 'segment', 0, 0, tiled=True)  8.12 us
    ppermute x1, waiting for transfers between devices, body(): lax.ppermute(outgoing, 'z', [(i, (i + n_z // 2) % n_z) for i in range(n_z)])  7.92 us
    ppermute x1, starting transfers between devices, body(): lax.ppermute(outgoing, 'z', [(i, (i + n_z // 2) % n_z) for i in range(n_z)])  7.61 us
    ppermute x1, starting transfers between devices, body(): near_a = lax.ppermute(first, ('segment', 'core'), ring)  4.67 us
  transfers between devices with their start and end apart: 10, of which 5 were waited for; matrix products, arithmetic and copies ran while one was open for 0% of the time, Pallas kernels for 3%

profile of v9, /device:TPU:8, one launch (start us, length us, event | category | flops | bytes accessed | tf_op | source)
XLA Modules:
  0.0 134.0 jit_solution(5624205871038909697)
XLA Ops:
  0.6 2.4 %packing.2 = bf16[256,2560]{1,0:T(8,128)(2,1)} custom-call(bf16[1,512,2048]{2,1,0:T(8,128)(2,1)} %w_in_ref.5, bf16[1,512,512]{2,1,0:T(8,128)(2,1)} %w_out_ref.5), custom_call_target="tpu_custom_call" | custom-call | tf_op jit(solution)/shard_map/packing/pallas_call | solution.py:384
  3.0 4.7 %collective-permute-start = (bf16[256,2560]{1,0:T(8,128)(2,1)}, bf16[256,2560]{1,0:T(8,128)(2,1)}, u32[]{:S(2)}, u32[]{:S(2)}) collective-permute-start(bf16[256,2560]{1,0:T(8,128)(2,1)} %packing.2), channel_id=1, source_target_pairs={{0,384},{128,0},{256,128},{384,256},{1,129},{129,257},{257,385},{3... | collective-permute-start | bytes 3932168 | tf_op jit(solution)/shard_map/section_weights/ppermute | solution.py:414
  7.7 3.4 %packing.3 = (bf16[256,2560]{1,0:T(8,128)(2,1)}, bf16[64,512]{1,0:T(8,128)(2,1)}, bf16[128,2,640]{2,1,0:T(2,128)(2,1)}) custom-call(s32[4]{0:T(128)} %plan_ref.3, s32[4]{0:T(128)} %bitcast.8, s32[4]{0:T(128)} %lengths_ref.1, bf16[4,64,512]{2,1,0:T(8,128)(2,1)} %events_ref.3, bf16[1,8,128]{2,1,0:T(8,128)(2,1)} %cot_ref.1, bf16[1,512,2048]{2,1,0:T(8,128)(2,1)} %w_in_ref.5, ...), custom_call_target="tpu_custom_call" | custom-call | tf_op jit(solution)/shard_map/packing/pallas_call | solution.py:391
  11.1 2.9 %collective-permute-start.2 = (bf16[256,2560]{1,0:T(8,128)(2,1)}, bf16[256,2560]{1,0:T(8,128)(2,1)}, u32[]{:S(2)}, u32[]{:S(2)}) collective-permute-start(bf16[256,2560]{1,0:T(8,128)(2,1)} %get-tuple-element.25), channel_id=1, source_target_pairs={{0,384},{128,0},{256,128},{384,256},{1,129},{129,257},{257,385},{3... | collective-permute-start | bytes 3932168 | tf_op jit(solution)/shard_map/section_weights/ppermute | solution.py:415
  14.0 17.4 %all-to-all-start = ((bf16[128,2,640]{2,1,0:T(2,128)(2,1)}), bf16[128,2,640]{2,1,0:T(2,128)(2,1)S(1)}, u32[]{:S(2)}, u32[]{:S(2)}) async-start(bf16[128,2,640]{2,1,0:T(2,128)(2,1)} %get-tuple-element.23), calls=%async_computation | async-start | bytes 655360 | tf_op jit(solution)/shard_map/routing/all_to_all | solution.py:421
  31.4 7.6 %collective-permute-start.1 = (bf16[64,512]{1,0:T(8,128)(2,1)}, bf16[64,512]{1,0:T(8,128)(2,1)S(1)}, u32[]{:S(2)}, u32[]{:S(2)}) collective-permute-start(bf16[64,512]{1,0:T(8,128)(2,1)} %get-tuple-element.22), channel_id=1, source_target_pairs={{0,64},{16,80},{32,96},{48,112},{64,0},{80,16},{96,32},{112,48},{1... | collective-permute-start | bytes 196616 | tf_op jit(solution)/shard_map/events/ppermute | solution.py:418
  39.0 7.9 %collective-permute-done.1.other_ref = bf16[64,512]{1,0:T(8,128)(2,1)S(1)} collective-permute-done((bf16[64,512]{1,0:T(8,128)(2,1)}, bf16[64,512]{1,0:T(8,128)(2,1)S(1)}, u32[]{:S(2)}, u32[]{:S(2)}) %collective-permute-start.1) | collective-permute-done | bytes 65568 | tf_op jit(solution)/shard_map/events/ppermute | solution.py:418
  46.9 0.5 all-to-all-done
  47.5 2.4 %collective-permute-start.3 = (bf16[256,2560]{1,0:T(8,128)(2,1)}, bf16[256,2560]{1,0:T(8,128)(2,1)}, u32[]{:S(2)}, u32[]{:S(2)}) collective-permute-start(bf16[256,2560]{1,0:T(8,128)(2,1)} %collective-permute-done.near_a), channel_id=1, source_target_pairs={{0,384},{128,0},{256,128},{384,256},{1,129},{129,257},{257,385},{3... | collective-permute-start | bytes 3932168 | tf_op jit(solution)/shard_map/section_weights/ppermute | solution.py:427
  49.9 2.2 %collective-permute-start.4 = (bf16[256,2560]{1,0:T(8,128)(2,1)}, bf16[256,2560]{1,0:T(8,128)(2,1)}, u32[]{:S(2)}, u32[]{:S(2)}) collective-permute-start(bf16[256,2560]{1,0:T(8,128)(2,1)} %collective-permute-done.2.near_b), channel_id=1, source_target_pairs={{0,1},{1,0},{2,3},{3,2},{4,5},{5,4},{6,7},{7,6},{8,9},{9,8},{10,11... | collective-permute-start | bytes 3932168 | tf_op jit(solution)/shard_map/section_weights/ppermute | solution.py:429
  52.1 1.3 routing.1
  53.4 3.8 %all-to-all-start.1 = ((bf16[4,32,128]{2,1,0:T(8,128)(2,1)}), bf16[4,32,128]{2,1,0:T(8,128)(2,1)S(1)}, u32[]{:S(2)}, u32[]{:S(2)}) async-start(bf16[4,32,128]{2,1,0:T(8,128)(2,1)} %get-tuple-element.31), calls=%async_computation.1 | async-start | bytes 65536 | tf_op jit(solution)/shard_map/routing/all_to_all | solution.py:440
  57.2 2.1 %collective-permute-start.5 = (bf16[256,2560]{1,0:T(8,128)(2,1)}, bf16[256,2560]{1,0:T(8,128)(2,1)}, u32[]{:S(2)}, u32[]{:S(2)}) collective-permute-start(bf16[256,2560]{1,0:T(8,128)(2,1)} %collective-permute-done.near_a), channel_id=1, source_target_pairs={{0,1},{1,0},{2,3},{3,2},{4,5},{5,4},{6,7},{7,6},{8,9},{9,8},{10,11... | collective-permute-start | bytes 3932168 | tf_op jit(solution)/shard_map/section_weights/ppermute | solution.py:428
  59.3 8.1 %all-to-all-done.1.cot_ref = bf16[4,32,128]{2,1,0:T(8,128)(2,1)S(1)} async-done(((bf16[4,32,128]{2,1,0:T(8,128)(2,1)}), bf16[4,32,128]{2,1,0:T(8,128)(2,1)S(1)}, u32[]{:S(2)}, u32[]{:S(2)}) %all-to-all-start.1) | async-done | bytes 32800 | tf_op jit(solution)/shard_map/routing/all_to_all | solution.py:440
  67.4 1.9 %collective-permute-start.6 = (bf16[256,2560]{1,0:T(8,128)(2,1)}, bf16[256,2560]{1,0:T(8,128)(2,1)S(1)}, u32[]{:S(2)}, u32[]{:S(2)}) collective-permute-start(bf16[256,2560]{1,0:T(8,128)(2,1)} %collective-permute-done.3.far_a), channel_id=1, source_target_pairs={{0,1},{1,0},{2,3},{3,2},{4,5},{5,4},{6,7},{7,6},{8,9},{9,8},{10,11... | collective-permute-start | bytes 3932168 | tf_op jit(solution)/shard_map/section_weights/ppermute | solution.py:443
  69.4 3.2 %collective-permute-done.6.far_b = bf16[256,2560]{1,0:T(8,128)(2,1)S(1)} collective-permute-done((bf16[256,2560]{1,0:T(8,128)(2,1)}, bf16[256,2560]{1,0:T(8,128)(2,1)S(1)}, u32[]{:S(2)}, u32[]{:S(2)}) %collective-permute-start.6) | collective-permute-done | bytes 1310752 | tf_op jit(solution)/shard_map/section_weights/ppermute | solution.py:443
  72.6 12.0 %layers.1 = bf16[4,208,512]{2,1,0:T(8,128)(2,1)S(1)} custom-call(s32[4]{0:T(128)S(1)} %copy-done.4, bf16[4,64,512]{2,1,0:T(8,128)(2,1)S(1)} %copy-done.2, bf16[64,512]{1,0:T(8,128)(2,1)S(1)} %collective-permute-done.1.other_ref, s32[64,128]{1,0:T(8,128)S(1)} %get-tuple-element.28.count_ref, bf16[4,32,128]{2,1,0:T(8,128)(2,1)S(1)} %all-to-all-done.1.cot_ref, ...), custom_call_target="tpu_custom_call" | custom-call | tf_op jit(solution)/shard_map/layers/pallas_call | solution.py:446
  84.6 18.2 %all_to_all.20.got_ref = bf16[4,208,512]{2,1,0:T(8,128)(2,1)S(1)} all-to-all(bf16[4,208,512]{2,1,0:T(8,128)(2,1)S(1)} %layers.1), channel_id=1, replica_groups=mesh['segment'=4,'z'=8,'y'=8,'core'=2] {'segment'}, dimensions={0} | all-to-all | bytes 1703936 | tf_op jit(solution)/shard_map/section_exchange/all_to_all | solution.py:469
  102.8 1.3 weight_gradient.3
  104.1 1.9 %collective-permute-start.7 = (bf16[272,512]{1,0:T(8,128)(2,1)S(1)}, bf16[272,512]{1,0:T(8,128)(2,1)S(1)}, u32[]{:S(2)}, u32[]{:S(2)}) collective-permute-start(bf16[272,512]{1,0:T(8,128)(2,1)S(1)} %get-tuple-element.36.send_ref), channel_id=1, source_target_pairs={{0,1},{1,0},{2,3},{3,2},{4,5},{5,4},{6,7},{7,6},{8,9},{9,8},{10,11... | collective-permute-start | bytes 835592 | tf_op jit(solution)/shard_map/weight_gradient/ppermute | solution.py:479
  106.0 1.5 %collective-permute-done.7.got_ref = bf16[272,512]{1,0:T(8,128)(2,1)S(1)} collective-permute-done((bf16[272,512]{1,0:T(8,128)(2,1)S(1)}, bf16[272,512]{1,0:T(8,128)(2,1)S(1)}, u32[]{:S(2)}, u32[]{:S(2)}) %collective-permute-start.7) | collective-permute-done | bytes 278560 | tf_op jit(solution)/shard_map/weight_gradient/ppermute | solution.py:479
  107.5 0.1 weight_gradient.4
  107.8 25.3 %all_to_all.21 = bf16[64,4,768]{2,1,0:T(4,128)(2,1)S(1)} all-to-all(bf16[64,4,768]{2,1,0:T(4,128)(2,1)S(1)} %reshape.20), channel_id=1, replica_groups=mesh['segment'=4,'z'=8,'y'=8,'core'=2] {'z','y'}, dimensions={0} | all-to-all | bytes 786432 | tf_op jit(solution)/shard_map/weight_gradient/all_to_all | solution.py:485
  133.2 0.8 weight_gradient.5
  (18 shorter events, 0.3 us)
Async XLA Ops:
  3.0 44.5 %collective-permute-start = (bf16[256,2560]{1,0:T(8,128)(2,1)}, bf16[256,2560]{1,0:T(8,128)(2,1)}, u32[]{:S(2)}, u32[]{:S(2)}) collective-permute-start(bf16[256,2560]{1,0:T(8,128)(2,1)} %packing.2), channel_id=1, source_target_pairs={{0,384},{128,0},{256,128},{384,256},{1,129},{129,257},{257,385},{3... | collective-permute-start | bytes 3932168 | tf_op jit(solution)/shard_map/section_weights/ppermute | solution.py:414
  7.7 64.9 %copy-start = (bf16[1,512,2048]{2,1,0:T(8,128)(2,1)S(1)}, bf16[1,512,2048]{2,1,0:T(8,128)(2,1)}, u32[]{:S(2)}) copy-start(bf16[1,512,2048]{2,1,0:T(8,128)(2,1)} %w_in_ref.5) | copy-start | bytes 6291460
  11.1 41.1 %copy-start.3 = (f32[1,8,64]{2,1,0:T(8,128)S(1)}, f32[1,8,64]{2,1,0:T(8,128)}, u32[]{:S(2)}) copy-start(f32[1,8,64]{2,1,0:T(8,128)} %bias_ref.1) | copy-start | bytes 6148
  11.1 61.5 %copy-start.1 = (bf16[1,512,512]{2,1,0:T(8,128)(2,1)S(1)}, bf16[1,512,512]{2,1,0:T(8,128)(2,1)}, u32[]{:S(2)}) copy-start(bf16[1,512,512]{2,1,0:T(8,128)(2,1)} %w_out_ref.5) | copy-start | bytes 1572868
  11.1 61.5 %copy-start.2 = (bf16[4,64,512]{2,1,0:T(8,128)(2,1)S(1)}, bf16[4,64,512]{2,1,0:T(8,128)(2,1)}, u32[]{:S(2)}) copy-start(bf16[4,64,512]{2,1,0:T(8,128)(2,1)} %events_ref.3) | copy-start | bytes 786436
  11.1 61.5 %copy-start.4 = (s32[4]{0:T(128)S(1)}, s32[4]{0:T(128)}, u32[]{:S(2)}) copy-start(s32[4]{0:T(128)} %plan_ref.3) | copy-start | bytes 52
  11.1 38.8 %collective-permute-start.2 = (bf16[256,2560]{1,0:T(8,128)(2,1)}, bf16[256,2560]{1,0:T(8,128)(2,1)}, u32[]{:S(2)}, u32[]{:S(2)}) collective-permute-start(bf16[256,2560]{1,0:T(8,128)(2,1)} %get-tuple-element.25), channel_id=1, source_target_pairs={{0,384},{128,0},{256,128},{384,256},{1,129},{129,257},{257,385},{3... | collective-permute-start | bytes 3932168 | tf_op jit(solution)/shard_map/section_weights/ppermute | solution.py:415
  14.0 33.4 %all-to-all-start = ((bf16[128,2,640]{2,1,0:T(2,128)(2,1)}), bf16[128,2,640]{2,1,0:T(2,128)(2,1)S(1)}, u32[]{:S(2)}, u32[]{:S(2)}) async-start(bf16[128,2,640]{2,1,0:T(2,128)(2,1)} %get-tuple-element.23), calls=%async_computation | async-start | bytes 655360 | tf_op jit(solution)/shard_map/routing/all_to_all | solution.py:421
  31.4 15.5 %collective-permute-start.1 = (bf16[64,512]{1,0:T(8,128)(2,1)}, bf16[64,512]{1,0:T(8,128)(2,1)S(1)}, u32[]{:S(2)}, u32[]{:S(2)}) collective-permute-start(bf16[64,512]{1,0:T(8,128)(2,1)} %get-tuple-element.22), channel_id=1, source_target_pairs={{0,64},{16,80},{32,96},{48,112},{64,0},{80,16},{96,32},{112,48},{1... | collective-permute-start | bytes 196616 | tf_op jit(solution)/shard_map/events/ppermute | solution.py:418
  47.5 20.0 %collective-permute-start.3 = (bf16[256,2560]{1,0:T(8,128)(2,1)}, bf16[256,2560]{1,0:T(8,128)(2,1)}, u32[]{:S(2)}, u32[]{:S(2)}) collective-permute-start(bf16[256,2560]{1,0:T(8,128)(2,1)} %collective-permute-done.near_a), channel_id=1, source_target_pairs={{0,384},{128,0},{256,128},{384,256},{1,129},{129,257},{257,385},{3... | collective-permute-start | bytes 3932168 | tf_op jit(solution)/shard_map/section_weights/ppermute | solution.py:427
  49.9 17.5 %collective-permute-start.4 = (bf16[256,2560]{1,0:T(8,128)(2,1)}, bf16[256,2560]{1,0:T(8,128)(2,1)}, u32[]{:S(2)}, u32[]{:S(2)}) collective-permute-start(bf16[256,2560]{1,0:T(8,128)(2,1)} %collective-permute-done.2.near_b), channel_id=1, source_target_pairs={{0,1},{1,0},{2,3},{3,2},{4,5},{5,4},{6,7},{7,6},{8,9},{9,8},{10,11... | collective-permute-start | bytes 3932168 | tf_op jit(solution)/shard_map/section_weights/ppermute | solution.py:429
  53.4 14.0 %all-to-all-start.1 = ((bf16[4,32,128]{2,1,0:T(8,128)(2,1)}), bf16[4,32,128]{2,1,0:T(8,128)(2,1)S(1)}, u32[]{:S(2)}, u32[]{:S(2)}) async-start(bf16[4,32,128]{2,1,0:T(8,128)(2,1)} %get-tuple-element.31), calls=%async_computation.1 | async-start | bytes 65536 | tf_op jit(solution)/shard_map/routing/all_to_all | solution.py:440
  57.2 12.2 %collective-permute-start.5 = (bf16[256,2560]{1,0:T(8,128)(2,1)}, bf16[256,2560]{1,0:T(8,128)(2,1)}, u32[]{:S(2)}, u32[]{:S(2)}) collective-permute-start(bf16[256,2560]{1,0:T(8,128)(2,1)} %collective-permute-done.near_a), channel_id=1, source_target_pairs={{0,1},{1,0},{2,3},{3,2},{4,5},{5,4},{6,7},{7,6},{8,9},{9,8},{10,11... | collective-permute-start | bytes 3932168 | tf_op jit(solution)/shard_map/section_weights/ppermute | solution.py:428
  67.4 5.1 %collective-permute-start.6 = (bf16[256,2560]{1,0:T(8,128)(2,1)}, bf16[256,2560]{1,0:T(8,128)(2,1)S(1)}, u32[]{:S(2)}, u32[]{:S(2)}) collective-permute-start(bf16[256,2560]{1,0:T(8,128)(2,1)} %collective-permute-done.3.far_a), channel_id=1, source_target_pairs={{0,1},{1,0},{2,3},{3,2},{4,5},{5,4},{6,7},{7,6},{8,9},{9,8},{10,11... | collective-permute-start | bytes 3932168 | tf_op jit(solution)/shard_map/section_weights/ppermute | solution.py:443
  104.1 3.4 %collective-permute-start.7 = (bf16[272,512]{1,0:T(8,128)(2,1)S(1)}, bf16[272,512]{1,0:T(8,128)(2,1)S(1)}, u32[]{:S(2)}, u32[]{:S(2)}) collective-permute-start(bf16[272,512]{1,0:T(8,128)(2,1)S(1)} %get-tuple-element.36.send_ref), channel_id=1, source_target_pairs={{0,1},{1,0},{2,3},{3,2},{4,5},{5,4},{6,7},{7,6},{8,9},{9,8},{10,11... | collective-permute-start | bytes 835592 | tf_op jit(solution)/shard_map/weight_gradient/ppermute | solution.py:479

commit v10 on v7

--- a/solution.py
+++ b/solution.py
@@ -48,23 +48,6 @@
 def wanted_value():
     upper = (lax.axis_index("z") >= lax.axis_size("z") // 2).astype(jnp.int32)
     return upper * DEV_HIST + lax.axis_index("segment")
-
-
-def weights_kernel(w_in_ref, w_out_ref, first_ref, second_ref, sems):
-    core = lax.axis_index("core")
-    half = WIDTH // 2
-    copies = []
-    for side, dest in ((core, first_ref), (1 - core, second_ref)):
-        for part in range(2):
-            rows = pl.ds(pl.multiple_of(side * half + part * (half // 2), half // 2), half // 2)
-            to = pl.ds(part * (half // 2), half // 2)
-            copies.append((w_in_ref.at[0, rows], dest.at[to, pl.ds(0, 4 * WIDTH)]))
-            copies.append((w_out_ref.at[0, rows], dest.at[to, pl.ds(4 * WIDTH, WIDTH)]))
-    copies = [pltpu.make_async_copy(*c, sems.at[n]) for n, c in enumerate(copies)]
-    for c in copies:
-        c.start()
-    for c in copies:
-        c.wait()
 
 
 def bias_rows(bias):
@@ -162,7 +145,7 @@
 
 def layers_kernel(
     plan_ref, events_ref, other_ref, count_ref, cot_ref,
-    w_in_ref, w_out_ref, near_a, near_b, swap_a, swap_b, far_a, far_b,
+    w_in_ref, w_out_ref, near_a, near_b, swap_a, swap_b, far_a, far_b, far_c, far_d,
     out_ref,
     weights, proj_s, dsilu_s, normed_s, rstd_s, norm_o_s, rstd_o_s, att_s, datt_s, sems,
 ):
@@ -171,27 +154,23 @@
     near = lax.rem(segment + 1 + 2 * core, LAYERS)
     swap = lax.rem(segment + 3 + 2 * core, LAYERS)
     far = lax.rem(segment + 2, LAYERS)
-    held = (
-        (near, near_a, core, near_b, 1 - core),
-        (swap, swap_a, 1 - core, swap_b, core),
-        (far, far_a, core, far_b, 1 - core),
-    )
+    whole = ((segment, w_in_ref.at[0], w_out_ref.at[0]), (near, near_a, near_b), (swap, swap_a, swap_b))
     for l in range(LAYERS):
-
-        @pl.when(segment == l)
-        def _():
-            for at in range(2):
-                rows = pl.ds(at * half, half)
-                for piece, cols in ((w_in_ref, pl.ds(0, 4 * WIDTH)), (w_out_ref, pl.ds(4 * WIDTH, WIDTH))):
-                    pltpu.make_async_copy(piece.at[0, rows], weights.at[l, rows, cols], sems.at[l, at]).start()
-
-        for slot, one, side, two, other_side in held:
+        for slot, w_in, w_out in whole:
 
             @pl.when(slot == l)
             def _():
-                for piece, at in ((one, side), (two, other_side)):
-                    rows = pl.ds(pl.multiple_of(at * half, half), half)
-                    pltpu.make_async_copy(piece, weights.at[l, rows], sems.at[l, at]).start()
+                for at in range(2):
+                    rows = pl.ds(at * half, half)
+                    for piece, cols in ((w_in, pl.ds(0, 4 * WIDTH)), (w_out, pl.ds(4 * WIDTH, WIDTH))):
+                        pltpu.make_async_copy(piece.at[rows], weights.at[l, rows, cols], sems.at[l, at]).start()
+
+        @pl.when(far == l)
+        def _():
+            for w_in, w_out, at in ((far_a, far_c, core), (far_b, far_d, 1 - core)):
+                rows = pl.ds(pl.multiple_of(at * half, half), half)
+                for piece, cols in ((w_in, pl.ds(0, 4 * WIDTH)), (w_out, pl.ds(4 * WIDTH, WIDTH))):
+                    pltpu.make_async_copy(piece, weights.at[l, rows, cols], sems.at[l, at]).start()
 
     row, lane = iota((ROWS, GROUP), 0), iota((ROWS, GROUP), 1)
     head = lane // HEAD_COLS
@@ -238,16 +217,19 @@
             tiles = [jnp.broadcast_to(table[p : p + 1], (ROWS, 128)) for p in (2 * g, 2 * g + 1)]
             bias.append(jnp.concatenate([pltpu.roll(t, 0, 1, stride=1, stride_axis=0) for t in tiles], axis=1))
         normed_b = normed.astype(BF)
-        for kind in range(4):
+        proj = {}
+        for kind in (3, 2, 1, 0):
             cols = pl.ds(kind * WIDTH, WIDTH)
             pre = mm(normed_b, weights[l, :, cols])
             gated = sigmoid(pre)
             silu = pre * gated
-            proj_s[l, :, cols] = silu.astype(BF)
+            proj[kind] = silu.astype(BF)
+            proj_s[l, :, cols] = proj[kind]
             dsilu_s[l, :, cols] = gated + silu * (1.0 - gated)
-        keys = [block_diagonal(proj_s[l, :, part(3, g)]) for g in range(GROUPS)]
-        values = [block_diagonal(proj_s[l, :, part(1, g)]) for g in range(GROUPS)]
-        scores = [mm(proj_s[l, :, part(2, g)], keys[g], NT) * 0.125 + bias[g] for g in range(GROUPS)]
+        cut = [slice(g * GROUP, (g + 1) * GROUP) for g in range(GROUPS)]
+        keys = [block_diagonal(proj[3][:, c]) for c in cut]
+        values = [block_diagonal(proj[1][:, c]) for c in cut]
+        scores = [mm(proj[2][:, cut[g]], keys[g], NT) * 0.125 + bias[g] for g in range(GROUPS)]
         outs = []
         for g in range(GROUPS):
             gated = sigmoid(scores[g])
@@ -262,7 +244,7 @@
         norm_o = centred * rstd
         norm_o_s[l] = norm_o
         rstd_o_s[l] = jnp.broadcast_to(rstd, (ROWS, 128))
-        branch = (norm_o * proj_s[l, :, pl.ds(0, WIDTH)].astype(F32)).astype(BF)
+        branch = (norm_o * proj[0].astype(F32)).astype(BF)
         out_ref[l, 64:128, :] = branch
         acts = (acts + mm(branch, weights[l, :, pl.ds(4 * WIDTH, WIDTH)])).astype(BF).astype(F32)
 
@@ -352,7 +334,7 @@
     return jax.ShapeDtypeStruct(dims, dtype)
 
 
-def call(kernel, outs, scratch=(), in_specs=None, out_specs=None, limit=48):
+def call(kernel, outs, scratch=(), in_specs=None, out_specs=None, limit=24):
     specs = {} if in_specs is None else {"in_specs": in_specs}
     specs |= {} if out_specs is None else {"out_specs": out_specs}
     return pl.pallas_call(
@@ -374,16 +356,12 @@
     any_spec, vmem = pl.BlockSpec(memory_space=pl.ANY), pl.BlockSpec(memory_space=pltpu.VMEM)
     smem = pl.BlockSpec(memory_space=pltpu.SMEM)
     with jax.named_scope("packing"):
-        first, second = call(
-            weights_kernel,
-            (shape((half, 5 * WIDTH), BF), shape((half, 5 * WIDTH), BF)),
-            scratch=[pltpu.SemaphoreType.DMA((8,))],
-            in_specs=[any_spec] * 2,
-            limit=58,
-        )(w_uvqk, w_out)
         outgoing, facts = call(
             facts_kernel,
-            (shape((ROWS, WIDTH), BF), shape((n_dp, 2, (SLOTS + 2) * 64), BF)),
+            (
+                shape((ROWS, WIDTH), BF),
+                shape((n_dp, 2, (SLOTS + 2) * 64), BF),
+            ),
             scratch=[
                 pltpu.SMEM((DEV_HIST,), jnp.int32),
                 pltpu.SMEM((DEV_HIST,), jnp.int32),
@@ -399,8 +377,8 @@
         ring = [(s * 2, (s - 1) % LAYERS * 2) for s in range(LAYERS)]
         ring += [(s * 2 + 1, (s + 1) % LAYERS * 2 + 1) for s in range(LAYERS)]
         swap = [(0, 1), (1, 0)]
-        near_a = lax.ppermute(first, ("segment", "core"), ring)
-        near_b = lax.ppermute(second, ("segment", "core"), ring)
+        near_a = lax.ppermute(w_uvqk[0], ("segment", "core"), ring)
+        near_b = lax.ppermute(w_out[0], ("segment", "core"), ring)
 
     with jax.named_scope("events"):
         other_events = lax.ppermute(outgoing, "z", [(i, (i + n_z // 2) % n_z) for i in range(n_z)])
@@ -408,12 +386,14 @@
     with jax.named_scope("routing"):
         facts = lax.all_to_all(facts, DP, 0, 0, tiled=True)
         near_a, other_events, facts = lax.optimization_barrier((near_a, other_events, facts))
-        near_b, facts = lax.optimization_barrier((near_b, facts))
+        near_b, near_c, facts = lax.optimization_barrier((near_b, near_a, facts))
         facts = facts.reshape(n_dp, (SLOTS + 2) * 128)
 
     with jax.named_scope("section_weights"):
-        far_a = lax.ppermute(near_a, ("segment", "core"), ring)
-        swap_a = lax.ppermute(near_a, "core", swap)
+        lower = lax.axis_index("core") == 0
+        onward = [jnp.where(lower, a[:half], a[half:]) for a in (near_a, near_b)]
+        far_a, far_c = (lax.ppermute(a, ("segment", "core"), ring) for a in onward)
+        swap_a = lax.ppermute(near_c, "core", swap)
         swap_b = lax.ppermute(near_b, "core", swap)
 
     with jax.named_scope("routing"):
@@ -426,9 +406,9 @@
             ),
         )(facts, rel_bias)
         seeds = lax.all_to_all(seeds, "segment", 0, 0, tiled=True)
-        far_a, swap_a, swap_b, seeds = lax.optimization_barrier((far_a, swap_a, swap_b, seeds))
+        far_a, far_c, swap_b, seeds = lax.optimization_barrier((far_a, far_c, swap_b, seeds))
     with jax.named_scope("section_weights"):
-        far_b = lax.ppermute(far_a, "core", swap)
+        far_b, far_d = (lax.ppermute(a, "core", swap) for a in (far_a, far_c))
 
     with jax.named_scope("layers"):
         message = call(
@@ -446,11 +426,11 @@
                 pltpu.VMEM((LAYERS, GROUPS, ROWS, GROUP), F32),
                 pltpu.SemaphoreType.DMA((LAYERS, 2)),
             ],
-            in_specs=[smem] + [vmem] * 4 + [any_spec] * 8,
+            in_specs=[smem] + [vmem] * 4 + [any_spec] * 10,
             limit=28,
         )(
             balance_plan, events, other_events, count, seeds,
-            w_uvqk, w_out, near_a, near_b, swap_a, swap_b, far_a, far_b,
+            w_uvqk, w_out, near_a, near_b, swap_a, swap_b, far_a, far_b, far_c, far_d,
         )
 
     with jax.named_scope("section_exchange"):

time: 135 us -> 128 us (0.948)
  blocking collectives: 55.8 us -> 49.4 us
  starting transfers between devices: 44.1 us -> 50.2 us
  waiting for transfers between devices: 12.6 us -> 8.17 us
  Pallas kernels: 21.2 us -> 17.5 us
    ppermute x5 -> x7, starting transfers between devices: 14.4 us -> 20.5 us  [the longest x2 6.82 us: body(): far_a, far_c = (lax.ppermute(a, ('segment', 'core'), ring) for a in onward)]
    all_to_all x1, blocking collectives: 13.6 us -> 7.8 us  [body(): seeds = lax.all_to_all(seeds, 'segment', 0, 0, tiled=True)]
    pallas_call x1 -> x0, Pallas kernels: 3.37 us -> none  [body(): call(weights_kernel, (shape((half, 5 * WIDTH), BF), shape((half, 5 * WIDT...]
    ppermute x1, waiting for transfers between devices: 7.92 us -> 4.96 us  [body(): lax.ppermute(outgoing, 'z', [(i, (i + n_z // 2) % n_z) for i in range(n_z)])]
    ppermute x5 -> x7, waiting for transfers between devices: 2.65 us -> 1.29 us  [the longest x2 1.14 us: body(): far_b, far_d = (lax.ppermute(a, 'core', swap) for a in (far_a, far_c))]
  transfers between devices with their start and end apart: 9 -> 11, of which waited for: 4 -> 5; matrix products, arithmetic and copies ran while one was open for 0% -> 1% of each run, Pallas kernels for 2% -> 3%
where the time goes in v10:
time: 128 us; the launch traced here: 127 us
  starting transfers between devices  50.2 us (39%)
  blocking collectives  49.4 us (39%)
  Pallas kernels  17.5 us (14%)
  waiting for transfers between devices  8.17 us (6%)
    all_to_all x1, blocking collectives, body(): blocks = lax.all_to_all(blocks, ('z', 'y'), 0, 0, tiled=True)  25.4 us
    all_to_all x1, starting transfers between devices, body(): facts = lax.all_to_all(facts, DP, 0, 0, tiled=True)  17.8 us
    all_to_all x1, blocking collectives, body(): arrived = lax.all_to_all(message, 'segment', 0, 0, tiled=True)  16.2 us
    pallas_call x1, Pallas kernels, body(): call(layers_kernel, shape((LAYERS, MSG, WIDTH), BF), scratch=[pltpu.VMEM(...  11.9 us
    all_to_all x1, blocking collectives, body(): seeds = lax.all_to_all(seeds, 'segment', 0, 0, tiled=True)  7.8 us
    ppermute x1, starting transfers between devices, body(): lax.ppermute(outgoing, 'z', [(i, (i + n_z // 2) % n_z) for i in range(n_z)])  7.61 us
    ppermute x2, starting transfers between devices, body(): far_a, far_c = (lax.ppermute(a, ('segment', 'core'), ring) for a in onward)  6.82 us
    ppermute x1, waiting for transfers between devices, body(): lax.ppermute(outgoing, 'z', [(i, (i + n_z // 2) % n_z) for i in range(n_z)])  4.96 us
  transfers between devices with their start and end apart: 11, of which 5 were waited for; matrix products, arithmetic and copies ran while one was open for 1% of the time, Pallas kernels for 3%

profile of v10, /device:TPU:8, one launch (start us, length us, event | category | flops | bytes accessed | tf_op | source)
XLA Modules:
  0.0 127.4 jit_solution(15742197892388636250)
XLA Ops:
  0.6 4.7 %collective-permute-start = (bf16[512,2048]{1,0:T(8,128)(2,1)}, bf16[512,2048]{1,0:T(8,128)(2,1)S(1)}, u32[]{:S(2)}, u32[]{:S(2)}) collective-permute-start(bf16[512,2048]{1,0:T(8,128)(2,1)} %bitcast.8), channel_id=1, source_target_pairs={{0,384},{128,0},{256,128},{384,256},{1,129},{129,257},{257,385},{3... | collective-permute-start | bytes 6291464 | tf_op jit(solution)/shard_map/section_weights/ppermute | solution.py:380
  5.3 2.3 %packing.1 = (bf16[64,512]{1,0:T(8,128)(2,1)}, bf16[128,2,640]{2,1,0:T(2,128)(2,1)}) custom-call(s32[4]{0:T(128)} %plan_ref.3, s32[4]{0:T(128)} %bitcast.11, s32[4]{0:T(128)} %lengths_ref.1, bf16[4,64,512]{2,1,0:T(8,128)(2,1)} %events_ref.3, bf16[1,8,128]{2,1,0:T(8,128)(2,1)} %cot_ref.1), custom_call_target="tpu_custom_call" | custom-call | tf_op jit(solution)/shard_map/packing/pallas_call | solution.py:359
  7.7 17.8 %all-to-all-start = ((bf16[128,2,640]{2,1,0:T(2,128)(2,1)}), bf16[128,2,640]{2,1,0:T(2,128)(2,1)}, u32[]{:S(2)}, u32[]{:S(2)}) async-start(bf16[128,2,640]{2,1,0:T(2,128)(2,1)} %get-tuple-element.24), calls=%async_computation | async-start | bytes 655360 | tf_op jit(solution)/shard_map/routing/all_to_all | solution.py:387
  25.4 7.6 %collective-permute-start.1 = (bf16[64,512]{1,0:T(8,128)(2,1)}, bf16[64,512]{1,0:T(8,128)(2,1)S(1)}, u32[]{:S(2)}, u32[]{:S(2)}) collective-permute-start(bf16[64,512]{1,0:T(8,128)(2,1)} %get-tuple-element.23), channel_id=1, source_target_pairs={{0,64},{16,80},{32,96},{48,112},{64,0},{80,16},{96,32},{112,48},{1... | collective-permute-start | bytes 196616 | tf_op jit(solution)/shard_map/events/ppermute | solution.py:384
  33.1 2.7 %collective-permute-start.2 = (bf16[512,512]{1,0:T(8,128)(2,1)}, bf16[512,512]{1,0:T(8,128)(2,1)S(1)}, u32[]{:S(2)}, u32[]{:S(2)}) collective-permute-start(bf16[512,512]{1,0:T(8,128)(2,1)} %bitcast.10), channel_id=1, source_target_pairs={{0,384},{128,0},{256,128},{384,256},{1,129},{129,257},{257,385},{3... | collective-permute-start | bytes 1572872 | tf_op jit(solution)/shard_map/section_weights/ppermute | solution.py:381
  35.9 5.0 %collective-permute-done.1.other_ref = bf16[64,512]{1,0:T(8,128)(2,1)S(1)} collective-permute-done((bf16[64,512]{1,0:T(8,128)(2,1)}, bf16[64,512]{1,0:T(8,128)(2,1)S(1)}, u32[]{:S(2)}, u32[]{:S(2)}) %collective-permute-start.1) | collective-permute-done | bytes 65568 | tf_op jit(solution)/shard_map/events/ppermute | solution.py:384
  40.8 0.4 all-to-all-done
  41.3 2.9 %collective-permute-start.3 = (bf16[256,2048]{1,0:T(8,128)(2,1)S(1)}, bf16[256,2048]{1,0:T(8,128)(2,1)S(1)}, u32[]{:S(2)}, u32[]{:S(2)}) collective-permute-start(bf16[256,2048]{1,0:T(8,128)(2,1)S(1)} %slice_select_fusion), channel_id=1, source_target_pairs={{0,384},{128,0},{256,128},{384,256},{1,129},{129,257},{257,385},{3... | collective-permute-start | bytes 3145736 | tf_op jit(solution)/shard_map/section_weights/ppermute | solution.py:395
  44.3 1.9 %collective-permute-start.6 = (bf16[512,2048]{1,0:T(8,128)(2,1)S(1)}, bf16[512,2048]{1,0:T(8,128)(2,1)S(1)}, u32[]{:S(2)}, u32[]{:S(2)}) collective-permute-start(bf16[512,2048]{1,0:T(8,128)(2,1)S(1)} %collective-permute-done.near_a), channel_id=1, source_target_pairs={{0,1},{1,0},{2,3},{3,2},{4,5},{5,4},{6,7},{7,6},{8,9},{9,8},{10,11... | collective-permute-start | bytes 6291464 | tf_op jit(solution)/shard_map/section_weights/ppermute | solution.py:396
  46.3 2.4 %collective-permute-start.5 = (bf16[512,512]{1,0:T(8,128)(2,1)S(1)}, bf16[512,512]{1,0:T(8,128)(2,1)S(1)}, u32[]{:S(2)}, u32[]{:S(2)}) collective-permute-start(bf16[512,512]{1,0:T(8,128)(2,1)S(1)} %collective-permute-done.2.near_b), channel_id=1, source_target_pairs={{0,1},{1,0},{2,3},{3,2},{4,5},{5,4},{6,7},{7,6},{8,9},{9,8},{10,11... | collective-permute-start | bytes 1572872 | tf_op jit(solution)/shard_map/section_weights/ppermute | solution.py:397
  48.7 3.9 %collective-permute-start.4 = (bf16[256,512]{1,0:T(8,128)(2,1)S(1)}, bf16[256,512]{1,0:T(8,128)(2,1)S(1)}, u32[]{:S(2)}, u32[]{:S(2)}) collective-permute-start(bf16[256,512]{1,0:T(8,128)(2,1)S(1)} %slice_select_fusion.1), channel_id=1, source_target_pairs={{0,384},{128,0},{256,128},{384,256},{1,129},{129,257},{257,385},{3... | collective-permute-start | bytes 786440 | tf_op jit(solution)/shard_map/section_weights/ppermute | solution.py:395
  52.7 1.0 copy.11
  53.7 1.0 routing.1
  54.7 7.8 %all_to_all.20.cot_ref = bf16[4,32,128]{2,1,0:T(8,128)(2,1)S(1)} all-to-all(bf16[4,32,128]{2,1,0:T(8,128)(2,1)S(1)} %get-tuple-element.31), channel_id=1, replica_groups=mesh['segment'=4,'z'=8,'y'=8,'core'=2] {'segment'}, dimensions={0} | all-to-all | bytes 65536 | tf_op jit(solution)/shard_map/routing/all_to_all | solution.py:408
  62.5 1.9 %collective-permute-start.7 = (bf16[256,2048]{1,0:T(8,128)(2,1)S(1)}, bf16[256,2048]{1,0:T(8,128)(2,1)S(1)}, u32[]{:S(2)}, u32[]{:S(2)}) collective-permute-start(bf16[256,2048]{1,0:T(8,128)(2,1)S(1)} %collective-permute-done.3.far_a), channel_id=1, source_target_pairs={{0,1},{1,0},{2,3},{3,2},{4,5},{5,4},{6,7},{7,6},{8,9},{9,8},{10,11... | collective-permute-start | bytes 3145736 | tf_op jit(solution)/shard_map/section_weights/ppermute | solution.py:411
  64.5 2.4 %collective-permute-start.8 = (bf16[256,512]{1,0:T(8,128)(2,1)S(1)}, bf16[256,512]{1,0:T(8,128)(2,1)S(1)}, u32[]{:S(2)}, u32[]{:S(2)}) collective-permute-start(bf16[256,512]{1,0:T(8,128)(2,1)S(1)} %collective-permute-done.4.far_c), channel_id=1, source_target_pairs={{0,1},{1,0},{2,3},{3,2},{4,5},{5,4},{6,7},{7,6},{8,9},{9,8},{10,11... | collective-permute-start | bytes 786440 | tf_op jit(solution)/shard_map/section_weights/ppermute | solution.py:411
  66.9 1.1 collective-permute-done.8.far_d
  68.1 11.9 %layers.1 = bf16[4,208,512]{2,1,0:T(8,128)(2,1)S(1)} custom-call(s32[4]{0:T(128)S(1)} %copy-done.4, bf16[4,64,512]{2,1,0:T(8,128)(2,1)S(1)} %copy-done.1, bf16[64,512]{1,0:T(8,128)(2,1)S(1)} %collective-permute-done.1.other_ref, s32[64,128]{1,0:T(8,128)S(1)} %get-tuple-element.29.count_ref, bf16[4,32,128]{2,1,0:T(8,128)(2,1)S(1)} %all_to_all.20.cot_ref, ...), custom_call_target="tpu_custom_call" | custom-call | tf_op jit(solution)/shard_map/layers/pallas_call | solution.py:414
  80.0 16.2 %all_to_all.21.got_ref = bf16[4,208,512]{2,1,0:T(8,128)(2,1)S(1)} all-to-all(bf16[4,208,512]{2,1,0:T(8,128)(2,1)S(1)} %layers.1), channel_id=1, replica_groups=mesh['segment'=4,'z'=8,'y'=8,'core'=2] {'segment'}, dimensions={0} | all-to-all | bytes 1703936 | tf_op jit(solution)/shard_map/section_exchange/all_to_all | solution.py:437
  96.2 1.3 weight_gradient.3
  97.5 1.9 %collective-permute-start.9 = (bf16[272,512]{1,0:T(8,128)(2,1)S(1)}, bf16[272,512]{1,0:T(8,128)(2,1)S(1)}, u32[]{:S(2)}, u32[]{:S(2)}) collective-permute-start(bf16[272,512]{1,0:T(8,128)(2,1)S(1)} %get-tuple-element.38.send_ref), channel_id=1, source_target_pairs={{0,1},{1,0},{2,3},{3,2},{4,5},{5,4},{6,7},{7,6},{8,9},{9,8},{10,11... | collective-permute-start | bytes 835592 | tf_op jit(solution)/shard_map/weight_gradient/ppermute | solution.py:447
  99.4 1.5 %collective-permute-done.9.got_ref = bf16[272,512]{1,0:T(8,128)(2,1)S(1)} collective-permute-done((bf16[272,512]{1,0:T(8,128)(2,1)S(1)}, bf16[272,512]{1,0:T(8,128)(2,1)S(1)}, u32[]{:S(2)}, u32[]{:S(2)}) %collective-permute-start.9) | collective-permute-done | bytes 278560 | tf_op jit(solution)/shard_map/weight_gradient/ppermute | solution.py:447
  101.1 25.4 %all_to_all.22 = bf16[64,4,768]{2,1,0:T(4,128)(2,1)S(1)} all-to-all(bf16[64,4,768]{2,1,0:T(4,128)(2,1)S(1)} %reshape.20), channel_id=1, replica_groups=mesh['segment'=4,'z'=8,'y'=8,'core'=2] {'z','y'}, dimensions={0} | all-to-all | bytes 786432 | tf_op jit(solution)/shard_map/weight_gradient/all_to_all | solution.py:453
  126.7 0.8 weight_gradient.5
  (22 shorter events, 0.6 us)
Async XLA Ops:
  0.6 40.6 %collective-permute-start = (bf16[512,2048]{1,0:T(8,128)(2,1)}, bf16[512,2048]{1,0:T(8,128)(2,1)S(1)}, u32[]{:S(2)}, u32[]{:S(2)}) collective-permute-start(bf16[512,2048]{1,0:T(8,128)(2,1)} %bitcast.8), channel_id=1, source_target_pairs={{0,384},{128,0},{256,128},{384,256},{1,129},{129,257},{257,385},{3... | collective-permute-start | bytes 6291464 | tf_op jit(solution)/shard_map/section_weights/ppermute | solution.py:380
  7.7 33.6 %all-to-all-start = ((bf16[128,2,640]{2,1,0:T(2,128)(2,1)}), bf16[128,2,640]{2,1,0:T(2,128)(2,1)}, u32[]{:S(2)}, u32[]{:S(2)}) async-start(bf16[128,2,640]{2,1,0:T(2,128)(2,1)} %get-tuple-element.24), calls=%async_computation | async-start | bytes 655360 | tf_op jit(solution)/shard_map/routing/all_to_all | solution.py:387
  25.4 15.4 %collective-permute-start.1 = (bf16[64,512]{1,0:T(8,128)(2,1)}, bf16[64,512]{1,0:T(8,128)(2,1)S(1)}, u32[]{:S(2)}, u32[]{:S(2)}) collective-permute-start(bf16[64,512]{1,0:T(8,128)(2,1)} %get-tuple-element.23), channel_id=1, source_target_pairs={{0,64},{16,80},{32,96},{48,112},{64,0},{80,16},{96,32},{112,48},{1... | collective-permute-start | bytes 196616 | tf_op jit(solution)/shard_map/events/ppermute | solution.py:384
  33.1 11.3 %collective-permute-start.2 = (bf16[512,512]{1,0:T(8,128)(2,1)}, bf16[512,512]{1,0:T(8,128)(2,1)S(1)}, u32[]{:S(2)}, u32[]{:S(2)}) collective-permute-start(bf16[512,512]{1,0:T(8,128)(2,1)} %bitcast.10), channel_id=1, source_target_pairs={{0,384},{128,0},{256,128},{384,256},{1,129},{129,257},{257,385},{3... | collective-permute-start | bytes 1572872 | tf_op jit(solution)/shard_map/section_weights/ppermute | solution.py:381
  35.8 17.9 %copy-start.3 = (f32[1,8,64]{2,1,0:T(8,128)S(1)}, f32[1,8,64]{2,1,0:T(8,128)}, u32[]{:S(2)}) copy-start(f32[1,8,64]{2,1,0:T(8,128)} %bias_ref.1) | copy-start | bytes 6148
  35.8 32.2 %copy-start.1 = (bf16[4,64,512]{2,1,0:T(8,128)(2,1)S(1)}, bf16[4,64,512]{2,1,0:T(8,128)(2,1)}, u32[]{:S(2)}) copy-start(bf16[4,64,512]{2,1,0:T(8,128)(2,1)} %events_ref.3) | copy-start | bytes 786436
  35.8 32.2 %copy-start.2 = (bf16[1,512,512]{2,1,0:T(8,128)(2,1)S(1)}, bf16[1,512,512]{2,1,0:T(8,128)(2,1)}, u32[]{:S(2)}) copy-start(bf16[1,512,512]{2,1,0:T(8,128)(2,1)} %w_out_ref.1) | copy-start | bytes 1572868
  35.9 32.2 %copy-start.4 = (s32[4]{0:T(128)S(1)}, s32[4]{0:T(128)}, u32[]{:S(2)}) copy-start(s32[4]{0:T(128)} %plan_ref.3) | copy-start | bytes 52
  41.2 26.8 %copy-start = (bf16[1,512,2048]{2,1,0:T(8,128)(2,1)S(1)}, bf16[1,512,2048]{2,1,0:T(8,128)(2,1)}, u32[]{:S(2)}) copy-start(bf16[1,512,2048]{2,1,0:T(8,128)(2,1)} %w_in_ref.1) | copy-start | bytes 6291460
  41.3 21.2 %collective-permute-start.3 = (bf16[256,2048]{1,0:T(8,128)(2,1)S(1)}, bf16[256,2048]{1,0:T(8,128)(2,1)S(1)}, u32[]{:S(2)}, u32[]{:S(2)}) collective-permute-start(bf16[256,2048]{1,0:T(8,128)(2,1)S(1)} %slice_select_fusion), channel_id=1, source_target_pairs={{0,384},{128,0},{256,128},{384,256},{1,129},{129,257},{257,385},{3... | collective-permute-start | bytes 3145736 | tf_op jit(solution)/shard_map/section_weights/ppermute | solution.py:395
  44.3 23.7 %collective-permute-start.6 = (bf16[512,2048]{1,0:T(8,128)(2,1)S(1)}, bf16[512,2048]{1,0:T(8,128)(2,1)S(1)}, u32[]{:S(2)}, u32[]{:S(2)}) collective-permute-start(bf16[512,2048]{1,0:T(8,128)(2,1)S(1)} %collective-permute-done.near_a), channel_id=1, source_target_pairs={{0,1},{1,0},{2,3},{3,2},{4,5},{5,4},{6,7},{7,6},{8,9},{9,8},{10,11... | collective-permute-start | bytes 6291464 | tf_op jit(solution)/shard_map/section_weights/ppermute | solution.py:396
  46.3 16.3 %collective-permute-start.5 = (bf16[512,512]{1,0:T(8,128)(2,1)S(1)}, bf16[512,512]{1,0:T(8,128)(2,1)S(1)}, u32[]{:S(2)}, u32[]{:S(2)}) collective-permute-start(bf16[512,512]{1,0:T(8,128)(2,1)S(1)} %collective-permute-done.2.near_b), channel_id=1, source_target_pairs={{0,1},{1,0},{2,3},{3,2},{4,5},{5,4},{6,7},{7,6},{8,9},{9,8},{10,11... | collective-permute-start | bytes 1572872 | tf_op jit(solution)/shard_map/section_weights/ppermute | solution.py:397
  48.7 13.8 %collective-permute-start.4 = (bf16[256,512]{1,0:T(8,128)(2,1)S(1)}, bf16[256,512]{1,0:T(8,128)(2,1)S(1)}, u32[]{:S(2)}, u32[]{:S(2)}) collective-permute-start(bf16[256,512]{1,0:T(8,128)(2,1)S(1)} %slice_select_fusion.1), channel_id=1, source_target_pairs={{0,384},{128,0},{256,128},{384,256},{1,129},{129,257},{257,385},{3... | collective-permute-start | bytes 786440 | tf_op jit(solution)/shard_map/section_weights/ppermute | solution.py:395
  62.5 5.5 %collective-permute-start.7 = (bf16[256,2048]{1,0:T(8,128)(2,1)S(1)}, bf16[256,2048]{1,0:T(8,128)(2,1)S(1)}, u32[]{:S(2)}, u32[]{:S(2)}) collective-permute-start(bf16[256,2048]{1,0:T(8,128)(2,1)S(1)} %collective-permute-done.3.far_a), channel_id=1, source_target_pairs={{0,1},{1,0},{2,3},{3,2},{4,5},{5,4},{6,7},{7,6},{8,9},{9,8},{10,11... | collective-permute-start | bytes 3145736 | tf_op jit(solution)/shard_map/section_weights/ppermute | solution.py:411
  64.5 3.6 %collective-permute-start.8 = (bf16[256,512]{1,0:T(8,128)(2,1)S(1)}, bf16[256,512]{1,0:T(8,128)(2,1)S(1)}, u32[]{:S(2)}, u32[]{:S(2)}) collective-permute-start(bf16[256,512]{1,0:T(8,128)(2,1)S(1)} %collective-permute-done.4.far_c), channel_id=1, source_target_pairs={{0,1},{1,0},{2,3},{3,2},{4,5},{5,4},{6,7},{7,6},{8,9},{9,8},{10,11... | collective-permute-start | bytes 786440 | tf_op jit(solution)/shard_map/section_weights/ppermute | solution.py:411
  97.5 3.4 %collective-permute-start.9 = (bf16[272,512]{1,0:T(8,128)(2,1)S(1)}, bf16[272,512]{1,0:T(8,128)(2,1)S(1)}, u32[]{:S(2)}, u32[]{:S(2)}) collective-permute-start(bf16[272,512]{1,0:T(8,128)(2,1)S(1)} %get-tuple-element.38.send_ref), channel_id=1, source_target_pairs={{0,1},{1,0},{2,3},{3,2},{4,5},{5,4},{6,7},{7,6},{8,9},{9,8},{10,11... | collective-permute-start | bytes 835592 | tf_op jit(solution)/shard_map/weight_gradient/ppermute | solution.py:447

commit v11 on v10

--- a/solution.py
+++ b/solution.py
@@ -68,9 +68,9 @@
 
 def facts_kernel(
     plan_ref, routes_ref, lengths_ref, events_ref, cot_ref, outgoing_ref, facts_ref,
-    plan, routes, lengths, cot_s, sems,
+    plan, routes, lengths, sems,
 ):
-    small = [(plan_ref, plan), (routes_ref, routes), (lengths_ref, lengths), (cot_ref.at[0], cot_s)]
+    small = [(plan_ref, plan), (routes_ref, routes), (lengths_ref, lengths)]
     small = [pltpu.make_async_copy(*c, sems.at[n]) for n, c in enumerate(small)]
     for c in small:
         c.start()
@@ -87,7 +87,7 @@
     for j, ref in enumerate((routes, plan, lengths)):
         for h in range(DEV_HIST):
             facts = jnp.where(lane == 4 * j + h, ref[h].astype(F32), facts)
-    cot = cot_s[...].astype(F32)
+    cot = cot_ref[0].astype(F32)
     blocks = [cot[k : k + 1] for k in range(SLOTS)] + [facts, jnp.zeros((1, 128), F32)]
     lines = [jnp.concatenate(blocks[k : k + 5], axis=1) for k in (0, 5)]
     facts_ref[...] = jnp.broadcast_to(jnp.concatenate(lines).astype(BF)[None], facts_ref.shape)
@@ -366,10 +366,9 @@
                 pltpu.SMEM((DEV_HIST,), jnp.int32),
                 pltpu.SMEM((DEV_HIST,), jnp.int32),
                 pltpu.SMEM((DEV_HIST,), jnp.int32),
-                pltpu.VMEM((SLOTS, 128), BF),
-                pltpu.SemaphoreType.DMA((5,)),
+                pltpu.SemaphoreType.DMA((4,)),
             ],
-            in_specs=[any_spec] * 5,
+            in_specs=[any_spec] * 4 + [vmem],
             limit=58,
         )(balance_plan, routes.reshape(DEV_HIST), lengths, events, state_cotangent)
 

time: 128 us -> 129 us (level)
  no operation moved by 1% of the time
where the time goes in v11:
time: 129 us; the launch traced here: 128 us
  starting transfers between devices  50.2 us (39%)
  blocking collectives  49.4 us (38%)
  Pallas kernels  18.1 us (14%)
  waiting for transfers between devices  8.17 us (6%)
    all_to_all x1, blocking collectives, body(): blocks = lax.all_to_all(blocks, ('z', 'y'), 0, 0, tiled=True)  25.4 us
    all_to_all x1, starting transfers between devices, body(): facts = lax.all_to_all(facts, DP, 0, 0, tiled=True)  17.8 us
    all_to_all x1, blocking collectives, body(): arrived = lax.all_to_all(message, 'segment', 0, 0, tiled=True)  16.2 us
    pallas_call x1, Pallas kernels, body(): call(layers_kernel, shape((LAYERS, MSG, WIDTH), BF), scratch=[pltpu.VMEM(...  11.9 us
    all_to_all x1, blocking collectives, body(): seeds = lax.all_to_all(seeds, 'segment', 0, 0, tiled=True)  7.8 us
    ppermute x1, starting transfers between devices, body(): lax.ppermute(outgoing, 'z', [(i, (i + n_z // 2) % n_z) for i in range(n_z)])  7.61 us
    ppermute x2, starting transfers between devices, body(): far_a, far_c = (lax.ppermute(a, ('segment', 'core'), ring) for a in onward)  6.82 us
    ppermute x1, waiting for transfers between devices, body(): lax.ppermute(outgoing, 'z', [(i, (i + n_z // 2) % n_z) for i in range(n_z)])  4.96 us
  transfers between devices with their start and end apart: 11, of which 5 were waited for; matrix products, arithmetic and copies ran while one was open for 1% of the time, Pallas kernels for 3%

profile of v11, /device:TPU:8, one launch (start us, length us, event | category | flops | bytes accessed | tf_op | source)
XLA Modules:
  0.0 128.0 jit_solution(16074775465993602289)
XLA Ops:
  0.6 4.7 %collective-permute-start = (bf16[512,2048]{1,0:T(8,128)(2,1)}, bf16[512,2048]{1,0:T(8,128)(2,1)S(1)}, u32[]{:S(2)}, u32[]{:S(2)}) collective-permute-start(bf16[512,2048]{1,0:T(8,128)(2,1)} %bitcast.8), channel_id=1, source_target_pairs={{0,384},{128,0},{256,128},{384,256},{1,129},{129,257},{257,385},{3... | collective-permute-start | bytes 6291464 | tf_op jit(solution)/shard_map/section_weights/ppermute | solution.py:379
  5.3 3.0 %packing.1 = (bf16[64,512]{1,0:T(8,128)(2,1)}, bf16[128,2,640]{2,1,0:T(2,128)(2,1)}) custom-call(s32[4]{0:T(128)} %plan_ref.3, s32[4]{0:T(128)} %bitcast.11, s32[4]{0:T(128)} %lengths_ref.1, bf16[4,64,512]{2,1,0:T(8,128)(2,1)} %events_ref.3, bf16[1,8,128]{2,1,0:T(8,128)(2,1)} %cot_ref.1), custom_call_target="tpu_custom_call" | custom-call | tf_op jit(solution)/shard_map/packing/pallas_call | solution.py:359
  8.3 17.8 %all-to-all-start = ((bf16[128,2,640]{2,1,0:T(2,128)(2,1)}), bf16[128,2,640]{2,1,0:T(2,128)(2,1)}, u32[]{:S(2)}, u32[]{:S(2)}) async-start(bf16[128,2,640]{2,1,0:T(2,128)(2,1)} %get-tuple-element.24), calls=%async_computation | async-start | bytes 655360 | tf_op jit(solution)/shard_map/routing/all_to_all | solution.py:386
  26.1 7.6 %collective-permute-start.1 = (bf16[64,512]{1,0:T(8,128)(2,1)}, bf16[64,512]{1,0:T(8,128)(2,1)S(1)}, u32[]{:S(2)}, u32[]{:S(2)}) collective-permute-start(bf16[64,512]{1,0:T(8,128)(2,1)} %get-tuple-element.23), channel_id=1, source_target_pairs={{0,64},{16,80},{32,96},{48,112},{64,0},{80,16},{96,32},{112,48},{1... | collective-permute-start | bytes 196616 | tf_op jit(solution)/shard_map/events/ppermute | solution.py:383
  33.7 2.7 %collective-permute-start.2 = (bf16[512,512]{1,0:T(8,128)(2,1)}, bf16[512,512]{1,0:T(8,128)(2,1)S(1)}, u32[]{:S(2)}, u32[]{:S(2)}) collective-permute-start(bf16[512,512]{1,0:T(8,128)(2,1)} %bitcast.10), channel_id=1, source_target_pairs={{0,384},{128,0},{256,128},{384,256},{1,129},{129,257},{257,385},{3... | collective-permute-start | bytes 1572872 | tf_op jit(solution)/shard_map/section_weights/ppermute | solution.py:380
  36.5 5.0 %collective-permute-done.1.other_ref = bf16[64,512]{1,0:T(8,128)(2,1)S(1)} collective-permute-done((bf16[64,512]{1,0:T(8,128)(2,1)}, bf16[64,512]{1,0:T(8,128)(2,1)S(1)}, u32[]{:S(2)}, u32[]{:S(2)}) %collective-permute-start.1) | collective-permute-done | bytes 65568 | tf_op jit(solution)/shard_map/events/ppermute | solution.py:383
  41.5 0.4 all-to-all-done
  42.0 2.9 %collective-permute-start.3 = (bf16[256,2048]{1,0:T(8,128)(2,1)S(1)}, bf16[256,2048]{1,0:T(8,128)(2,1)S(1)}, u32[]{:S(2)}, u32[]{:S(2)}) collective-permute-start(bf16[256,2048]{1,0:T(8,128)(2,1)S(1)} %slice_select_fusion), channel_id=1, source_target_pairs={{0,384},{128,0},{256,128},{384,256},{1,129},{129,257},{257,385},{3... | collective-permute-start | bytes 3145736 | tf_op jit(solution)/shard_map/section_weights/ppermute | solution.py:394
  45.0 1.9 %collective-permute-start.6 = (bf16[512,2048]{1,0:T(8,128)(2,1)S(1)}, bf16[512,2048]{1,0:T(8,128)(2,1)S(1)}, u32[]{:S(2)}, u32[]{:S(2)}) collective-permute-start(bf16[512,2048]{1,0:T(8,128)(2,1)S(1)} %collective-permute-done.near_a), channel_id=1, source_target_pairs={{0,1},{1,0},{2,3},{3,2},{4,5},{5,4},{6,7},{7,6},{8,9},{9,8},{10,11... | collective-permute-start | bytes 6291464 | tf_op jit(solution)/shard_map/section_weights/ppermute | solution.py:395
  46.9 2.4 %collective-permute-start.5 = (bf16[512,512]{1,0:T(8,128)(2,1)S(1)}, bf16[512,512]{1,0:T(8,128)(2,1)S(1)}, u32[]{:S(2)}, u32[]{:S(2)}) collective-permute-start(bf16[512,512]{1,0:T(8,128)(2,1)S(1)} %collective-permute-done.2.near_b), channel_id=1, source_target_pairs={{0,1},{1,0},{2,3},{3,2},{4,5},{5,4},{6,7},{7,6},{8,9},{9,8},{10,11... | collective-permute-start | bytes 1572872 | tf_op jit(solution)/shard_map/section_weights/ppermute | solution.py:396
  49.4 3.9 %collective-permute-start.4 = (bf16[256,512]{1,0:T(8,128)(2,1)S(1)}, bf16[256,512]{1,0:T(8,128)(2,1)S(1)}, u32[]{:S(2)}, u32[]{:S(2)}) collective-permute-start(bf16[256,512]{1,0:T(8,128)(2,1)S(1)} %slice_select_fusion.1), channel_id=1, source_target_pairs={{0,384},{128,0},{256,128},{384,256},{1,129},{129,257},{257,385},{3... | collective-permute-start | bytes 786440 | tf_op jit(solution)/shard_map/section_weights/ppermute | solution.py:394
  53.3 1.0 copy.11
  54.4 1.0 routing.1
  55.4 7.8 %all_to_all.20.cot_ref = bf16[4,32,128]{2,1,0:T(8,128)(2,1)S(1)} all-to-all(bf16[4,32,128]{2,1,0:T(8,128)(2,1)S(1)} %get-tuple-element.31), channel_id=1, replica_groups=mesh['segment'=4,'z'=8,'y'=8,'core'=2] {'segment'}, dimensions={0} | all-to-all | bytes 65536 | tf_op jit(solution)/shard_map/routing/all_to_all | solution.py:407
  63.2 1.9 %collective-permute-start.7 = (bf16[256,2048]{1,0:T(8,128)(2,1)S(1)}, bf16[256,2048]{1,0:T(8,128)(2,1)S(1)}, u32[]{:S(2)}, u32[]{:S(2)}) collective-permute-start(bf16[256,2048]{1,0:T(8,128)(2,1)S(1)} %collective-permute-done.3.far_a), channel_id=1, source_target_pairs={{0,1},{1,0},{2,3},{3,2},{4,5},{5,4},{6,7},{7,6},{8,9},{9,8},{10,11... | collective-permute-start | bytes 3145736 | tf_op jit(solution)/shard_map/section_weights/ppermute | solution.py:410
  65.1 2.4 %collective-permute-start.8 = (bf16[256,512]{1,0:T(8,128)(2,1)S(1)}, bf16[256,512]{1,0:T(8,128)(2,1)S(1)}, u32[]{:S(2)}, u32[]{:S(2)}) collective-permute-start(bf16[256,512]{1,0:T(8,128)(2,1)S(1)} %collective-permute-done.4.far_c), channel_id=1, source_target_pairs={{0,1},{1,0},{2,3},{3,2},{4,5},{5,4},{6,7},{7,6},{8,9},{9,8},{10,11... | collective-permute-start | bytes 786440 | tf_op jit(solution)/shard_map/section_weights/ppermute | solution.py:410
  67.5 1.1 collective-permute-done.8.far_d
  68.7 11.9 %layers.1 = bf16[4,208,512]{2,1,0:T(8,128)(2,1)S(1)} custom-call(s32[4]{0:T(128)S(1)} %copy-done.4, bf16[4,64,512]{2,1,0:T(8,128)(2,1)S(1)} %copy-done.1, bf16[64,512]{1,0:T(8,128)(2,1)S(1)} %collective-permute-done.1.other_ref, s32[64,128]{1,0:T(8,128)S(1)} %get-tuple-element.29.count_ref, bf16[4,32,128]{2,1,0:T(8,128)(2,1)S(1)} %all_to_all.20.cot_ref, ...), custom_call_target="tpu_custom_call" | custom-call | tf_op jit(solution)/shard_map/layers/pallas_call | solution.py:413
  80.7 16.2 %all_to_all.21.got_ref = bf16[4,208,512]{2,1,0:T(8,128)(2,1)S(1)} all-to-all(bf16[4,208,512]{2,1,0:T(8,128)(2,1)S(1)} %layers.1), channel_id=1, replica_groups=mesh['segment'=4,'z'=8,'y'=8,'core'=2] {'segment'}, dimensions={0} | all-to-all | bytes 1703936 | tf_op jit(solution)/shard_map/section_exchange/all_to_all | solution.py:436
  96.9 1.3 weight_gradient.3
  98.1 1.9 %collective-permute-start.9 = (bf16[272,512]{1,0:T(8,128)(2,1)S(1)}, bf16[272,512]{1,0:T(8,128)(2,1)S(1)}, u32[]{:S(2)}, u32[]{:S(2)}) collective-permute-start(bf16[272,512]{1,0:T(8,128)(2,1)S(1)} %get-tuple-element.38.send_ref), channel_id=1, source_target_pairs={{0,1},{1,0},{2,3},{3,2},{4,5},{5,4},{6,7},{7,6},{8,9},{9,8},{10,11... | collective-permute-start | bytes 835592 | tf_op jit(solution)/shard_map/weight_gradient/ppermute | solution.py:446
  100.1 1.5 %collective-permute-done.9.got_ref = bf16[272,512]{1,0:T(8,128)(2,1)S(1)} collective-permute-done((bf16[272,512]{1,0:T(8,128)(2,1)S(1)}, bf16[272,512]{1,0:T(8,128)(2,1)S(1)}, u32[]{:S(2)}, u32[]{:S(2)}) %collective-permute-start.9) | collective-permute-done | bytes 278560 | tf_op jit(solution)/shard_map/weight_gradient/ppermute | solution.py:446
  101.8 25.4 %all_to_all.22 = bf16[64,4,768]{2,1,0:T(4,128)(2,1)S(1)} all-to-all(bf16[64,4,768]{2,1,0:T(4,128)(2,1)S(1)} %reshape.20), channel_id=1, replica_groups=mesh['segment'=4,'z'=8,'y'=8,'core'=2] {'z','y'}, dimensions={0} | all-to-all | bytes 786432 | tf_op jit(solution)/shard_map/weight_gradient/all_to_all | solution.py:452
  127.3 0.8 weight_gradient.5
  (22 shorter events, 0.6 us)
Async XLA Ops:
  0.6 41.2 %collective-permute-start = (bf16[512,2048]{1,0:T(8,128)(2,1)}, bf16[512,2048]{1,0:T(8,128)(2,1)S(1)}, u32[]{:S(2)}, u32[]{:S(2)}) collective-permute-start(bf16[512,2048]{1,0:T(8,128)(2,1)} %bitcast.8), channel_id=1, source_target_pairs={{0,384},{128,0},{256,128},{384,256},{1,129},{129,257},{257,385},{3... | collective-permute-start | bytes 6291464 | tf_op jit(solution)/shard_map/section_weights/ppermute | solution.py:379
  8.3 33.6 %all-to-all-start = ((bf16[128,2,640]{2,1,0:T(2,128)(2,1)}), bf16[128,2,640]{2,1,0:T(2,128)(2,1)}, u32[]{:S(2)}, u32[]{:S(2)}) async-start(bf16[128,2,640]{2,1,0:T(2,128)(2,1)} %get-tuple-element.24), calls=%async_computation | async-start | bytes 655360 | tf_op jit(solution)/shard_map/routing/all_to_all | solution.py:386
  26.1 15.4 %collective-permute-start.1 = (bf16[64,512]{1,0:T(8,128)(2,1)}, bf16[64,512]{1,0:T(8,128)(2,1)S(1)}, u32[]{:S(2)}, u32[]{:S(2)}) collective-permute-start(bf16[64,512]{1,0:T(8,128)(2,1)} %get-tuple-element.23), channel_id=1, source_target_pairs={{0,64},{16,80},{32,96},{48,112},{64,0},{80,16},{96,32},{112,48},{1... | collective-permute-start | bytes 196616 | tf_op jit(solution)/shard_map/events/ppermute | solution.py:383
  33.7 11.3 %collective-permute-start.2 = (bf16[512,512]{1,0:T(8,128)(2,1)}, bf16[512,512]{1,0:T(8,128)(2,1)S(1)}, u32[]{:S(2)}, u32[]{:S(2)}) collective-permute-start(bf16[512,512]{1,0:T(8,128)(2,1)} %bitcast.10), channel_id=1, source_target_pairs={{0,384},{128,0},{256,128},{384,256},{1,129},{129,257},{257,385},{3... | collective-permute-start | bytes 1572872 | tf_op jit(solution)/shard_map/section_weights/ppermute | solution.py:380
  36.5 17.9 %copy-start.3 = (f32[1,8,64]{2,1,0:T(8,128)S(1)}, f32[1,8,64]{2,1,0:T(8,128)}, u32[]{:S(2)}) copy-start(f32[1,8,64]{2,1,0:T(8,128)} %bias_ref.1) | copy-start | bytes 6148
  36.5 32.2 %copy-start.1 = (bf16[4,64,512]{2,1,0:T(8,128)(2,1)S(1)}, bf16[4,64,512]{2,1,0:T(8,128)(2,1)}, u32[]{:S(2)}) copy-start(bf16[4,64,512]{2,1,0:T(8,128)(2,1)} %events_ref.3) | copy-start | bytes 786436
  36.5 32.2 %copy-start.2 = (bf16[1,512,512]{2,1,0:T(8,128)(2,1)S(1)}, bf16[1,512,512]{2,1,0:T(8,128)(2,1)}, u32[]{:S(2)}) copy-start(bf16[1,512,512]{2,1,0:T(8,128)(2,1)} %w_out_ref.1) | copy-start | bytes 1572868
  36.5 32.2 %copy-start.4 = (s32[4]{0:T(128)S(1)}, s32[4]{0:T(128)}, u32[]{:S(2)}) copy-start(s32[4]{0:T(128)} %plan_ref.3) | copy-start | bytes 52
  41.9 26.8 %copy-start = (bf16[1,512,2048]{2,1,0:T(8,128)(2,1)S(1)}, bf16[1,512,2048]{2,1,0:T(8,128)(2,1)}, u32[]{:S(2)}) copy-start(bf16[1,512,2048]{2,1,0:T(8,128)(2,1)} %w_in_ref.1) | copy-start | bytes 6291460
  42.0 21.2 %collective-permute-start.3 = (bf16[256,2048]{1,0:T(8,128)(2,1)S(1)}, bf16[256,2048]{1,0:T(8,128)(2,1)S(1)}, u32[]{:S(2)}, u32[]{:S(2)}) collective-permute-start(bf16[256,2048]{1,0:T(8,128)(2,1)S(1)} %slice_select_fusion), channel_id=1, source_target_pairs={{0,384},{128,0},{256,128},{384,256},{1,129},{129,257},{257,385},{3... | collective-permute-start | bytes 3145736 | tf_op jit(solution)/shard_map/section_weights/ppermute | solution.py:394
  45.0 23.7 %collective-permute-start.6 = (bf16[512,2048]{1,0:T(8,128)(2,1)S(1)}, bf16[512,2048]{1,0:T(8,128)(2,1)S(1)}, u32[]{:S(2)}, u32[]{:S(2)}) collective-permute-start(bf16[512,2048]{1,0:T(8,128)(2,1)S(1)} %collective-permute-done.near_a), channel_id=1, source_target_pairs={{0,1},{1,0},{2,3},{3,2},{4,5},{5,4},{6,7},{7,6},{8,9},{9,8},{10,11... | collective-permute-start | bytes 6291464 | tf_op jit(solution)/shard_map/section_weights/ppermute | solution.py:395
  46.9 16.3 %collective-permute-start.5 = (bf16[512,512]{1,0:T(8,128)(2,1)S(1)}, bf16[512,512]{1,0:T(8,128)(2,1)S(1)}, u32[]{:S(2)}, u32[]{:S(2)}) collective-permute-start(bf16[512,512]{1,0:T(8,128)(2,1)S(1)} %collective-permute-done.2.near_b), channel_id=1, source_target_pairs={{0,1},{1,0},{2,3},{3,2},{4,5},{5,4},{6,7},{7,6},{8,9},{9,8},{10,11... | collective-permute-start | bytes 1572872 | tf_op jit(solution)/shard_map/section_weights/ppermute | solution.py:396
  49.4 13.8 %collective-permute-start.4 = (bf16[256,512]{1,0:T(8,128)(2,1)S(1)}, bf16[256,512]{1,0:T(8,128)(2,1)S(1)}, u32[]{:S(2)}, u32[]{:S(2)}) collective-permute-start(bf16[256,512]{1,0:T(8,128)(2,1)S(1)} %slice_select_fusion.1), channel_id=1, source_target_pairs={{0,384},{128,0},{256,128},{384,256},{1,129},{129,257},{257,385},{3... | collective-permute-start | bytes 786440 | tf_op jit(solution)/shard_map/section_weights/ppermute | solution.py:394
  63.2 5.5 %collective-permute-start.7 = (bf16[256,2048]{1,0:T(8,128)(2,1)S(1)}, bf16[256,2048]{1,0:T(8,128)(2,1)S(1)}, u32[]{:S(2)}, u32[]{:S(2)}) collective-permute-start(bf16[256,2048]{1,0:T(8,128)(2,1)S(1)} %collective-permute-done.3.far_a), channel_id=1, source_target_pairs={{0,1},{1,0},{2,3},{3,2},{4,5},{5,4},{6,7},{7,6},{8,9},{9,8},{10,11... | collective-permute-start | bytes 3145736 | tf_op jit(solution)/shard_map/section_weights/ppermute | solution.py:410
  65.1 3.6 %collective-permute-start.8 = (bf16[256,512]{1,0:T(8,128)(2,1)S(1)}, bf16[256,512]{1,0:T(8,128)(2,1)S(1)}, u32[]{:S(2)}, u32[]{:S(2)}) collective-permute-start(bf16[256,512]{1,0:T(8,128)(2,1)S(1)} %collective-permute-done.4.far_c), channel_id=1, source_target_pairs={{0,1},{1,0},{2,3},{3,2},{4,5},{5,4},{6,7},{7,6},{8,9},{9,8},{10,11... | collective-permute-start | bytes 786440 | tf_op jit(solution)/shard_map/section_weights/ppermute | solution.py:410
  98.1 3.4 %collective-permute-start.9 = (bf16[272,512]{1,0:T(8,128)(2,1)S(1)}, bf16[272,512]{1,0:T(8,128)(2,1)S(1)}, u32[]{:S(2)}, u32[]{:S(2)}) collective-permute-start(bf16[272,512]{1,0:T(8,128)(2,1)S(1)} %get-tuple-element.38.send_ref), channel_id=1, source_target_pairs={{0,1},{1,0},{2,3},{3,2},{4,5},{5,4},{6,7},{7,6},{8,9},{9,8},{10,11... | collective-permute-start | bytes 835592 | tf_op jit(solution)/shard_map/weight_gradient/ppermute | solution.py:446
